TPU v7x, 32 devices: a whole 2x2x4 slice. The times are simulated.
32 devices in a mesh: row: 4 (over x, core), col: 8 (over z, y).
Axes of the slice: x: 2, y: 2, z: 4, core: 2. Of those that a mesh axis runs over, the one named last changes fastest.
Arguments:
- block_in: bfloat16 [4096, 2048], P('col', 'row'), may hold values from -6 to 6
- cotangent: bfloat16 [4096, 2048], P('col', 'row'), may hold values from -6 to 6
- segments: int32 [4096], P('row'), may hold values from 0 to 31, never falling along the last dimension, each value on 1 to 1024 neighbouring positions
- w_query: bfloat16 [2048, 2048], P('row', 'col'), may hold values from -0.125 to 0.125
- w_key: bfloat16 [2048, 2048], P('row', 'col'), may hold values from -0.125 to 0.125
- w_value: bfloat16 [2048, 4096], P('row', 'col'), may hold values from -0.125 to 0.125
- w_gate: bfloat16 [2048, 4096], P('row', 'col'), may hold values from -0.125 to 0.125
- w_out: bfloat16 [4096, 2048], P('col', 'row'), may hold values from -0.09375 to 0.09375
- w_up: bfloat16 [2048, 4096], P('row', 'col'), may hold values from -0.125 to 0.125
- w_down: bfloat16 [4096, 2048], P('col', 'row'), may hold values from -0.09375 to 0.09375
- retention_norm_gain: float32 [2048], P('row'), may hold values from 0.25 to 1.75
- retention_norm_bias: float32 [2048], P('row'), may hold values from -3 to 3
- feedforward_norm_gain: float32 [2048], P('row'), may hold values from 0.25 to 1.75
- feedforward_norm_bias: float32 [2048], P('row'), may hold values from -3 to 3
Outputs:
- block_out: bfloat16 [4096, 2048], P('col', 'row')
- grad_in: float32 [4096, 2048], P('col', 'row')
- grad_query: float32 [2048, 2048], P('row', 'col')
- grad_key: float32 [2048, 2048], P('row', 'col')
- grad_value: float32 [2048, 4096], P('row', 'col')
- grad_gate: float32 [2048, 4096], P('row', 'col')
- grad_out: float32 [4096, 2048], P('col', 'row')
- grad_up: float32 [2048, 4096], P('row', 'col')
- grad_down: float32 [4096, 2048], P('col', 'row')
- grad_attn_gain: float32 [2048], P('row')
- grad_attn_bias: float32 [2048], P('row')
- grad_ffn_gain: float32 [2048], P('row')
- grad_ffn_bias: float32 [2048], P('row')
Inputs may be any that keep to these rules, and one draw needn't show every extreme that they name: `segments`: segment numbers never fall along the tokens; a document holds 1 to 1024 tokens.
All inputs are finite; a program needn't handle non-finite values.
Results may differ from a plain program's by a relative error of at most 0.014.
The roundings to bfloat16 on the way count: a program that leaves them out, or rounds other values in their place, can miss the bound.
Values may be sent and summed in bfloat16 or wider, within the bound.
No kernel may reach another device: no remote copies, remote signals or barrier semaphores. Data moves between devices by JAX's collectives and lax.ppermute only.
A program may use at most 320 MiB of HBM per device.

v0:
```python
import jax
import jax.numpy as jnp
from jax import lax
from jax.sharding import PartitionSpec as P

HEADS = 8
SEQ = 1024
SPAN = 512


eps_norm = 1e-05
group_eps = 0.25


def decay_block(first_branch, seg_query, seg_keys, loggam):
    rows = first_branch + lax.iota(jnp.int32, seg_query.shape[0])
    cols = lax.iota(jnp.int32, seg_keys.shape[0])
    gap = rows[:, None] - cols[None, :]
    inside = (gap >= 0) & (seg_query[:, None] == seg_keys[None, :])
    return jnp.where(
        inside, jnp.exp(jnp.maximum(gap, 0).astype(jnp.float32) * loggam), jnp.float32(0.0)
    )


def layernorm_statistics(first_branch, second_branch):
    return lax.psum((first_branch, second_branch), "row")


def token_gather(part):
    return lax.all_gather(part, "col", axis=0, tiled=True)


def token_reduce(term):
    return lax.psum_scatter(term, "col", scatter_dimension=0, tiled=True)


def unit_reduce(term):
    return lax.psum_scatter(term, "row", scatter_dimension=1, tiled=True)


def unit_gather(part):
    return lax.all_gather(part, "row", axis=1, tiled=True)


def heads_in(part):
    return lax.all_to_all(part, "col", split_axis=0, concat_axis=1, tiled=True)


def heads_out(part):
    return lax.all_to_all(part, "col", split_axis=1, concat_axis=0, tiled=True)


def layernorm_forward(residual_stream, norm_gain, norm_offset, model_width):
    total, squares = layernorm_statistics(
        jnp.sum(residual_stream, axis=1), jnp.sum(residual_stream * residual_stream, axis=1)
    )
    row_average = total / model_width
    inverse_deviation = lax.rsqrt(squares / model_width - row_average * row_average + eps_norm)
    standardized = (residual_stream - row_average[:, None]) * inverse_deviation[:, None]
    return (
        standardized,
        inverse_deviation,
        (standardized * norm_gain + norm_offset).astype(jnp.bfloat16),
    )


def layernorm_backward(upstream_gradient, standardized, inverse_deviation, norm_gain, model_width):
    scaled_rows = upstream_gradient * norm_gain
    first_branch, second_branch = layernorm_statistics(
        jnp.sum(scaled_rows, axis=1), jnp.sum(scaled_rows * standardized, axis=1)
    )
    input_gradient = inverse_deviation[:, None] * (
        scaled_rows
        - (first_branch / model_width)[:, None]
        - standardized * (second_branch / model_width)[:, None]
    )
    return (
        input_gradient,
        jnp.sum(upstream_gradient * standardized, axis=0),
        jnp.sum(upstream_gradient, axis=0),
    )


def gelu_exact(value):
    return jax.nn.gelu(value, approximate=False)


def gelu_grad(pre, upstream_gradient):
    return jax.vjp(gelu_exact, pre)[1](upstream_gradient)[0]


def split_heads(weight):
    return weight.reshape(weight.shape[0], -1, HEADS).transpose(0, 2, 1)


def join_heads(part):
    return part.transpose(0, 2, 1).reshape(part.shape[0], -1)


def group_normalize(retained):
    row_average = jnp.mean(retained, axis=0)
    centered = retained - row_average
    return centered * lax.rsqrt(jnp.mean(centered * centered, axis=0) + group_eps)


def unit_forward(inputs):
    query, keys, values, segs, loggam = inputs
    length = query.shape[1]
    scale = query.shape[0] ** (-0.5)

    def step(index, retained):
        first_branch = index * SPAN
        q_blk = lax.dynamic_slice_in_dim(query, first_branch, SPAN, 1)
        seg_q = lax.dynamic_slice_in_dim(segs, first_branch, SPAN, 0)
        raw = lax.dot_general(
            q_blk, keys, (((0,), (0,)), ((), ())), preferred_element_type=jnp.float32
        )
        weights = (raw * scale * decay_block(first_branch, seg_q, segs, loggam)).astype(
            jnp.bfloat16
        )
        block = lax.dot_general(
            values, weights, (((1,), (1,)), ((), ())), preferred_element_type=jnp.float32
        )
        return lax.dynamic_update_slice_in_dim(retained, block, first_branch, 1)

    retained = lax.fori_loop(
        0, length // SPAN, step, jnp.zeros((values.shape[0], length), jnp.float32)
    )
    return (group_normalize(retained), retained)


def unit_backward(inputs):
    query, keys, values, segs, loggam, retained, grad_normed = inputs
    length = query.shape[1]
    scale = query.shape[0] ** (-0.5)
    incoming = grad_normed.astype(jnp.float32)
    grad_ret = jax.vjp(group_normalize, retained)[1](incoming)[0].astype(jnp.bfloat16)

    def step(index, carry):
        grad_query, grad_keys, grad_values = carry
        first_branch = index * SPAN
        q_blk = lax.dynamic_slice_in_dim(query, first_branch, SPAN, 1)
        seg_q = lax.dynamic_slice_in_dim(segs, first_branch, SPAN, 0)
        decay = decay_block(first_branch, seg_q, segs, loggam)
        raw = lax.dot_general(
            q_blk, keys, (((0,), (0,)), ((), ())), preferred_element_type=jnp.float32
        )
        weights = (raw * scale * decay).astype(jnp.bfloat16)
        grad_blk = lax.dynamic_slice_in_dim(grad_ret, first_branch, SPAN, 1)
        grad_weights = lax.dot_general(
            grad_blk, values, (((0,), (0,)), ((), ())), preferred_element_type=jnp.float32
        )
        grad_scores = (grad_weights * decay * scale).astype(jnp.bfloat16)
        query_part = lax.dot_general(
            keys, grad_scores, (((1,), (1,)), ((), ())), preferred_element_type=jnp.float32
        )
        grad_query = lax.dynamic_update_slice_in_dim(grad_query, query_part, first_branch, 1)
        grad_keys = grad_keys + lax.dot_general(
            q_blk, grad_scores, (((1,), (0,)), ((), ())), preferred_element_type=jnp.float32
        )
        grad_values = grad_values + lax.dot_general(
            grad_blk, weights, (((1,), (0,)), ((), ())), preferred_element_type=jnp.float32
        )
        return (grad_query, grad_keys, grad_values)

    start = (
        jnp.zeros(query.shape, jnp.float32),
        jnp.zeros(keys.shape, jnp.float32),
        jnp.zeros(values.shape, jnp.float32),
    )
    grad_query, grad_keys, grad_values = lax.fori_loop(0, length // SPAN, step, start)
    return (
        grad_query.astype(jnp.bfloat16),
        grad_keys.astype(jnp.bfloat16),
        grad_values.astype(jnp.bfloat16),
    )


def body(
    block_in,
    cotangent,
    segments,
    w_query,
    w_key,
    w_value,
    w_gate,
    w_out,
    w_up,
    w_down,
    retention_norm_gain,
    retention_norm_bias,
    feedforward_norm_gain,
    feedforward_norm_bias,
):
    row_count = lax.axis_size("row")
    col_count = lax.axis_size("col")
    model_part = block_in.shape[1]
    model_width = model_part * row_count
    key_part = w_query.shape[1] // HEADS
    value_part = w_value.shape[1] // HEADS
    triple = 2 * key_part + value_part
    seq_rows = segments.shape[0] // SEQ
    batches = seq_rows * row_count
    units = HEADS * seq_rows // col_count
    residual_stream = block_in.astype(jnp.float32)
    first_standardized, first_inverse_deviation, first_normed = layernorm_forward(
        residual_stream, retention_norm_gain, retention_norm_bias, model_width
    )
    gathered_one = token_gather(first_normed).reshape(batches, SEQ, model_part)
    stacked = jnp.concatenate(
        [split_heads(w_query), split_heads(w_key), split_heads(w_value), split_heads(w_gate)],
        axis=2,
    )
    partial_proj = jnp.einsum(
        "bsd,dhw->hbws", gathered_one, stacked, preferred_element_type=jnp.float32
    )
    inner = unit_reduce(partial_proj)
    gate = inner[:, :, triple:]
    sending = inner[:, :, :triple].astype(jnp.bfloat16).reshape(HEADS * seq_rows, triple, SEQ)
    arrived = heads_in(sending).reshape(units, col_count, triple, SEQ)
    query = arrived[:, :, :key_part].reshape(units, key_part * col_count, SEQ)
    keys = arrived[:, :, key_part : 2 * key_part].reshape(units, key_part * col_count, SEQ)
    values = arrived[:, :, 2 * key_part :].reshape(units, value_part * col_count, SEQ)
    unit_ids = lax.axis_index("col") * units + lax.iota(jnp.int32, units)
    head_ids = unit_ids // seq_rows
    loggam = jnp.log1p(-jnp.exp2(-5.0 - head_ids.astype(jnp.float32)))
    seq_ids = unit_ids % seq_rows
    seg_rows = segments.reshape(seq_rows, SEQ)
    picked = seq_ids[:, None] == lax.iota(jnp.int32, seq_rows)[None, :]
    unit_segs = jnp.sum(jnp.where(picked[:, :, None], seg_rows[None, :, :], 0), axis=1)
    normed, retained_units = lax.map(unit_forward, (query, keys, values, unit_segs, loggam))
    normed_back = (
        heads_out(normed.astype(jnp.bfloat16))
        .reshape(HEADS, seq_rows, value_part, SEQ)
        .astype(jnp.float32)
    )
    sigma = jax.nn.sigmoid(gate)
    swish = gate * sigma
    hidden = (swish * normed_back).astype(jnp.bfloat16)
    hidden_all = unit_gather(hidden)
    out_heads = w_out.reshape(value_part, HEADS, model_part)
    attn_part = jnp.einsum(
        "hbvs,vhd->bsd", hidden_all, out_heads, preferred_element_type=jnp.float32
    )
    attn_sum = token_reduce(attn_part.reshape(batches * SEQ, model_part))
    residual_between = residual_stream + attn_sum
    second_standardized, second_inverse_deviation, second_normed = layernorm_forward(
        residual_between, feedforward_norm_gain, feedforward_norm_bias, model_width
    )
    grad_top = cotangent.astype(jnp.float32)
    gathered_two = token_gather(second_normed).reshape(batches, SEQ, model_part)
    pre = unit_reduce(
        jnp.einsum("bsd,df->bfs", gathered_two, w_up, preferred_element_type=jnp.float32)[None]
    )
    act = gelu_exact(pre).astype(jnp.bfloat16)
    act_all = unit_gather(act)[0]
    down_part = jnp.einsum("bfs,fd->bsd", act_all, w_down, preferred_element_type=jnp.float32)
    ffn_out = token_reduce(down_part.reshape(batches * SEQ, model_part))
    grad_spread = token_gather(cotangent).reshape(batches, SEQ, model_part)
    grad_down = jnp.einsum("bfs,bsd->fd", act_all, grad_spread, preferred_element_type=jnp.float32)
    grad_act = unit_reduce(
        jnp.einsum("bsd,fd->bfs", grad_spread, w_down, preferred_element_type=jnp.float32)[None]
    )
    grad_pre = gelu_grad(pre, grad_act).astype(jnp.bfloat16)
    grad_pre_all = unit_gather(grad_pre)[0]
    grad_up = jnp.einsum(
        "bsd,bfs->df", gathered_two, grad_pre_all, preferred_element_type=jnp.float32
    )
    back_part = jnp.einsum("bfs,df->bsd", grad_pre_all, w_up, preferred_element_type=jnp.float32)
    gradient_second_normed = token_reduce(back_part.reshape(batches * SEQ, model_part))
    block_out = (residual_between + ffn_out).astype(jnp.bfloat16)
    grad_from_two, grad_ffn_gain, grad_ffn_bias = layernorm_backward(
        gradient_second_normed,
        second_standardized,
        second_inverse_deviation,
        feedforward_norm_gain,
        model_width,
    )
    grad_mid = grad_top + grad_from_two
    grad_mid_low = grad_mid.astype(jnp.bfloat16)
    grad_attn = token_gather(grad_mid_low).reshape(batches, SEQ, model_part)
    grad_out = jnp.einsum(
        "hbvs,bsd->vhd", hidden_all, grad_attn, preferred_element_type=jnp.float32
    ).reshape(value_part * HEADS, model_part)
    grad_hidden = unit_reduce(
        jnp.einsum("bsd,vhd->hbvs", grad_attn, out_heads, preferred_element_type=jnp.float32)
    )
    gate_back = (grad_hidden * normed_back * (sigma * (1.0 + gate * (1.0 - sigma)))).astype(
        jnp.bfloat16
    )
    grad_normed = (
        (grad_hidden * swish).astype(jnp.bfloat16).reshape(HEADS * seq_rows, value_part, SEQ)
    )
    grad_units = heads_in(grad_normed)
    grad_q, grad_k, grad_v = lax.map(
        unit_backward, (query, keys, values, unit_segs, loggam, retained_units, grad_units)
    )
    packed = jnp.concatenate(
        [
            grad_q.reshape(units, col_count, key_part, SEQ),
            grad_k.reshape(units, col_count, key_part, SEQ),
            grad_v.reshape(units, col_count, value_part, SEQ),
        ],
        axis=2,
    ).reshape(units, col_count * triple, SEQ)
    grad_triple = heads_out(packed).reshape(HEADS, seq_rows, triple, SEQ)
    grad_proj = unit_gather(jnp.concatenate([grad_triple, gate_back], axis=2))
    grad_stacked = jnp.einsum(
        "bsd,hbws->dhw", gathered_one, grad_proj, preferred_element_type=jnp.float32
    )
    grad_query = join_heads(grad_stacked[:, :, :key_part])
    grad_key = join_heads(grad_stacked[:, :, key_part : 2 * key_part])
    grad_value = join_heads(grad_stacked[:, :, 2 * key_part : triple])
    grad_gate = join_heads(grad_stacked[:, :, triple:])
    back_one = jnp.einsum("hbws,dhw->bsd", grad_proj, stacked, preferred_element_type=jnp.float32)
    gradient_first_normed = token_reduce(back_one.reshape(batches * SEQ, model_part))
    grad_from_one, grad_attn_gain, grad_attn_bias = layernorm_backward(
        gradient_first_normed,
        first_standardized,
        first_inverse_deviation,
        retention_norm_gain,
        model_width,
    )
    grad_in = grad_mid + grad_from_one
    totals = lax.psum((grad_attn_gain, grad_attn_bias, grad_ffn_gain, grad_ffn_bias), "col")
    return (
        block_out,
        grad_in,
        grad_query,
        grad_key,
        grad_value,
        grad_gate,
        grad_out,
        grad_up,
        grad_down,
        totals[0],
        totals[1],
        totals[2],
        totals[3],
    )


def solution(mesh):
    return jax.shard_map(
        body,
        mesh=mesh,
        in_specs=(
            P("col", "row"),
            P("col", "row"),
            P("row"),
            P("row", "col"),
            P("row", "col"),
            P("row", "col"),
            P("row", "col"),
            P("col", "row"),
            P("row", "col"),
            P("col", "row"),
            P("row"),
            P("row"),
            P("row"),
            P("row"),
        ),
        out_specs=(
            P("col", "row"),
            P("col", "row"),
            P("row", "col"),
            P("row", "col"),
            P("row", "col"),
            P("row", "col"),
            P("col", "row"),
            P("row", "col"),
            P("col", "row"),
            P("row"),
            P("row"),
            P("row"),
            P("row"),
        ),
        check_vma=False,
    )
```

profile of v0, /device:TPU:0, one launch (start us, length us, event | category | flops | bytes accessed | tf_op | source)
XLA Modules:
  0.0 2191.7 jit_solution(5902416762991694232)
XLA Ops:
  8.7 8.3 all-reduce.6
  20.6 72.5 %all-gather.9.cloned.1.call-done = bf16[4096,512]{1,0:T(8,128)(2,1)} async-done(((bf16[512,512]{1,0:T(8,128)(2,1)}), bf16[4096,512]{1,0:T(8,128)(2,1)}) %all-gather.9.cloned.1.call-update) | async-done | bytes 4194320 | tf_op jit(solution)/shard_map/all_gather | solution.py:30
  93.1 14.2 convolution_bitcast_fusion.2
  108.6 420.1 %all-reduce.10.cloned.1.call-done = f32[8,4,192,1024]{3,2,1,0:T(8,128)} async-done(((f32[8,4,192,1024]{3,2,1,0:T(8,128)}), f32[8,4,192,1024]{3,2,1,0:T(8,128)}) %all-reduce.10.cloned.1.call-update) | async-done | bytes 25165840
  539.1 47.9 %all-to-all-done = bf16[8,128,1024]{2,1,0:T(8,128)(2,1)S(1)} async-done(((bf16[8,128,1024]{2,1,0:T(8,128)(2,1)}), bf16[8,128,1024]{2,1,0:T(8,128)(2,1)S(1)}, u32[]{:S(2)}, u32[]{:S(2)}) %all-to-all-start) | async-done | bytes 2097184 | tf_op jit(solution)/shard_map/all_to_all | solution.py:46
  603.1 9.0 reduce
  619.5 25.1 %all-to-all-done.1 = bf16[8,2,32768]{2,1,0:T(2,128)(2,1)} async-done(((bf16[8,2,32768]{2,1,0:T(2,128)(2,1)}), bf16[8,2,32768]{2,1,0:T(2,128)(2,1)}, u32[]{:S(2)}, u32[]{:S(2)}) %all-to-all-start.1) | async-done | bytes 1048608 | tf_op jit(solution)/shard_map/all_to_all | solution.py:50
  657.8 33.1 %all-gather.11.cloned.1.call-done = bf16[8,4,64,1024]{3,2,1,0:T(8,128)(2,1)} async-done(((bf16[8,1,64,1024]{3,2,1,0:T(8,128)(2,1)}), bf16[8,4,64,1024]{3,2,1,0:T(8,128)(2,1)}) %all-gather.11.cloned.1.call-update) | async-done | bytes 4194320 | tf_op jit(solution)/shard_map/all_gather | solution.py:42
  699.9 148.5 %reduce-scatter.13.cloned.1.call-done = f32[512,512]{1,0:T(8,128)} async-done(((f32[4096,512]{1,0:T(8,128)}), f32[512,512]{1,0:T(8,128)}) %reduce-scatter.13.cloned.1.call-update) | async-done | bytes 1048592 | tf_op jit(solution)/shard_map/reduce_scatter | solution.py:34
  860.2 62.7 %all-gather.17.cloned.1.call-done = bf16[4096,512]{1,0:T(8,128)(2,1)} async-done(((bf16[512,512]{1,0:T(8,128)(2,1)}), bf16[4096,512]{1,0:T(8,128)(2,1)}) %all-gather.17.cloned.1.call-update) | async-done | bytes 4194320 | tf_op jit(solution)/shard_map/all_gather | solution.py:30
  922.9 7.8 convolution_bitcast_fusion.4
  930.7 66.4 %all-gather.13.cloned.1.call-done = bf16[4096,512]{1,0:T(8,128)(2,1)} async-done(((bf16[512,512]{1,0:T(8,128)(2,1)}), bf16[4096,512]{1,0:T(8,128)(2,1)}) %all-gather.13.cloned.1.call-update) | async-done | bytes 4194320 | tf_op jit(solution)/shard_map/all_gather | solution.py:30
  997.1 8.3 convolution_bitcast_fusion.5
  1005.5 64.2 %reduce-scatter.19.cloned.1.call-done = f32[1,1,512,1024]{2,3,1,0:T(8,128)} async-done(((f32[1,4,512,1024]{2,3,1,0:T(8,128)}), f32[1,1,512,1024]{2,3,1,0:T(8,128)}) %reduce-scatter.19.cloned.1.call-update) | async-done | bytes 2097168 | tf_op jit(solution)/shard_map/reduce_scatter | solution.py:38
  1069.7 74.5 %reduce-scatter.15.cloned.1.call-done = f32[1,1,512,1024]{2,3,1,0:T(8,128)} async-done(((f32[1,4,512,1024]{2,3,1,0:T(8,128)}), f32[1,1,512,1024]{2,3,1,0:T(8,128)}) %reduce-scatter.15.cloned.1.call-update) | async-done | bytes 2097168 | tf_op jit(solution)/shard_map/reduce_scatter | solution.py:38
  1160.1 28.3 %all-gather.19.cloned.1.call-done = bf16[1,4,512,1024]{3,2,0,1:T(8,128)(2,1)} async-done(((bf16[1,1,512,1024]{3,2,0,1:T(8,128)(2,1)}), bf16[1,4,512,1024]{3,2,0,1:T(8,128)(2,1)}) %all-gather.19.cloned.1.call-update) | async-done | bytes 4194320 | tf_op jit(solution)/shard_map/all_gather | solution.py:42
  1194.6 8.0 fusion.88
  1202.7 22.3 %all-gather.15.cloned.1.call-done = bf16[1,4,512,1024]{3,2,0,1:T(8,128)(2,1)} async-done(((bf16[1,1,512,1024]{3,2,0,1:T(8,128)(2,1)}), bf16[1,4,512,1024]{3,2,0,1:T(8,128)(2,1)}) %all-gather.15.cloned.1.call-update) | async-done | bytes 4194320 | tf_op jit(solution)/shard_map/all_gather | solution.py:42
  1231.2 7.8 fusion.87
  1239.0 138.6 %reduce-scatter.21.cloned.1.call-done = f32[512,512]{1,0:T(8,128)} async-done(((f32[4096,512]{1,0:T(8,128)}), f32[512,512]{1,0:T(8,128)}) %reduce-scatter.21.cloned.1.call-update) | async-done | bytes 1048592 | tf_op jit(solution)/shard_map/reduce_scatter | solution.py:34
  1387.0 142.5 %reduce-scatter.17.cloned.1.call-done = f32[512,512]{1,0:T(8,128)} async-done(((f32[4096,512]{1,0:T(8,128)}), f32[512,512]{1,0:T(8,128)}) %reduce-scatter.17.cloned.1.call-update) | async-done | bytes 1048592 | tf_op jit(solution)/shard_map/reduce_scatter | solution.py:34
  1533.2 72.5 %all-gather.21.cloned.1.call-done = bf16[4096,512]{1,0:T(8,128)(2,1)} async-done(((bf16[512,512]{1,0:T(8,128)(2,1)}), bf16[4096,512]{1,0:T(8,128)(2,1)}) %all-gather.21.cloned.1.call-update) | async-done | bytes 4194320 | tf_op jit(solution)/shard_map/all_gather | solution.py:30
  1605.7 7.8 convolution_bitcast_fusion.6
  1613.6 151.3 %all-reduce.12.cloned.1.call-done = f32[8,4,64,1024]{3,2,1,0:T(8,128)} async-done(((f32[8,4,64,1024]{3,2,1,0:T(8,128)}), f32[8,4,64,1024]{3,2,1,0:T(8,128)}) %all-reduce.12.cloned.1.call-update) | async-done | bytes 8388624
  1776.7 25.3 %all-to-all-done.2 = bf16[8,64,1024]{2,1,0:T(8,128)(2,1)} async-done(((bf16[8,64,1024]{2,1,0:T(8,128)(2,1)}), bf16[8,64,1024]{2,1,0:T(8,128)(2,1)}, u32[]{:S(2)}, u32[]{:S(2)}) %all-to-all-start.2) | async-done | bytes 1048608 | tf_op jit(solution)/shard_map/all_to_all | solution.py:46
  1808.2 18.9 while.51
  1834.5 12.8 reduce.1
  1851.1 51.9 %all_to_all.16 = bf16[8,2,65536]{2,1,0:T(2,128)(2,1)S(1)} all-to-all(bf16[8,2,65536]{2,1,0:T(2,128)(2,1)} %reshape.252), channel_id=1, replica_groups=mesh['row'=4,'col'=8] {'col'}, dimensions={0} | all-to-all | bytes 4194304 | tf_op jit(solution)/shard_map/all_to_all | solution.py:50
  1912.4 80.8 %all-gather.23.cloned.1.call-done = bf16[8,4,192,1024]{3,2,0,1:T(8,128)(2,1)} async-done(((bf16[8,1,192,1024]{3,2,0,1:T(8,128)(2,1)}), bf16[8,4,192,1024]{3,2,0,1:T(8,128)(2,1)}) %all-gather.23.cloned.1.call-update) | async-done | bytes 12582928 | tf_op jit(solution)/shard_map/all_gather | solution.py:42
  1993.3 11.9 fusion.51
  2038.1 116.3 %reduce-scatter.23.cloned.1.call-done = f32[512,512]{1,0:T(8,128)} async-done(((f32[4096,512]{1,0:T(8,128)}), f32[512,512]{1,0:T(8,128)}) %reduce-scatter.23.cloned.1.call-update) | async-done | bytes 1048592 | tf_op jit(solution)/shard_map/reduce_scatter | solution.py:34
  2163.2 20.3 all-reduce.2
  (243 shorter events, 221.6 us)
Async XLA Ops:
  7.2 686.3 %copy-start = (bf16[512,512]{1,0:T(8,128)(2,1)S(1)}, bf16[512,512]{1,0:T(8,128)(2,1)}, u32[]{:S(2)}) copy-start(bf16[512,512]{1,0:T(8,128)(2,1)} %param.25) | copy-start | bytes 1572868
  7.2 85.8 %all-gather.9.cloned.1.call-start = ((), (), s32[]{:S(2)}) async-start(), calls=%async_computation.10 | async-start | bytes 4718592 | tf_op jit(solution)/shard_map/all_gather | solution.py:30
  19.2 509.5 %all-reduce.10.cloned.1.call-start = ((), (), s32[]{:S(2)}) async-start(), calls=%async_computation.24 | async-start | bytes 50331648
  20.2 87.1 %copy-start.31 = (bf16[512,8,32]{0,2,1:T(8,128)(2,1)}, bf16[512,8,32]{0,2,1:T(8,128)(2,1)S(1)}, u32[]{:S(2)}) copy-start(bf16[512,8,32]{0,2,1:T(8,128)(2,1)S(1)} %get-tuple-element.541) | copy-start | bytes 786436
  533.2 53.7 %all-to-all-start = ((bf16[8,128,1024]{2,1,0:T(8,128)(2,1)}), bf16[8,128,1024]{2,1,0:T(8,128)(2,1)S(1)}, u32[]{:S(2)}, u32[]{:S(2)}) async-start(bf16[8,128,1024]{2,1,0:T(8,128)(2,1)} %fusion.43), calls=%async_computation | async-start | bytes 4194304 | tf_op jit(solution)/shard_map/all_to_all | solution.py:46
  614.7 29.9 %all-to-all-start.1 = ((bf16[8,2,32768]{2,1,0:T(2,128)(2,1)}), bf16[8,2,32768]{2,1,0:T(2,128)(2,1)}, u32[]{:S(2)}, u32[]{:S(2)}) async-start(bf16[8,2,32768]{2,1,0:T(2,128)(2,1)} %reshape.250), calls=%async_computation.1 | async-start | bytes 2097152 | tf_op jit(solution)/shard_map/all_to_all | solution.py:50
  619.0 71.9 %all-gather.11.cloned.1.call-start = ((), (), s32[]{:S(2)}) async-start(), calls=%async_computation.11 | async-start | bytes 5242880 | tf_op jit(solution)/shard_map/all_gather | solution.py:42
  657.7 190.8 %reduce-scatter.13.cloned.1.call-start = ((), (), s32[]{:S(2)}) async-start(), calls=%async_computation.12 | async-start | bytes 9437184 | tf_op jit(solution)/shard_map/reduce_scatter | solution.py:34
  699.2 149.2 %copy-start.7 = (bf16[512,512]{1,0:T(8,128)(2,1)S(1)}, bf16[512,512]{1,0:T(8,128)(2,1)}, u32[]{:S(2)}) copy-start(bf16[512,512]{1,0:T(8,128)(2,1)} %param.18) | copy-start | bytes 1572868
  699.3 158.5 %copy-start.38 = (f32[512]{0:T(512)S(1)}, f32[512]{0:T(512)}, u32[]{:S(2)}) copy-start(f32[512]{0:T(512)} %param.30) | copy-start | bytes 6148
  699.3 158.5 %copy-start.42 = (f32[512]{0:T(512)S(1)}, f32[512]{0:T(512)}, u32[]{:S(2)}) copy-start(f32[512]{0:T(512)} %param.31) | copy-start | bytes 6148
  699.3 223.6 %all-gather.17.cloned.1.call-start = ((), (), s32[]{:S(2)}) async-start(), calls=%async_computation.17 | async-start | bytes 4718592 | tf_op jit(solution)/shard_map/all_gather | solution.py:30
  699.9 297.2 %all-gather.13.cloned.1.call-start = ((), (), s32[]{:S(2)}) async-start(), calls=%async_computation.13 | async-start | bytes 4718592 | tf_op jit(solution)/shard_map/all_gather | solution.py:30
  860.1 209.6 %reduce-scatter.19.cloned.1.call-start = ((), (), s32[]{:S(2)}) async-start(), calls=%async_computation.18 | async-start | bytes 10485760 | tf_op jit(solution)/shard_map/reduce_scatter | solution.py:38
  930.7 213.5 %reduce-scatter.15.cloned.1.call-start = ((), (), s32[]{:S(2)}) async-start(), calls=%async_computation.14 | async-start | bytes 10485760 | tf_op jit(solution)/shard_map/reduce_scatter | solution.py:38
  1005.5 182.9 %all-gather.19.cloned.1.call-start = ((), (), s32[]{:S(2)}) async-start(), calls=%async_computation.19 | async-start | bytes 5242880 | tf_op jit(solution)/shard_map/all_gather | solution.py:42
  1153.8 71.1 %all-gather.15.cloned.1.call-start = ((), (), s32[]{:S(2)}) async-start(), calls=%async_computation.15 | async-start | bytes 5242880 | tf_op jit(solution)/shard_map/all_gather | solution.py:42
  1160.0 217.6 %reduce-scatter.21.cloned.1.call-start = ((), (), s32[]{:S(2)}) async-start(), calls=%async_computation.20 | async-start | bytes 9437184 | tf_op jit(solution)/shard_map/reduce_scatter | solution.py:34
  1202.6 326.9 %reduce-scatter.17.cloned.1.call-start = ((), (), s32[]{:S(2)}) async-start(), calls=%async_computation.16 | async-start | bytes 9437184 | tf_op jit(solution)/shard_map/reduce_scatter | solution.py:34
  1239.0 290.6 %copy-start.18 = (bf16[512,512]{1,0:T(8,128)(2,1)S(1)}, bf16[512,512]{1,0:T(8,128)(2,1)}, u32[]{:S(2)}) copy-start(bf16[512,512]{1,0:T(8,128)(2,1)} %param.19) | copy-start | bytes 1572868
  1239.0 366.8 %all-gather.21.cloned.1.call-start = ((), (), s32[]{:S(2)}) async-start(), calls=%async_computation.21 | async-start | bytes 4718592 | tf_op jit(solution)/shard_map/all_gather | solution.py:30
  1533.2 231.7 %all-reduce.12.cloned.1.call-start = ((), (), s32[]{:S(2)}) async-start(), calls=%async_computation.25 | async-start | bytes 16777216
  1770.7 31.3 %all-to-all-start.2 = ((bf16[8,64,1024]{2,1,0:T(8,128)(2,1)}), bf16[8,64,1024]{2,1,0:T(8,128)(2,1)}, u32[]{:S(2)}, u32[]{:S(2)}) async-start(bf16[8,64,1024]{2,1,0:T(8,128)(2,1)} %get-tuple-element.525), calls=%async_computation.7 | async-start | bytes 2097152 | tf_op jit(solution)/shard_map/all_to_all | solution.py:46
  1776.3 217.0 %all-gather.23.cloned.1.call-start = ((), (), s32[]{:S(2)}) async-start(), calls=%async_computation.22 | async-start | bytes 15728640 | tf_op jit(solution)/shard_map/all_gather | solution.py:42
  1912.4 242.0 %reduce-scatter.23.cloned.1.call-start = ((), (), s32[]{:S(2)}) async-start(), calls=%async_computation.23 | async-start | bytes 9437184 | tf_op jit(solution)/shard_map/reduce_scatter | solution.py:34
  2036.1 118.3 %copy-start.8 = (bf16[512,512]{1,0:T(8,128)(2,1)S(1)}, bf16[512,512]{1,0:T(8,128)(2,1)}, u32[]{:S(2)}) copy-start(bf16[512,512]{1,0:T(8,128)(2,1)} %param.18) | copy-start | bytes 1572868
  2036.1 118.3 %copy-start.35 = (f32[512]{0:T(512)S(1)}, f32[512]{0:T(512)}, u32[]{:S(2)}) copy-start(f32[512]{0:T(512)} %copy-done.34) | copy-start | bytes 6148
  2036.1 118.3 %copy-start.37 = (f32[512]{0:T(512)S(1)}, f32[512]{0:T(512)}, u32[]{:S(2)}) copy-start(f32[512]{0:T(512)} %copy-done.36) | copy-start | bytes 6148
  2036.1 118.3 %copy-start.39 = (f32[512]{0:T(512)S(1)}, f32[512]{0:T(512)}, u32[]{:S(2)}) copy-start(f32[512]{0:T(512)} %param.28) | copy-start | bytes 6148
  2036.7 126.4 %copy-start.40 = (f32[512]{0:T(512)S(1)}, f32[512]{0:T(512)}, u32[]{:S(2)}) copy-start(f32[512]{0:T(512)} %get-tuple-element.462) | copy-start | bytes 6148
  2036.8 126.4 %copy-start.41 = (f32[512]{0:T(512)S(1)}, f32[512]{0:T(512)}, u32[]{:S(2)}) copy-start(f32[512]{0:T(512)} %get-tuple-element.468) | copy-start | bytes 6148
  2036.8 146.8 %copy-start.15 = (f32[512,512]{1,0:T(8,128)S(1)}, f32[512,512]{1,0:T(8,128)}, u32[]{:S(2)}) copy-start(f32[512,512]{1,0:T(8,128)} %get-tuple-element.521) | copy-start | bytes 3145732
  (39 other events, 752.4 us)
Sparse Core Ops, SparseCore 0:
  19.3 73.7 all-gather.8
  107.5 421.1 all-reduce.9
  657.8 33.0 all-gather.10
  699.4 149.0 reduce-scatter.12
  850.4 72.3 all-gather.16
  925.4 71.6 all-gather.12
  999.7 69.9 reduce-scatter.18
  1072.5 71.6 reduce-scatter.14
  1153.9 34.4 all-gather.18
  1190.4 34.4 all-gather.14
  1228.5 148.9 reduce-scatter.20
  1381.5 147.9 reduce-scatter.16
  1533.3 72.4 all-gather.20
  1613.7 151.1 all-reduce.11
  1912.5 80.7 all-gather.22
  2005.3 149.0 reduce-scatter.22
where the time goes:
time: 2200 us; the launch traced here: 2190 us
  waiting for transfers between devices  1790 us (81%)
  matrix products  113 us (5%)
  blocking collectives  101 us (5%)
  local copies, waits for them, and re-layouts  79.6 us (4%)
  other arithmetic  71.3 us (3%)
    unnamed x18, waiting for transfers between devices  572 us
    reduce_scatter x4, waiting for transfers between devices, token_reduce(): return lax.psum_scatter(term, 'col', scatter_dimension=0, tiled=True)  546 us
    all_gather x4, waiting for transfers between devices, token_gather(): return lax.all_gather(part, 'col', axis=0, tiled=True)  274 us
    all_gather x4, waiting for transfers between devices, unit_gather(): return lax.all_gather(part, 'row', axis=1, tiled=True)  165 us
    reduce_scatter x2, waiting for transfers between devices, unit_reduce(): return lax.psum_scatter(term, 'row', scatter_dimension=1, tiled=True)  139 us
    all_to_all x2, waiting for transfers between devices, heads_in(): return lax.all_to_all(part, 'col', split_axis=0, concat_axis=1, tiled=True)  73.2 us
    all_to_all x1, blocking collectives, heads_out(): return lax.all_to_all(part, 'col', split_axis=1, concat_axis=0, tiled=True)  51.9 us
  transfers between devices with their start and end apart: 19, of which 19 were waited for; matrix products, arithmetic and copies ran while one was open for 4% of the time, Pallas kernels for 0%

commit v1 on v0

v1 whole, which is shorter than its diff:
```python
import jax
import jax.numpy as jnp
from jax import lax
from jax.sharding import Mesh
from jax.sharding import PartitionSpec as P

HEADS = 8
EPS_NORM = 1e-05
EPS_GROUP = 0.25

ROW = ("x", "k")
GROUP = ("x", "k", "y")
EVERY = ("x", "k", "z", "y")
F32 = jnp.float32
BF16 = jnp.bfloat16


def dot(left, right, over):
    return lax.dot_general(left, right, (over, ((), ())), preferred_element_type=F32)


def swap(value, mask):
    return lax.ppermute(value, GROUP, [(i, i ^ mask) for i in range(8)])


def group_gather(part):
    near = jnp.stack([part, swap(part, 1), swap(part, 4), swap(part, 5)])
    near = near.reshape((2, 1, 2) + part.shape)
    return jnp.concatenate([near, swap(near, 2)], axis=1).reshape((-1,) + part.shape[1:])


def group_reduce(total):
    blocks = total.reshape(2, 2, 2, total.shape[0] // 8, total.shape[1])
    pair = (blocks[:, 0] + swap(blocks[:, 1].astype(BF16), 2).astype(F32)).astype(BF16)
    own = pair[0, 0].astype(F32)
    for i, j in ((0, 1), (1, 0), (1, 1)):
        own = own + swap(pair[i, j], 4 * i + j).astype(F32)
    return own


def row_exchange(parts):
    return lax.all_to_all(parts, ROW, split_axis=0, concat_axis=0, tiled=True)


def to_tokens(part):
    tokens, width = part.shape
    moved = row_exchange(part.reshape(4, tokens // 4, width))
    return moved.transpose(1, 0, 2).reshape(tokens // 4, 4 * width)


def from_tokens(part):
    tokens, width = part.shape
    moved = row_exchange(part.reshape(tokens, 4, width // 4).transpose(1, 0, 2))
    return moved.reshape(4 * tokens, width // 4)


def head_order(count):
    units = count // HEADS
    j = lax.iota(jnp.int32, count)
    target = (j % HEADS) * units + j // HEADS
    return (target[:, None] == lax.iota(jnp.int32, count)[None, :]).astype(BF16)


def layernorm(value, gain, bias):
    mean = jnp.mean(value, axis=1, keepdims=True)
    centered = value - mean
    inverse = lax.rsqrt(jnp.mean(centered * centered, axis=1, keepdims=True) + EPS_NORM)
    hat = centered * inverse
    return hat, inverse, (hat * gain + bias).astype(BF16)


def layernorm_back(grad, hat, inverse, gain):
    scaled = grad * gain
    first = jnp.mean(scaled, axis=1, keepdims=True)
    second = jnp.mean(scaled * hat, axis=1, keepdims=True)
    return (
        inverse * (scaled - first - hat * second),
        jnp.sum(grad * hat, axis=0),
        jnp.sum(grad, axis=0),
    )


def gelu_exact(value):
    return jax.nn.gelu(value, approximate=False)


def body(
    block_in,
    cotangent,
    segments,
    w_query,
    w_key,
    w_value,
    w_gate,
    w_out,
    w_up,
    w_down,
    retention_norm_gain,
    retention_norm_bias,
    feedforward_norm_gain,
    feedforward_norm_bias,
):
    depth = lax.axis_size("z")
    part = block_in.shape[1]
    width = 4 * part
    own = lax.axis_index(GROUP)
    plane = lax.axis_index("z")
    tokens = block_in.shape[0] // 4
    seq = 8 * tokens

    kq = w_query.shape[1] // HEADS
    kv = w_value.shape[1] // HEADS
    order_q = head_order(w_query.shape[1])
    order_v = head_order(w_value.shape[1])

    def by_head(weight, order):
        return dot(order, weight, ((0,), (1,))).astype(BF16).reshape(HEADS, -1, part)

    send_qkv = jnp.concatenate(
        [by_head(w_query, order_q), by_head(w_key, order_q), by_head(w_value, order_v)], axis=1
    )
    send_go = jnp.concatenate(
        [
            by_head(w_gate, order_v),
            dot(order_v, w_out, ((0,), (0,))).astype(BF16).reshape(HEADS, -1, part),
        ],
        axis=1,
    )

    def to_heads(send):
        got = lax.all_to_all(send, GROUP, split_axis=0, concat_axis=0, tiled=True)
        got = got.reshape(4, 2, send.shape[1], part).transpose(1, 2, 0, 3)
        return got.reshape(2, send.shape[1], width)

    got_qkv = to_heads(send_qkv)
    got_go = to_heads(send_go)
    mine_qkv = jnp.concatenate(
        [
            got_qkv[:, :kq].reshape(2 * kq, width),
            got_qkv[:, kq : 2 * kq].reshape(2 * kq, width),
            got_qkv[:, 2 * kq :].reshape(2 * kv, width),
        ],
        axis=0,
    )
    mine_go = jnp.concatenate(
        [got_go[:, :kv].reshape(2 * kv, width), got_go[:, kv:].reshape(2 * kv, width)], axis=0
    )

    def to_units(weight):
        got = row_exchange(weight.reshape(4, -1, part))
        return got.transpose(1, 0, 2).reshape(-1, width)

    mine_up = to_units(w_up.T)
    mine_down = to_units(w_down)

    def planes(mine):
        return lax.all_gather(mine, "z", axis=0, tiled=True)

    all_qkv = planes(mine_qkv)
    all_go = planes(mine_go).reshape(depth, 4 * kv, width)
    wt_gate = all_go[:, : 2 * kv].reshape(-1, width)
    wt_out = all_go[:, 2 * kv :].reshape(-1, width)
    wt_up = planes(mine_up)
    wt_down = planes(mine_down)

    params = lax.all_gather(
        jnp.stack(
            [
                retention_norm_gain,
                retention_norm_bias,
                feedforward_norm_gain,
                feedforward_norm_bias,
            ]
        ),
        ROW,
        axis=1,
        tiled=True,
    )
    stream = to_tokens(block_in).astype(F32)
    cot_own = to_tokens(cotangent)
    hat_one, inv_one, norm_one = layernorm(stream, params[0], params[1])
    x_one = group_gather(norm_one)
    cot = group_gather(cot_own)

    segs = lax.all_gather(segments, ROW, axis=0, tiled=True).reshape(depth, 8, tokens)
    ids = lax.iota(jnp.int32, 8) ^ own
    ids = (ids % 2) * 4 + ids // 2
    picked = (ids[:, None] == lax.iota(jnp.int32, 8)[None, :])[:, :, None]
    here = (lax.iota(jnp.int32, depth) == plane)[:, None, None]
    seg_plane = jnp.sum(jnp.where(here, segs, 0), axis=0)
    seg = jnp.sum(jnp.where(picked, seg_plane[None], 0), axis=1).reshape(seq)
    pos = (ids[:, None] * tokens + lax.iota(jnp.int32, tokens)[None, :]).reshape(seq)

    loggam = jnp.log1p(-jnp.exp2(-5.0 - own.astype(F32)))
    gap = pos[:, None] - pos[None, :]
    inside = (gap >= 0) & (seg[:, None] == seg[None, :])
    decay = jnp.where(inside, jnp.exp(jnp.maximum(gap, 0).astype(F32) * loggam), F32(0.0))
    scale = (kq * 2 * depth) ** (-0.5)

    qkv = dot(all_qkv, x_one, ((1,), (1,))).astype(BF16).reshape(depth, -1, seq)
    query = qkv[:, : 2 * kq].reshape(-1, seq)
    keys = qkv[:, 2 * kq : 4 * kq].reshape(-1, seq)
    values = qkv[:, 4 * kq :].reshape(-1, seq)
    raw = dot(query, keys, ((0,), (0,)))
    weights = (raw * scale * decay).astype(BF16)
    retained = dot(values, weights, ((1,), (1,)))
    centered = retained - jnp.mean(retained, axis=0, keepdims=True)
    inv_group = lax.rsqrt(jnp.mean(centered * centered, axis=0, keepdims=True) + EPS_GROUP)
    normed = centered * inv_group
    normed_low = normed.astype(BF16).astype(F32)
    gate = dot(wt_gate, x_one, ((1,), (1,)))
    sigma = jax.nn.sigmoid(gate)
    swish = gate * sigma
    hidden = (swish * normed_low).astype(BF16)
    middle = stream + group_reduce(dot(hidden, wt_out, ((0,), (0,))))

    hat_two, inv_two, norm_two = layernorm(middle, params[2], params[3])
    x_two = group_gather(norm_two)
    pre = dot(wt_up, x_two, ((1,), (1,)))
    act_wide, act_pull = jax.vjp(gelu_exact, pre)
    act = act_wide.astype(BF16)
    grad_act = dot(wt_down, cot, ((1,), (1,)))
    grad_pre = act_pull(grad_act)[0].astype(BF16)
    grad_two = group_reduce(dot(grad_pre, wt_up, ((0,), (0,))))
    ffn = group_reduce(dot(act, wt_down, ((0,), (0,))))
    block_out = from_tokens((middle + ffn).astype(BF16))

    def home(full):
        return lax.psum_scatter(full.astype(BF16), "z", scatter_dimension=0, tiled=True)

    def from_units(mine):
        send = mine.reshape(-1, 4, part).transpose(1, 0, 2)
        return row_exchange(send).reshape(-1, part)

    grad_down = from_units(home(dot(act, cot, ((1,), (0,))))).astype(F32)
    grad_up = from_units(home(dot(grad_pre, x_two, ((1,), (0,))))).T.astype(F32)

    back_two, grad_ffn_gain, grad_ffn_bias = layernorm_back(grad_two, hat_two, inv_two, params[2])
    grad_mid = cot_own.astype(F32) + back_two
    x_mid = group_gather(grad_mid.astype(BF16))

    grad_out_full = dot(hidden, x_mid, ((1,), (0,)))
    grad_hidden = dot(wt_out, x_mid, ((1,), (1,)))
    grad_gate = (grad_hidden * normed_low * (sigma * (1.0 + gate * (1.0 - sigma)))).astype(BF16)
    grad_normed = (grad_hidden * swish).astype(BF16).astype(F32)
    grad_ret = (
        inv_group
        * (
            grad_normed
            - jnp.mean(grad_normed, axis=0, keepdims=True)
            - normed * jnp.mean(grad_normed * normed, axis=0, keepdims=True)
        )
    ).astype(BF16)
    grad_scores = (dot(grad_ret, values, ((0,), (0,))) * decay * scale).astype(BF16)
    grad_q = dot(keys, grad_scores, ((1,), (1,))).astype(BF16)
    grad_k = dot(query, grad_scores, ((1,), (0,))).astype(BF16)
    grad_v = dot(grad_ret, weights, ((1,), (0,))).astype(BF16)
    grad_qkv = jnp.concatenate(
        [
            grad_q.reshape(depth, -1, seq),
            grad_k.reshape(depth, -1, seq),
            grad_v.reshape(depth, -1, seq),
        ],
        axis=1,
    ).reshape(-1, seq)
    grad_one = group_reduce(
        dot(grad_qkv, all_qkv, ((0,), (0,))) + dot(grad_gate, wt_gate, ((0,), (0,)))
    )

    def from_heads(mine, count):
        send = mine.reshape(2, count, 4, part).transpose(2, 0, 1, 3).reshape(8, count, part)
        return lax.all_to_all(send, GROUP, split_axis=0, concat_axis=0, tiled=True)

    home_go = home(
        jnp.concatenate(
            [
                dot(grad_gate, x_one, ((1,), (0,))).reshape(depth, -1, width),
                grad_out_full.reshape(depth, -1, width),
            ],
            axis=1,
        ).reshape(-1, width)
    )
    home_qkv = home(dot(grad_qkv, x_one, ((1,), (0,))))
    go = from_heads(
        jnp.concatenate(
            [home_go[: 2 * kv].reshape(2, kv, width), home_go[2 * kv :].reshape(2, kv, width)],
            axis=1,
        ),
        2 * kv,
    )
    back = from_heads(
        jnp.concatenate(
            [
                home_qkv[: 2 * kq].reshape(2, kq, width),
                home_qkv[2 * kq : 4 * kq].reshape(2, kq, width),
                home_qkv[4 * kq :].reshape(2, kv, width),
            ],
            axis=1,
        ),
        2 * kq + kv,
    )

    def columns(grads, order):
        return dot(grads.reshape(-1, part), order, ((0,), (1,)))

    out_gate = columns(go[:, :kv], order_v)
    out_out = dot(order_v, go[:, kv:].reshape(-1, part), ((1,), (0,)))
    out_query = columns(back[:, :kq], order_q)
    out_key = columns(back[:, kq : 2 * kq], order_q)
    out_value = columns(back[:, 2 * kq :], order_v)

    back_one, grad_attn_gain, grad_attn_bias = layernorm_back(grad_one, hat_one, inv_one, params[0])
    grad_in = from_tokens((grad_mid + back_one).astype(BF16)).astype(F32)
    totals = lax.psum(
        jnp.stack([grad_attn_gain, grad_attn_bias, grad_ffn_gain, grad_ffn_bias]), EVERY
    )
    totals = lax.dynamic_slice_in_dim(totals, lax.axis_index(ROW) * part, part, 1)
    return (
        block_out,
        grad_in,
        out_query,
        out_key,
        out_value,
        out_gate,
        out_out,
        grad_up,
        grad_down,
        totals[0],
        totals[1],
        totals[2],
        totals[3],
    )


def solution(mesh):
    rows, cols = mesh.devices.shape
    fine = Mesh(mesh.devices.reshape(rows // 2, 2, cols // 2, 2), ("x", "k", "z", "y"))
    row, col = ("x", "k"), ("z", "y")
    tok, unit = P(col, row), P(row, col)
    return jax.shard_map(
        body,
        mesh=fine,
        in_specs=(tok, tok, P(row), unit, unit, unit, unit, tok, unit, tok)
        + (P(row),) * 4,
        out_specs=(tok, tok, unit, unit, unit, unit, tok, unit, tok) + (P(row),) * 4,
        check_vma=False,
    )
```

time: 2200 us -> 729 us (0.33)
  waiting for transfers between devices: 1790 us -> 303 us
  starting transfers between devices: 17.2 us -> 65.1 us
  matrix products: 113 us -> 89.4 us
    reduce_scatter x6 -> x4, waiting for transfers between devices: 685 us -> 14.4 us  [home(): lax.psum_scatter(full.astype(BF16), 'z', scatter_dimension=0, tiled=True)]
    unnamed x18 -> x8, waiting for transfers between devices: 572 us -> 0.13 us
    all_gather x8 -> x4, waiting for transfers between devices: 439 us -> 104 us  [planes(): return lax.all_gather(mine, 'z', axis=0, tiled=True)]
    ppermute x0 -> x32, waiting for transfers between devices: none -> 134 us  [swap(): return lax.ppermute(value, GROUP, [(i, i ^ mask) for i in range(8)])]
    all_to_all x3 -> x9, waiting for transfers between devices: 98.3 us -> 50 us  [the longest x7 39.7 us: row_exchange(): return lax.all_to_all(parts, ROW, split_axis=0, concat_axis=0, tiled=True)]
    ppermute x0 -> x32, starting transfers between devices: none -> 30.4 us  [swap(): return lax.ppermute(value, GROUP, [(i, i ^ mask) for i in range(8)])]
    dot_general x22 -> x31, matrix products: 113 us -> 89.4 us  [dot(): lax.dot_general(left, right, (over, ((), ())), preferred_element_type=F32)]
    all_to_all x1 -> x3, blocking collectives: 51.9 us -> 47.9 us  [the longest x2 36.4 us: to_heads(): got = lax.all_to_all(send, GROUP, split_axis=0, concat_axis=0, tiled=True)]
  transfers between devices with their start and end apart: 19 -> 49, of which waited for: 19 -> 24; matrix products, arithmetic and copies ran while one was open for 4% -> 20% of each run, Pallas kernels for 0% -> 0%
where the time goes in v1:
time: 729 us; the launch traced here: 720 us
  waiting for transfers between devices  303 us (42%)
  blocking collectives  115 us (16%)
  matrix products  89.4 us (12%)
  local copies, waits for them, and re-layouts  75 us (10%)
  starting transfers between devices  65.1 us (9%)
  other arithmetic  56.8 us (8%)
  between operations  16 us (2%)
    ppermute x32, waiting for transfers between devices, swap(): return lax.ppermute(value, GROUP, [(i, i ^ mask) for i in range(8)])  134 us
    all_gather x4, waiting for transfers between devices, planes(): return lax.all_gather(mine, 'z', axis=0, tiled=True)  104 us
    dot_general x31, matrix products, dot(): lax.dot_general(left, right, (over, ((), ())), preferred_element_type=F32)  89.4 us
    psum x1, blocking collectives, body(): lax.psum(jnp.stack([grad_attn_gain, grad_attn_bias, grad_ffn_gain, grad_f...  52.2 us
    all_to_all x7, waiting for transfers between devices, row_exchange(): return lax.all_to_all(parts, ROW, split_axis=0, concat_axis=0, tiled=True)  39.7 us
    all_to_all x2, blocking collectives, to_heads(): got = lax.all_to_all(send, GROUP, split_axis=0, concat_axis=0, tiled=True)  36.4 us
    unnamed x118, local copies, waits for them, and re-layouts  33.2 us
    ppermute x32, starting transfers between devices, swap(): return lax.ppermute(value, GROUP, [(i, i ^ mask) for i in range(8)])  30.4 us
  transfers between devices with their start and end apart: 49, of which 24 were waited for; matrix products, arithmetic and copies ran while one was open for 20% of the time, Pallas kernels for 0%

profile of v1, /device:TPU:0, one launch (start us, length us, event | category | flops | bytes accessed | tf_op | source)
XLA Modules:
  0.0 720.1 jit_solution(10810222214048122269)
XLA Ops:
  10.6 19.4 %all_to_all.60 = bf16[8,128,512]{2,1,0:T(8,128)(2,1)S(1)} all-to-all(bf16[8,128,512]{2,1,0:T(8,128)(2,1)S(1)} %pad_maximum_fusion.10), channel_id=1, replica_groups=mesh['x'=2,'k'=2,'z'=4,'y'=2] {'x','k','y'}, dimensions={0} | all-to-all | bytes 2097152 | tf_op jit(solution)/shard_map/all_to_all | solution.py:131
  34.4 17.0 %all_to_all.61 = bf16[8,128,512]{2,1,0:T(8,128)(2,1)S(1)} all-to-all(bf16[8,128,512]{2,1,0:T(8,128)(2,1)S(1)} %pad_maximum_fusion.12), channel_id=1, replica_groups=mesh['x'=2,'k'=2,'z'=4,'y'=2] {'x','k','y'}, dimensions={0} | all-to-all | bytes 2097152 | tf_op jit(solution)/shard_map/all_to_all | solution.py:131
  59.7 9.8 %all_gather.19 = f32[4,2048]{1,0:T(4,128)S(1)} all-gather(f32[4,512]{1,0:T(4,128)S(1)} %pad_maximum_fusion.16), channel_id=1, replica_groups=mesh['x'=2,'k'=2,'z'=4,'y'=2] {'x','k'}, dimensions={1}, use_global_device_ids=true | all-gather | bytes 40960 | tf_op jit(solution)/shard_map/all_gather | solution.py:166
  76.6 10.8 %collective-permute-done.2 = bf16[128,2048]{1,0:T(8,128)(2,1)} collective-permute-done((bf16[128,2048]{1,0:T(8,128)(2,1)}, bf16[128,2048]{1,0:T(8,128)(2,1)}, u32[]{:S(2)}, u32[]{:S(2)}) %collective-permute-start.2) | collective-permute-done | bytes 524320 | tf_op jit(solution)/shard_map/ppermute | solution.py:23
  87.4 10.6 %collective-permute-done.1 = bf16[128,2048]{1,0:T(8,128)(2,1)} collective-permute-done((bf16[128,2048]{1,0:T(8,128)(2,1)}, bf16[128,2048]{1,0:T(8,128)(2,1)}, u32[]{:S(2)}, u32[]{:S(2)}) %collective-permute-start.1) | collective-permute-done | bytes 524320 | tf_op jit(solution)/shard_map/ppermute | solution.py:23
  99.8 5.4 all_gather.21
  114.1 4.7 fusion.117
  118.8 76.7 %all-gather.7.cloned.1.call-done = bf16[1024,2048]{1,0:T(8,128)(2,1)} async-done(((bf16[256,2048]{1,0:T(8,128)(2,1)}), bf16[1024,2048]{1,0:T(8,128)(2,1)}) %all-gather.7.cloned.1.call-update) | async-done | bytes 4194320 | tf_op jit(solution)/shard_map/all_gather | solution.py:157
  195.5 8.0 %convolution_convert_fusion.5 = bf16[1024,1024]{1,0:T(8,128)(2,1)S(1)} fusion(bf16[1024,2048]{1,0:T(8,128)(2,1)} %all-gather.7.cloned.1.call-done, bf16[1024,2048]{1,0:T(8,128)(2,1)} %bitcast.420), kind=kOutput, calls=%fused_computation.105 | convolution fusion | flops 4296015872 | bytes 10485760 | tf_op jit(solution)/shard_map/dot_general | solution.py:19
  249.4 20.6 %all-to-all-done.3 = bf16[4,128,512]{2,1,0:T(8,128)(2,1)S(1)} async-done(((bf16[4,128,512]{2,1,0:T(8,128)(2,1)}), bf16[4,128,512]{2,1,0:T(8,128)(2,1)S(1)}, u32[]{:S(2)}, u32[]{:S(2)}) %all-to-all-start.3) | async-done | bytes 524320 | tf_op jit(solution)/shard_map/all_to_all | solution.py:42
  277.5 4.8 collective-permute-done.18
  283.8 8.8 %collective-permute-done.17 = bf16[128,2048]{1,0:T(8,128)(2,1)} collective-permute-done((bf16[128,2048]{1,0:T(8,128)(2,1)S(1)}, bf16[128,2048]{1,0:T(8,128)(2,1)}, u32[]{:S(2)}, u32[]{:S(2)}) %collective-permute-start.17) | collective-permute-done | bytes 524320 | tf_op jit(solution)/shard_map/ppermute | solution.py:23
  295.7 8.1 %collective-permute-done.9 = bf16[128,2048]{1,0:T(8,128)(2,1)S(1)} collective-permute-done((bf16[128,2048]{1,0:T(8,128)(2,1)S(1)}, bf16[128,2048]{1,0:T(8,128)(2,1)S(1)}, u32[]{:S(2)}, u32[]{:S(2)}) %collective-permute-start.9) | collective-permute-done | bytes 524320 | tf_op jit(solution)/shard_map/ppermute | solution.py:23
  304.6 10.2 %collective-permute-done.10 = bf16[128,2048]{1,0:T(8,128)(2,1)S(1)} collective-permute-done((bf16[128,2048]{1,0:T(8,128)(2,1)S(1)}, bf16[128,2048]{1,0:T(8,128)(2,1)S(1)}, u32[]{:S(2)}, u32[]{:S(2)}) %collective-permute-start.10) | collective-permute-done | bytes 524320 | tf_op jit(solution)/shard_map/ppermute | solution.py:23
  316.5 11.5 %all_to_all.62 = bf16[4,128,512]{2,1,0:T(8,128)(2,1)S(1)} all-to-all(bf16[4,128,512]{2,1,0:T(8,128)(2,1)S(1)} %bitcast.472), channel_id=1, replica_groups=mesh['x'=2,'k'=2,'z'=4,'y'=2] {'x','k'}, dimensions={0} | all-to-all | bytes 1048576 | tf_op jit(solution)/shard_map/all_to_all | solution.py:42
  329.1 4.7 pad_maximum_fusion.2
  338.4 10.8 %fusion.40 = (bf16[512,1024]{1,0:T(8,128)(2,1)}, f32[512,1024]{1,0:T(8,128)}, f32[1024,512]{0,1:T(8,128)}) fusion(bf16[1024,2048]{1,0:T(8,128)(2,1)} %bitcast.427, bf16[512,2048]{0,1:T(8,128)(2,1)} %all-gather.9.cloned.1.call-done), kind=kOutput, calls=%fused_computation.81 | convolution fusion | flops 2181562368 | bytes 11534336 | tf_op jit(solution)/shard_map/dot_general | solution.py:19
  349.2 22.8 %all-gather.11.cloned.1.call-done = bf16[512,2048]{0,1:T(8,128)(2,1)} async-done(((bf16[128,2048]{0,1:T(8,128)(2,1)}), bf16[512,2048]{0,1:T(8,128)(2,1)}) %all-gather.11.cloned.1.call-update) | async-done | bytes 2097168 | tf_op jit(solution)/shard_map/all_gather | solution.py:157
  372.1 7.1 fusion.37
  411.7 17.0 %collective-permute-done.21 = bf16[128,2048]{1,0:T(8,128)(2,1)S(1)} collective-permute-done((bf16[128,2048]{1,0:T(8,128)(2,1)S(1)}, bf16[128,2048]{1,0:T(8,128)(2,1)S(1)}, u32[]{:S(2)}, u32[]{:S(2)}) %collective-permute-start.21) | collective-permute-done | bytes 524320 | tf_op jit(solution)/shard_map/ppermute | solution.py:23
  430.9 19.1 %collective-permute-done.13 = bf16[128,2048]{1,0:T(8,128)(2,1)S(1)} collective-permute-done((bf16[128,2048]{1,0:T(8,128)(2,1)S(1)}, bf16[128,2048]{1,0:T(8,128)(2,1)S(1)}, u32[]{:S(2)}, u32[]{:S(2)}) %collective-permute-start.13) | collective-permute-done | bytes 524320 | tf_op jit(solution)/shard_map/ppermute | solution.py:23
  456.8 12.3 %collective-permute-done.26 = bf16[128,2048]{1,0:T(8,128)(2,1)S(1)} collective-permute-done((bf16[128,2048]{1,0:T(8,128)(2,1)S(1)}, bf16[128,2048]{1,0:T(8,128)(2,1)S(1)}, u32[]{:S(2)}, u32[]{:S(2)}) %collective-permute-start.26) | collective-permute-done | bytes 524320 | tf_op jit(solution)/shard_map/ppermute | solution.py:23
  469.1 9.3 %collective-permute-done.25 = bf16[128,2048]{1,0:T(8,128)(2,1)S(1)} collective-permute-done((bf16[128,2048]{1,0:T(8,128)(2,1)S(1)}, bf16[128,2048]{1,0:T(8,128)(2,1)S(1)}, u32[]{:S(2)}, u32[]{:S(2)}) %collective-permute-start.25) | collective-permute-done | bytes 524320 | tf_op jit(solution)/shard_map/ppermute | solution.py:23
  512.1 6.0 convolution_convert_fusion
  518.2 7.3 %fusion.131 = f32[1024,2048]{1,0:T(8,128)S(1)} fusion(bf16[1024,1024]{1,0:T(8,128)(2,1)} %bitcast.444, bf16[1024,2048]{1,0:T(8,128)(2,1)} %all-gather.7.cloned.1.call-done), kind=kOutput, calls=%fused_computation.267 | convolution fusion | flops 4294967296 | bytes 14680064 | tf_op jit(solution)/shard_map/dot_general | solution.py:19
  537.4 8.9 %all-to-all-done.5 = bf16[4,128,512]{2,1,0:T(8,128)(2,1)} async-done(((bf16[4,128,512]{2,1,0:T(8,128)(2,1)}), bf16[4,128,512]{2,1,0:T(8,128)(2,1)}, u32[]{:S(2)}, u32[]{:S(2)}) %all-to-all-start.5) | async-done | bytes 524320 | tf_op jit(solution)/shard_map/all_to_all | solution.py:42
  557.7 5.4 all-to-all-done.10
  579.1 15.5 %collective-permute-done.29 = bf16[128,2048]{1,0:T(8,128)(2,1)} collective-permute-done((bf16[128,2048]{1,0:T(8,128)(2,1)}, bf16[128,2048]{1,0:T(8,128)(2,1)}, u32[]{:S(2)}, u32[]{:S(2)}) %collective-permute-start.29) | collective-permute-done | bytes 524320 | tf_op jit(solution)/shard_map/ppermute | solution.py:23
  609.9 4.9 all-to-all-done.7
  618.4 52.2 %psum.7 = f32[4,2048]{1,0:T(4,128)S(1)} all-reduce(f32[4,2048]{1,0:T(4,128)S(1)} %pad_maximum_fusion.15), channel_id=1, replica_groups=mesh['x'=2,'k'=2,'z'=4,'y'=2] {'x','k','z','y'}, use_global_device_ids=true, to_apply=%region_22.23 | all-reduce | flops 8192 | bytes 65536 | tf_op jit(solution)/shard_map/psum | solution.py:314
  671.3 14.4 %reduce-scatter.5.cloned.1.call-done = bf16[256,2048]{1,0:T(8,128)(2,1)} async-done(((bf16[1024,2048]{1,0:T(8,128)(2,1)}), bf16[256,2048]{1,0:T(8,128)(2,1)}) %reduce-scatter.5.cloned.1.call-update) | async-done | bytes 1048592 | tf_op jit(solution)/shard_map/reduce_scatter | solution.py:229
  696.8 10.3 %all-to-all-done.8 = bf16[8,128,512]{2,1,0:T(8,128)(2,1)S(1)} async-done(((bf16[8,128,512]{2,1,0:T(8,128)(2,1)}), bf16[8,128,512]{2,1,0:T(8,128)(2,1)S(1)}, u32[]{:S(2)}, u32[]{:S(2)}) %all-to-all-start.8) | async-done | bytes 1048608 | tf_op jit(solution)/shard_map/all_to_all | solution.py:272
  (345 shorter events, 249.7 us)
Async XLA Ops:
  7.2 106.9 %all-gather.5.cloned.1.call-start = ((), (), s32[]{:S(2)}) async-start(), calls=%async_computation.16 | async-start | bytes 5242880 | tf_op jit(solution)/shard_map/all_gather | solution.py:157
  32.9 162.7 %all-gather.7.cloned.1.call-start = ((), (), s32[]{:S(2)}) async-start(), calls=%async_computation.17 | async-start | bytes 5242880 | tf_op jit(solution)/shard_map/all_gather | solution.py:157
  72.6 25.4 %collective-permute-start.1 = (bf16[128,2048]{1,0:T(8,128)(2,1)}, bf16[128,2048]{1,0:T(8,128)(2,1)}, u32[]{:S(2)}, u32[]{:S(2)}) collective-permute-start(bf16[128,2048]{1,0:T(8,128)(2,1)} %add_convert_fusion.2), channel_id=1, source_target_pairs={{0,16},{1,17},{8,24},{9,25},{16,0},{17,1},{24,8},{25,9},{2,18},{3,... | collective-permute-start | bytes 1572872 | tf_op jit(solution)/shard_map/ppermute | solution.py:23
  74.3 23.7 %collective-permute-start = (bf16[128,2048]{1,0:T(8,128)(2,1)}, bf16[128,2048]{1,0:T(8,128)(2,1)}, u32[]{:S(2)}, u32[]{:S(2)}) collective-permute-start(bf16[128,2048]{1,0:T(8,128)(2,1)} %add_convert_fusion.2), channel_id=1, source_target_pairs={{0,1},{1,0},{8,9},{9,8},{16,17},{17,16},{24,25},{25,24},{2,3},{3,2... | collective-permute-start | bytes 1572872 | tf_op jit(solution)/shard_map/ppermute | solution.py:23
  236.7 34.6 %collective-permute-start.5 = (bf16[128,2048]{1,0:T(8,128)(2,1)}, bf16[128,2048]{1,0:T(8,128)(2,1)}, u32[]{:S(2)}, u32[]{:S(2)}) collective-permute-start(bf16[128,2048]{1,0:T(8,128)(2,1)} %get-tuple-element.48), channel_id=1, source_target_pairs={{0,1},{1,0},{8,9},{9,8},{16,17},{17,16},{24,25},{25,24},{2,3},{3,2... | collective-permute-start | bytes 1572872 | tf_op jit(solution)/shard_map/ppermute | solution.py:23
  238.2 34.7 %collective-permute-start.7 = (bf16[128,2048]{1,0:T(8,128)(2,1)}, bf16[128,2048]{1,0:T(8,128)(2,1)}, u32[]{:S(2)}, u32[]{:S(2)}) collective-permute-start(bf16[128,2048]{1,0:T(8,128)(2,1)} %get-tuple-element.49), channel_id=1, source_target_pairs={{0,17},{1,16},{8,25},{9,24},{16,1},{17,0},{24,9},{25,8},{2,19},{3,... | collective-permute-start | bytes 1572872 | tf_op jit(solution)/shard_map/ppermute | solution.py:23
  239.6 33.3 %collective-permute-start.6 = (bf16[128,2048]{1,0:T(8,128)(2,1)}, bf16[128,2048]{1,0:T(8,128)(2,1)}, u32[]{:S(2)}, u32[]{:S(2)}) collective-permute-start(bf16[128,2048]{1,0:T(8,128)(2,1)} %get-tuple-element.50), channel_id=1, source_target_pairs={{0,16},{1,17},{8,24},{9,25},{16,0},{17,1},{24,8},{25,9},{2,18},{3,... | collective-permute-start | bytes 1572872 | tf_op jit(solution)/shard_map/ppermute | solution.py:23
  241.2 28.8 %all-to-all-start.3 = ((bf16[4,128,512]{2,1,0:T(8,128)(2,1)}), bf16[4,128,512]{2,1,0:T(8,128)(2,1)S(1)}, u32[]{:S(2)}, u32[]{:S(2)}) async-start(bf16[4,128,512]{2,1,0:T(8,128)(2,1)} %bitcast.60), calls=%async_computation.3 | async-start | bytes 1048576 | tf_op jit(solution)/shard_map/all_to_all | solution.py:42
  244.6 93.8 %all-gather.9.cloned.1.call-start = ((), (), s32[]{:S(2)}) async-start(), calls=%async_computation.18 | async-start | bytes 2621440 | tf_op jit(solution)/shard_map/all_gather | solution.py:157
  244.7 37.6 %collective-permute-start.18 = (bf16[128,2048]{1,0:T(8,128)(2,1)S(1)}, bf16[128,2048]{1,0:T(8,128)(2,1)}, u32[]{:S(2)}, u32[]{:S(2)}) collective-permute-start(bf16[128,2048]{1,0:T(8,128)(2,1)S(1)} %bitcast.434), channel_id=1, source_target_pairs={{0,17},{1,16},{8,25},{9,24},{16,1},{17,0},{24,9},{25,8},{2,19},{3,... | collective-permute-start | bytes 1572872 | tf_op jit(solution)/shard_map/ppermute | solution.py:23
  247.7 44.9 %collective-permute-start.17 = (bf16[128,2048]{1,0:T(8,128)(2,1)S(1)}, bf16[128,2048]{1,0:T(8,128)(2,1)}, u32[]{:S(2)}, u32[]{:S(2)}) collective-permute-start(bf16[128,2048]{1,0:T(8,128)(2,1)S(1)} %bitcast.435), channel_id=1, source_target_pairs={{0,16},{1,17},{8,24},{9,25},{16,0},{17,1},{24,8},{25,9},{2,18},{3,... | collective-permute-start | bytes 1572872 | tf_op jit(solution)/shard_map/ppermute | solution.py:23
  271.0 101.0 %all-gather.11.cloned.1.call-start = ((), (), s32[]{:S(2)}) async-start(), calls=%async_computation.19 | async-start | bytes 2621440 | tf_op jit(solution)/shard_map/all_gather | solution.py:157
  275.4 28.3 %collective-permute-start.9 = (bf16[128,2048]{1,0:T(8,128)(2,1)S(1)}, bf16[128,2048]{1,0:T(8,128)(2,1)S(1)}, u32[]{:S(2)}, u32[]{:S(2)}) collective-permute-start(bf16[128,2048]{1,0:T(8,128)(2,1)S(1)} %add_convert_fusion.1), channel_id=1, source_target_pairs={{0,16},{1,17},{8,24},{9,25},{16,0},{17,1},{24,8},{25,9},{2,18},{3,... | collective-permute-start | bytes 1572872 | tf_op jit(solution)/shard_map/ppermute | solution.py:23
  277.0 27.7 %collective-permute-start.8 = (bf16[128,2048]{1,0:T(8,128)(2,1)S(1)}, bf16[128,2048]{1,0:T(8,128)(2,1)S(1)}, u32[]{:S(2)}, u32[]{:S(2)}) collective-permute-start(bf16[128,2048]{1,0:T(8,128)(2,1)S(1)} %add_convert_fusion.1), channel_id=1, source_target_pairs={{0,1},{1,0},{8,9},{9,8},{16,17},{17,16},{24,25},{25,24},{2,3},{3,2... | collective-permute-start | bytes 1572872 | tf_op jit(solution)/shard_map/ppermute | solution.py:23
  282.3 32.5 %collective-permute-start.10 = (bf16[128,2048]{1,0:T(8,128)(2,1)S(1)}, bf16[128,2048]{1,0:T(8,128)(2,1)S(1)}, u32[]{:S(2)}, u32[]{:S(2)}) collective-permute-start(bf16[128,2048]{1,0:T(8,128)(2,1)S(1)} %add_convert_fusion.1), channel_id=1, source_target_pairs={{0,17},{1,16},{8,25},{9,24},{16,1},{17,0},{24,9},{25,8},{2,19},{3,... | collective-permute-start | bytes 1572872 | tf_op jit(solution)/shard_map/ppermute | solution.py:23
  295.4 33.7 %collective-permute-start.19 = (bf16[2,1,2,128,2048]{4,3,2,1,0:T(8,128)(2,1)}, bf16[2,1,2,128,2048]{4,3,2,1,0:T(8,128)(2,1)}, u32[]{:S(2)}, u32[]{:S(2)}) collective-permute-start(bf16[2,1,2,128,2048]{4,3,2,1,0:T(8,128)(2,1)} %bitcast.83), channel_id=1, source_target_pairs={{0,8},{1,9},{8,0},{9,1},{16,24},{17,25},{24,16},{25,17},{2,10},{3,... | collective-permute-start | bytes 6291464 | tf_op jit(solution)/shard_map/ppermute | solution.py:23
  329.0 217.3 %reduce-scatter.9.cloned.1.call-start = ((), (), s32[]{:S(2)}) async-start(), calls=%async_computation.22 | async-start | bytes 2621440 | tf_op jit(solution)/shard_map/reduce_scatter | solution.py:229
  398.5 149.6 %reduce-scatter.11.cloned.1.call-start = ((), (), s32[]{:S(2)}) async-start(), calls=%async_computation.23 | async-start | bytes 2621440 | tf_op jit(solution)/shard_map/reduce_scatter | solution.py:229
  402.6 26.1 %collective-permute-start.21 = (bf16[128,2048]{1,0:T(8,128)(2,1)S(1)}, bf16[128,2048]{1,0:T(8,128)(2,1)S(1)}, u32[]{:S(2)}, u32[]{:S(2)}) collective-permute-start(bf16[128,2048]{1,0:T(8,128)(2,1)S(1)} %get-tuple-element.42), channel_id=1, source_target_pairs={{0,1},{1,0},{8,9},{9,8},{16,17},{17,16},{24,25},{25,24},{2,3},{3,2... | collective-permute-start | bytes 1572872 | tf_op jit(solution)/shard_map/ppermute | solution.py:23
  404.2 26.0 %collective-permute-start.23 = (bf16[128,2048]{1,0:T(8,128)(2,1)S(1)}, bf16[128,2048]{1,0:T(8,128)(2,1)S(1)}, u32[]{:S(2)}, u32[]{:S(2)}) collective-permute-start(bf16[128,2048]{1,0:T(8,128)(2,1)S(1)} %get-tuple-element.43), channel_id=1, source_target_pairs={{0,17},{1,16},{8,25},{9,24},{16,1},{17,0},{24,9},{25,8},{2,19},{3,... | collective-permute-start | bytes 1572872 | tf_op jit(solution)/shard_map/ppermute | solution.py:23
  405.6 24.6 %collective-permute-start.22 = (bf16[128,2048]{1,0:T(8,128)(2,1)S(1)}, bf16[128,2048]{1,0:T(8,128)(2,1)S(1)}, u32[]{:S(2)}, u32[]{:S(2)}) collective-permute-start(bf16[128,2048]{1,0:T(8,128)(2,1)S(1)} %get-tuple-element.44), channel_id=1, source_target_pairs={{0,16},{1,17},{8,24},{9,25},{16,0},{17,1},{24,8},{25,9},{2,18},{3,... | collective-permute-start | bytes 1572872 | tf_op jit(solution)/shard_map/ppermute | solution.py:23
  408.6 41.4 %collective-permute-start.13 = (bf16[128,2048]{1,0:T(8,128)(2,1)S(1)}, bf16[128,2048]{1,0:T(8,128)(2,1)S(1)}, u32[]{:S(2)}, u32[]{:S(2)}) collective-permute-start(bf16[128,2048]{1,0:T(8,128)(2,1)S(1)} %get-tuple-element.45), channel_id=1, source_target_pairs={{0,1},{1,0},{8,9},{9,8},{16,17},{17,16},{24,25},{25,24},{2,3},{3,2... | collective-permute-start | bytes 1572872 | tf_op jit(solution)/shard_map/ppermute | solution.py:23
  410.2 39.8 %collective-permute-start.15 = (bf16[128,2048]{1,0:T(8,128)(2,1)S(1)}, bf16[128,2048]{1,0:T(8,128)(2,1)S(1)}, u32[]{:S(2)}, u32[]{:S(2)}) collective-permute-start(bf16[128,2048]{1,0:T(8,128)(2,1)S(1)} %get-tuple-element.46), channel_id=1, source_target_pairs={{0,17},{1,16},{8,25},{9,24},{16,1},{17,0},{24,9},{25,8},{2,19},{3,... | collective-permute-start | bytes 1572872 | tf_op jit(solution)/shard_map/ppermute | solution.py:23
  428.7 22.7 %collective-permute-start.14 = (bf16[128,2048]{1,0:T(8,128)(2,1)S(1)}, bf16[128,2048]{1,0:T(8,128)(2,1)S(1)}, u32[]{:S(2)}, u32[]{:S(2)}) collective-permute-start(bf16[128,2048]{1,0:T(8,128)(2,1)S(1)} %get-tuple-element.47), channel_id=1, source_target_pairs={{0,16},{1,17},{8,24},{9,25},{16,0},{17,1},{24,8},{25,9},{2,18},{3,... | collective-permute-start | bytes 1572872 | tf_op jit(solution)/shard_map/ppermute | solution.py:23
  455.9 22.6 %collective-permute-start.25 = (bf16[128,2048]{1,0:T(8,128)(2,1)S(1)}, bf16[128,2048]{1,0:T(8,128)(2,1)S(1)}, u32[]{:S(2)}, u32[]{:S(2)}) collective-permute-start(bf16[128,2048]{1,0:T(8,128)(2,1)S(1)} %get-tuple-element.27), channel_id=1, source_target_pairs={{0,16},{1,17},{8,24},{9,25},{16,0},{17,1},{24,8},{25,9},{2,18},{3,... | collective-permute-start | bytes 1572872 | tf_op jit(solution)/shard_map/ppermute | solution.py:23
  484.4 121.6 %reduce-scatter.7.cloned.1.call-start = ((), (), s32[]{:S(2)}) async-start(), calls=%async_computation.21 | async-start | bytes 5242880 | tf_op jit(solution)/shard_map/reduce_scatter | solution.py:229
  499.3 186.3 %reduce-scatter.5.cloned.1.call-start = ((), (), s32[]{:S(2)}) async-start(), calls=%async_computation.20 | async-start | bytes 5242880 | tf_op jit(solution)/shard_map/reduce_scatter | solution.py:229
  531.7 22.5 %collective-permute-start.28 = (bf16[2,2,128,2048]{3,2,1,0:T(8,128)(2,1)S(1)}, bf16[2,2,128,2048]{3,2,1,0:T(8,128)(2,1)}, u32[]{:S(2)}, u32[]{:S(2)}) collective-permute-start(bf16[2,2,128,2048]{3,2,1,0:T(8,128)(2,1)S(1)} %fusion.31), channel_id=1, source_target_pairs={{0,8},{1,9},{8,0},{9,1},{16,24},{17,25},{24,16},{25,17},{2,10},{3,... | collective-permute-start | bytes 6291464 | tf_op jit(solution)/shard_map/ppermute | solution.py:23
  568.7 25.8 %collective-permute-start.29 = (bf16[128,2048]{1,0:T(8,128)(2,1)}, bf16[128,2048]{1,0:T(8,128)(2,1)}, u32[]{:S(2)}, u32[]{:S(2)}) collective-permute-start(bf16[128,2048]{1,0:T(8,128)(2,1)} %get-tuple-element.37), channel_id=1, source_target_pairs={{0,1},{1,0},{8,9},{9,8},{16,17},{17,16},{24,25},{25,24},{2,3},{3,2... | collective-permute-start | bytes 1572872 | tf_op jit(solution)/shard_map/ppermute | solution.py:23
  570.1 24.4 %collective-permute-start.31 = (bf16[128,2048]{1,0:T(8,128)(2,1)}, bf16[128,2048]{1,0:T(8,128)(2,1)}, u32[]{:S(2)}, u32[]{:S(2)}) collective-permute-start(bf16[128,2048]{1,0:T(8,128)(2,1)} %get-tuple-element.38), channel_id=1, source_target_pairs={{0,17},{1,16},{8,25},{9,24},{16,1},{17,0},{24,9},{25,8},{2,19},{3,... | collective-permute-start | bytes 1572872 | tf_op jit(solution)/shard_map/ppermute | solution.py:23
  572.1 26.8 %collective-permute-start.30 = (bf16[128,2048]{1,0:T(8,128)(2,1)}, bf16[128,2048]{1,0:T(8,128)(2,1)}, u32[]{:S(2)}, u32[]{:S(2)}) collective-permute-start(bf16[128,2048]{1,0:T(8,128)(2,1)} %get-tuple-element.39), channel_id=1, source_target_pairs={{0,16},{1,17},{8,24},{9,25},{16,0},{17,1},{24,8},{25,9},{2,18},{3,... | collective-permute-start | bytes 1572872 | tf_op jit(solution)/shard_map/ppermute | solution.py:23
  614.7 74.0 %all-to-all-start.9 = ((bf16[8,128,512]{2,1,0:T(8,128)(2,1)}), bf16[8,128,512]{2,1,0:T(8,128)(2,1)S(1)}, u32[]{:S(2)}, u32[]{:S(2)}) async-start(bf16[8,128,512]{2,1,0:T(8,128)(2,1)} %bitcast.126), calls=%async_computation.11 | async-start | bytes 2097152 | tf_op jit(solution)/shard_map/all_to_all | solution.py:272
  (76 other events, 578.0 us)
Sparse Core Ops, SparseCore 0:
  33.0 81.0 all-gather.4
  116.2 79.2 all-gather.6
  271.1 44.7 all-gather.8
  329.1 42.8 all-gather.10
  398.6 42.0 reduce-scatter.8
  484.5 41.9 reduce-scatter.10
  528.8 76.0 reduce-scatter.6
  607.3 78.2 reduce-scatter.4

commit v2 on v1

--- a/solution.py
+++ b/solution.py
@@ -24,28 +24,62 @@
 
 
 def group_gather(part):
-    near = jnp.stack([part, swap(part, 1), swap(part, 4), swap(part, 5)])
-    near = near.reshape((2, 1, 2) + part.shape)
-    return jnp.concatenate([near, swap(near, 2)], axis=1).reshape((-1,) + part.shape[1:])
+    near = [part, swap(part, 1), swap(part, 4), swap(part, 5)]
+    far = [swap(block, 2) for block in near]
+    return jnp.concatenate(near[:2] + far[:2] + near[2:] + far[2:], axis=0)
 
 
 def group_reduce(total):
-    blocks = total.reshape(2, 2, 2, total.shape[0] // 8, total.shape[1])
-    pair = (blocks[:, 0] + swap(blocks[:, 1].astype(BF16), 2).astype(F32)).astype(BF16)
-    own = pair[0, 0].astype(F32)
-    for i, j in ((0, 1), (1, 0), (1, 1)):
-        own = own + swap(pair[i, j], 4 * i + j).astype(F32)
-    return own
+    height = total.shape[0] // 8
+    half = height // 2
+
+    def pair(j):
+        kept = total[j * height : (j + 1) * height]
+        sent = total[(j + 2) * height : (j + 3) * height].astype(BF16)
+        return kept + swap(sent, 2).astype(F32)
+
+    across, over_x, over_y, own = pair(5).astype(BF16), pair(4), pair(1), pair(0)
+    top, low = swap(across[:half], 1).astype(F32), swap(across[half:], 4).astype(F32)
+    over_x = jnp.concatenate([over_x[:half] + top, over_x[half:]], axis=0).astype(BF16)
+    over_y = jnp.concatenate([over_y[:half], over_y[half:] + low], axis=0).astype(BF16)
+    return own + swap(over_x, 4).astype(F32) + swap(over_y, 1).astype(F32)
+
+
+def after(value, *others):
+    return lax.optimization_barrier((value,) + others)[0]
+
+
+def total_over_all(value):
+    for mask in (2, 1, 4):
+        value = value + swap(value, mask)
+    depth = lax.axis_size("z")
+    if depth > 4:
+        return lax.psum(value, "z")
+    own = value
+    for step in range(1, depth):
+        value = value + lax.ppermute(own, "z", [(i, (i + step) % depth) for i in range(depth)])
+    return value
+
+
+def row_gather(value):
+    got = [value, swap(value, 2), swap(value, 4), swap(value, 6)]
+    own = lax.axis_index(ROW)
+    rows = []
+    for i in range(4):
+        picks = [jnp.where((own ^ j) == i, got[j], 0.0) for j in range(4)]
+        rows.append(picks[0] + picks[1] + picks[2] + picks[3])
+    return jnp.stack(rows)
 
 
 def row_exchange(parts):
     return lax.all_to_all(parts, ROW, split_axis=0, concat_axis=0, tiled=True)
 
 
-def to_tokens(part):
-    tokens, width = part.shape
-    moved = row_exchange(part.reshape(4, tokens // 4, width))
-    return moved.transpose(1, 0, 2).reshape(tokens // 4, 4 * width)
+def to_wide(*parts):
+    height, width = parts[0].shape
+    moved = row_exchange(jnp.stack([p.reshape(4, -1, width) for p in parts], axis=1))
+    moved = moved.transpose(1, 2, 0, 3).reshape(len(parts), height // 4, 4 * width)
+    return [moved[i] for i in range(len(parts))]
 
 
 def from_tokens(part):
@@ -116,24 +150,19 @@
     def by_head(weight, order):
         return dot(order, weight, ((0,), (1,))).astype(BF16).reshape(HEADS, -1, part)
 
-    send_qkv = jnp.concatenate(
-        [by_head(w_query, order_q), by_head(w_key, order_q), by_head(w_value, order_v)], axis=1
-    )
-    send_go = jnp.concatenate(
-        [
-            by_head(w_gate, order_v),
-            dot(order_v, w_out, ((0,), (0,))).astype(BF16).reshape(HEADS, -1, part),
-        ],
-        axis=1,
-    )
-
     def to_heads(send):
         got = lax.all_to_all(send, GROUP, split_axis=0, concat_axis=0, tiled=True)
         got = got.reshape(4, 2, send.shape[1], part).transpose(1, 2, 0, 3)
         return got.reshape(2, send.shape[1], width)
 
-    got_qkv = to_heads(send_qkv)
-    got_go = to_heads(send_go)
+    def planes(mine):
+        return lax.all_gather(mine, "z", axis=0, tiled=True)
+
+    got_qkv = to_heads(
+        jnp.concatenate(
+            [by_head(w_query, order_q), by_head(w_key, order_q), by_head(w_value, order_v)], axis=1
+        )
+    )
     mine_qkv = jnp.concatenate(
         [
             got_qkv[:, :kq].reshape(2 * kq, width),
@@ -142,47 +171,41 @@
         ],
         axis=0,
     )
+    all_qkv = planes(mine_qkv)
+    send_go = jnp.concatenate(
+        [
+            by_head(w_gate, order_v),
+            dot(order_v, w_out, ((0,), (0,))).astype(BF16).reshape(HEADS, -1, part),
+        ],
+        axis=1,
+    )
+    got_go = to_heads(after(send_go, mine_qkv))
     mine_go = jnp.concatenate(
         [got_go[:, :kv].reshape(2 * kv, width), got_go[:, kv:].reshape(2 * kv, width)], axis=0
     )
-
-    def to_units(weight):
-        got = row_exchange(weight.reshape(4, -1, part))
-        return got.transpose(1, 0, 2).reshape(-1, width)
-
-    mine_up = to_units(w_up.T)
-    mine_down = to_units(w_down)
-
-    def planes(mine):
-        return lax.all_gather(mine, "z", axis=0, tiled=True)
-
-    all_qkv = planes(mine_qkv)
     all_go = planes(mine_go).reshape(depth, 4 * kv, width)
-    wt_gate = all_go[:, : 2 * kv].reshape(-1, width)
-    wt_out = all_go[:, 2 * kv :].reshape(-1, width)
-    wt_up = planes(mine_up)
-    wt_down = planes(mine_down)
-
-    params = lax.all_gather(
-        jnp.stack(
-            [
-                retention_norm_gain,
-                retention_norm_bias,
-                feedforward_norm_gain,
-                feedforward_norm_bias,
-            ]
-        ),
-        ROW,
-        axis=1,
-        tiled=True,
-    )
-    stream = to_tokens(block_in).astype(F32)
-    cot_own = to_tokens(cotangent)
+
+    small = jnp.concatenate(
+        [
+            retention_norm_gain,
+            retention_norm_bias,
+            feedforward_norm_gain,
+            feedforward_norm_bias,
+            segments.astype(F32),
+        ]
+    )
+    small = row_gather(after(small, mine_qkv))
+    params = small[:, : 4 * part].reshape(4, 4, part).transpose(1, 0, 2).reshape(4, width)
+    segs = small[:, 4 * part :].astype(jnp.int32).reshape(depth, 8, tokens)
+    block_in, cotangent = after(block_in, got_go), after(cotangent, got_go)
+    stream_low, cot_own = to_wide(block_in, cotangent)
+    mine_up, mine_down = to_wide(after(w_up, stream_low).T, after(w_down, stream_low))
+    wt_up = planes(after(mine_up, mine_go))
+    wt_down = planes(after(mine_down, mine_go))
+    stream = stream_low.astype(F32)
     hat_one, inv_one, norm_one = layernorm(stream, params[0], params[1])
     x_one = group_gather(norm_one)
-    cot = group_gather(cot_own)
-
-    segs = lax.all_gather(segments, ROW, axis=0, tiled=True).reshape(depth, 8, tokens)
+
     ids = lax.iota(jnp.int32, 8) ^ own
     ids = (ids % 2) * 4 + ids // 2
     picked = (ids[:, None] == lax.iota(jnp.int32, 8)[None, :])[:, :, None]
@@ -197,6 +220,7 @@
     decay = jnp.where(inside, jnp.exp(jnp.maximum(gap, 0).astype(F32) * loggam), F32(0.0))
     scale = (kq * 2 * depth) ** (-0.5)
 
+    x_one = after(x_one, mine_up, mine_down)
     qkv = dot(all_qkv, x_one, ((1,), (1,))).astype(BF16).reshape(depth, -1, seq)
     query = qkv[:, : 2 * kq].reshape(-1, seq)
     keys = qkv[:, 2 * kq : 4 * kq].reshape(-1, seq)
@@ -208,40 +232,45 @@
     inv_group = lax.rsqrt(jnp.mean(centered * centered, axis=0, keepdims=True) + EPS_GROUP)
     normed = centered * inv_group
     normed_low = normed.astype(BF16).astype(F32)
-    gate = dot(wt_gate, x_one, ((1,), (1,)))
+    cot = group_gather(after(cot_own, x_one))
+    retained = after(retained, cot)
+    wt_gate = all_go[:, : 2 * kv].reshape(-1, width)
+    wt_out = all_go[:, 2 * kv :].reshape(-1, width)
+    gate = dot(wt_gate, after(x_one, normed), ((1,), (1,)))
     sigma = jax.nn.sigmoid(gate)
     swish = gate * sigma
     hidden = (swish * normed_low).astype(BF16)
-    middle = stream + group_reduce(dot(hidden, wt_out, ((0,), (0,))))
+    attn = dot(hidden, wt_out, ((0,), (0,)))
+    middle = stream + group_reduce(attn)
 
     hat_two, inv_two, norm_two = layernorm(middle, params[2], params[3])
     x_two = group_gather(norm_two)
+    grad_act = dot(wt_down, cot, ((1,), (1,)))
     pre = dot(wt_up, x_two, ((1,), (1,)))
     act_wide, act_pull = jax.vjp(gelu_exact, pre)
     act = act_wide.astype(BF16)
-    grad_act = dot(wt_down, cot, ((1,), (1,)))
     grad_pre = act_pull(grad_act)[0].astype(BF16)
-    grad_two = group_reduce(dot(grad_pre, wt_up, ((0,), (0,))))
-    ffn = group_reduce(dot(act, wt_down, ((0,), (0,))))
-    block_out = from_tokens((middle + ffn).astype(BF16))
-
-    def home(full):
-        return lax.psum_scatter(full.astype(BF16), "z", scatter_dimension=0, tiled=True)
+    two_part = dot(grad_pre, wt_up, ((0,), (0,)))
+    grad_two = group_reduce(two_part)
+
+    def home(*fulls):
+        fulls = [f.astype(BF16).reshape(depth, -1, width) for f in fulls]
+        full = jnp.concatenate(fulls, axis=1).reshape(-1, width)
+        return lax.psum_scatter(full, "z", scatter_dimension=0, tiled=True)
 
     def from_units(mine):
         send = mine.reshape(-1, 4, part).transpose(1, 0, 2)
         return row_exchange(send).reshape(-1, part)
 
-    grad_down = from_units(home(dot(act, cot, ((1,), (0,))))).astype(F32)
-    grad_up = from_units(home(dot(grad_pre, x_two, ((1,), (0,))))).T.astype(F32)
+    home_ud = home(dot(act, cot, ((1,), (0,))), dot(grad_pre, x_two, ((1,), (0,))))
 
     back_two, grad_ffn_gain, grad_ffn_bias = layernorm_back(grad_two, hat_two, inv_two, params[2])
     grad_mid = cot_own.astype(F32) + back_two
     x_mid = group_gather(grad_mid.astype(BF16))
 
-    grad_out_full = dot(hidden, x_mid, ((1,), (0,)))
     grad_hidden = dot(wt_out, x_mid, ((1,), (1,)))
     grad_gate = (grad_hidden * normed_low * (sigma * (1.0 + gate * (1.0 - sigma)))).astype(BF16)
+    home_go = home(dot(grad_gate, x_one, ((1,), (0,))), dot(hidden, x_mid, ((1,), (0,))))
     grad_normed = (grad_hidden * swish).astype(BF16).astype(F32)
     grad_ret = (
         inv_group
@@ -263,24 +292,34 @@
         ],
         axis=1,
     ).reshape(-1, seq)
+    full_qkv = dot(grad_qkv, x_one, ((1,), (0,))).astype(BF16)
+    home_qkv = home(full_qkv)
+    grad_qkv, grad_gate = after(grad_qkv, full_qkv), after(grad_gate, full_qkv)
     grad_one = group_reduce(
         dot(grad_qkv, all_qkv, ((0,), (0,))) + dot(grad_gate, wt_gate, ((0,), (0,)))
     )
+    ffn = group_reduce(dot(after(act, grad_qkv), wt_down, ((0,), (0,))))
+    block_out = from_tokens((middle + ffn).astype(BF16))
 
     def from_heads(mine, count):
         send = mine.reshape(2, count, 4, part).transpose(2, 0, 1, 3).reshape(8, count, part)
         return lax.all_to_all(send, GROUP, split_axis=0, concat_axis=0, tiled=True)
 
-    home_go = home(
-        jnp.concatenate(
-            [
-                dot(grad_gate, x_one, ((1,), (0,))).reshape(depth, -1, width),
-                grad_out_full.reshape(depth, -1, width),
-            ],
-            axis=1,
-        ).reshape(-1, width)
-    )
-    home_qkv = home(dot(grad_qkv, x_one, ((1,), (0,))))
+    def columns(grads, order):
+        return dot(grads.reshape(-1, part), order, ((0,), (1,)))
+
+    back_one, grad_attn_gain, grad_attn_bias = layernorm_back(grad_one, hat_one, inv_one, params[0])
+    grad_in = from_tokens((grad_mid + back_one).astype(BF16)).astype(F32)
+    totals = total_over_all(
+        jnp.stack([grad_attn_gain, grad_attn_bias, grad_ffn_gain, grad_ffn_bias])
+    )
+    totals = lax.dynamic_slice_in_dim(totals, lax.axis_index(ROW) * part, part, 1)
+
+    home_ud = after(home_ud, grad_one)
+    half = home_ud.shape[0] // 2
+    grad_down = from_units(home_ud[:half]).astype(F32)
+    grad_up = from_units(home_ud[half:]).T.astype(F32)
+    home_go = after(home_go, grad_in, grad_down, grad_up, block_out)
     go = from_heads(
         jnp.concatenate(
             [home_go[: 2 * kv].reshape(2, kv, width), home_go[2 * kv :].reshape(2, kv, width)],
@@ -288,6 +327,7 @@
         ),
         2 * kv,
     )
+    home_qkv = after(home_qkv, go, totals)
     back = from_heads(
         jnp.concatenate(
             [
@@ -299,22 +339,11 @@
         ),
         2 * kq + kv,
     )
-
-    def columns(grads, order):
-        return dot(grads.reshape(-1, part), order, ((0,), (1,)))
-
     out_gate = columns(go[:, :kv], order_v)
     out_out = dot(order_v, go[:, kv:].reshape(-1, part), ((1,), (0,)))
     out_query = columns(back[:, :kq], order_q)
     out_key = columns(back[:, kq : 2 * kq], order_q)
     out_value = columns(back[:, 2 * kq :], order_v)
-
-    back_one, grad_attn_gain, grad_attn_bias = layernorm_back(grad_one, hat_one, inv_one, params[0])
-    grad_in = from_tokens((grad_mid + back_one).astype(BF16)).astype(F32)
-    totals = lax.psum(
-        jnp.stack([grad_attn_gain, grad_attn_bias, grad_ffn_gain, grad_ffn_bias]), EVERY
-    )
-    totals = lax.dynamic_slice_in_dim(totals, lax.axis_index(ROW) * part, part, 1)
     return (
         block_out,
         grad_in,

time: 729 us -> 631 us (0.87)
  blocking collectives: 115 us -> 47.6 us
  waiting for transfers between devices: 303 us -> 280 us
  other arithmetic: 56.8 us -> 35.5 us
  starting transfers between devices: 65.1 us -> 73.8 us
    all_gather x4, waiting for transfers between devices: 104 us -> 51.4 us  [planes(): return lax.all_gather(mine, 'z', axis=0, tiled=True)]
    psum x1 -> x0, blocking collectives: 52.2 us -> none  [body(): lax.psum(jnp.stack([grad_attn_gain, grad_attn_bias, grad_ffn_gain, grad_f...]
    ppermute x32 -> x66, waiting for transfers between devices: 134 us -> 162 us  [swap(): return lax.ppermute(value, GROUP, [(i, i ^ mask) for i in range(8)])]
    convert_element_type x12 -> x2, other arithmetic: 21.7 us -> 2.51 us  [the longest x1 2.01 us: body(): block_out = from_tokens((middle + ffn).astype(BF16))]
    all_gather x2 -> x0, blocking collectives: 15.1 us -> none  [the longest x1 9.79 us: body(): lax.all_gather(jnp.stack([retention_norm_gain, retention_norm_bias, feedf...]
    ppermute x32 -> x66, starting transfers between devices: 30.4 us -> 43.8 us  [swap(): return lax.ppermute(value, GROUP, [(i, i ^ mask) for i in range(8)])]
    concatenate x5 -> x11, other arithmetic: 15.7 us -> 6.34 us  [the longest x2 5.23 us: home(): full = jnp.concatenate(fulls, axis=1).reshape(-1, width)]
    slice x0 -> x22, local copies, waits for them, and re-layouts: none -> 8.91 us  [the longest x4 3.81 us: pair(): sent = total[(j + 2) * height:(j + 3) * height].astype(BF16)]
  transfers between devices with their start and end apart: 49 -> 83, of which waited for: 24 -> 38; matrix products, arithmetic and copies ran while one was open for 20% -> 24% of each run, Pallas kernels for 0% -> 0%
where the time goes in v2:
time: 631 us; the launch traced here: 621 us
  waiting for transfers between devices  280 us (44%)
  matrix products  91.3 us (14%)
  local copies, waits for them, and re-layouts  77.4 us (12%)
  starting transfers between devices  73.8 us (12%)
  blocking collectives  47.6 us (8%)
  other arithmetic  35.5 us (6%)
  between operations  16.3 us (3%)
    ppermute x66, waiting for transfers between devices, swap(): return lax.ppermute(value, GROUP, [(i, i ^ mask) for i in range(8)])  162 us
    dot_general x31, matrix products, dot(): lax.dot_general(left, right, (over, ((), ())), preferred_element_type=F32)  91.3 us
    all_gather x4, waiting for transfers between devices, planes(): return lax.all_gather(mine, 'z', axis=0, tiled=True)  51.4 us
    ppermute x66, starting transfers between devices, swap(): return lax.ppermute(value, GROUP, [(i, i ^ mask) for i in range(8)])  43.8 us
    all_to_all x5, waiting for transfers between devices, row_exchange(): return lax.all_to_all(parts, ROW, split_axis=0, concat_axis=0, tiled=True)  39.3 us
    all_to_all x2, blocking collectives, to_heads(): got = lax.all_to_all(send, GROUP, split_axis=0, concat_axis=0, tiled=True)  36.4 us
    unnamed x143, local copies, waits for them, and re-layouts  27.9 us
    all_to_all x5, starting transfers between devices, row_exchange(): return lax.all_to_all(parts, ROW, split_axis=0, concat_axis=0, tiled=True)  17.7 us
  transfers between devices with their start and end apart: 83, of which 38 were waited for; matrix products, arithmetic and copies ran while one was open for 24% of the time, Pallas kernels for 0%

profile of v2, /device:TPU:0, one launch (start us, length us, event | category | flops | bytes accessed | tf_op | source)
XLA Modules:
  0.0 621.5 jit_solution(15810641262763787621)
XLA Ops:
  10.7 19.4 %all_to_all.50 = bf16[8,128,512]{2,1,0:T(8,128)(2,1)S(1)} all-to-all(bf16[8,128,512]{2,1,0:T(8,128)(2,1)S(1)} %pad_maximum_fusion.4), channel_id=1, replica_groups=mesh['x'=2,'k'=2,'z'=4,'y'=2] {'x','k','y'}, dimensions={0} | all-to-all | bytes 2097152 | tf_op jit(solution)/shard_map/all_to_all | solution.py:154
  37.6 17.0 %all_to_all.51 = bf16[8,128,512]{2,1,0:T(8,128)(2,1)S(1)} all-to-all(bf16[8,128,512]{2,1,0:T(8,128)(2,1)S(1)} %pad_maximum_fusion.3), channel_id=1, replica_groups=mesh['x'=2,'k'=2,'z'=4,'y'=2] {'x','k','y'}, dimensions={0} | all-to-all | bytes 2097152 | tf_op jit(solution)/shard_map/all_to_all | solution.py:154
  69.6 14.3 %all-to-all-done.2 = bf16[4,2,128,512]{3,2,1,0:T(8,128)(2,1)S(1)} async-done(((bf16[4,2,128,512]{3,2,1,0:T(8,128)(2,1)}), bf16[4,2,128,512]{3,2,1,0:T(8,128)(2,1)S(1)}, u32[]{:S(2)}, u32[]{:S(2)}) %all-to-all-start.2) | async-done | bytes 1048608 | tf_op jit(solution)/shard_map/all_to_all | solution.py:75
  96.3 6.1 collective-permute-done.7
  102.4 10.0 %collective-permute-done.6 = bf16[128,2048]{1,0:T(8,128)(2,1)} collective-permute-done((bf16[128,2048]{1,0:T(8,128)(2,1)}, bf16[128,2048]{1,0:T(8,128)(2,1)}, u32[]{:S(2)}, u32[]{:S(2)}) %collective-permute-start.6) | collective-permute-done | bytes 524320 | tf_op jit(solution)/shard_map/ppermute | solution.py:23
  115.6 6.7 %all-to-all-done.3 = bf16[4,2,128,512]{3,2,1,0:T(8,128)(2,1)S(1)} async-done(((bf16[4,2,128,512]{3,2,1,0:T(8,128)(2,1)}), bf16[4,2,128,512]{3,2,1,0:T(8,128)(2,1)S(1)}, u32[]{:S(2)}, u32[]{:S(2)}) %all-to-all-start.3) | async-done | bytes 1048608 | tf_op jit(solution)/shard_map/all_to_all | solution.py:75
  133.9 8.0 %convolution_convert_fusion.5 = bf16[1024,1024]{1,0:T(8,128)(2,1)S(1)} fusion(bf16[1024,2048]{1,0:T(8,128)(2,1)} %all-gather.7.cloned.1.call-done, bf16[1024,2048]{1,0:T(8,128)(2,1)} %constant_dynamic-update-slice_fusion.1), kind=kOutput, calls=%fused_computation.56 | convolution fusion | flops 4296015872 | bytes 10485760 | tf_op jit(solution)/shard_map/dot_general | solution.py:19
  147.5 51.4 %all-gather.5.cloned.1.call-done = bf16[1024,2048]{1,0:T(8,128)(2,1)} async-done(((bf16[256,2048]{1,0:T(8,128)(2,1)}), bf16[1024,2048]{1,0:T(8,128)(2,1)}) %all-gather.5.cloned.1.call-update) | async-done | bytes 4194320 | tf_op jit(solution)/shard_map/all_gather | solution.py:159
  218.6 18.3 %collective-permute-done.25 = bf16[128,2048]{1,0:T(8,128)(2,1)} collective-permute-done((bf16[128,2048]{1,0:T(8,128)(2,1)S(1)}, bf16[128,2048]{1,0:T(8,128)(2,1)}, u32[]{:S(2)}, u32[]{:S(2)}) %collective-permute-start.25) | collective-permute-done | bytes 524320 | tf_op jit(solution)/shard_map/ppermute | solution.py:23
  244.7 5.4 collective-permute-done.16
  255.1 9.6 %collective-permute-done.17 = bf16[128,2048]{1,0:T(8,128)(2,1)S(1)} collective-permute-done((bf16[128,2048]{1,0:T(8,128)(2,1)S(1)}, bf16[128,2048]{1,0:T(8,128)(2,1)S(1)}, u32[]{:S(2)}, u32[]{:S(2)}) %collective-permute-start.17) | collective-permute-done | bytes 524320 | tf_op jit(solution)/shard_map/ppermute | solution.py:23
  272.7 20.8 %collective-permute-done.18 = bf16[128,2048]{1,0:T(8,128)(2,1)S(1)} collective-permute-done((bf16[128,2048]{1,0:T(8,128)(2,1)S(1)}, bf16[128,2048]{1,0:T(8,128)(2,1)S(1)}, u32[]{:S(2)}, u32[]{:S(2)}) %collective-permute-start.18) | collective-permute-done | bytes 524320 | tf_op jit(solution)/shard_map/ppermute | solution.py:23
  300.8 6.5 %fusion.133 = f32[512,1024]{1,0:T(8,128)} fusion(bf16[512,2048]{0,1:T(8,128)(2,1)} %all-gather.9.cloned.1.call-done, bf16[1024,2048]{1,0:T(8,128)(2,1)} %constant_dynamic-update-slice_fusion.9), kind=kOutput, calls=%fused_computation.309 | convolution fusion | flops 2147483648 | bytes 8388608 | tf_op jit(solution)/shard_map/dot_general | solution.py:19
  307.3 9.7 %add_convert_fusion = (bf16[512,1024]{1,0:T(8,128)(2,1)S(1)}, f32[512,1024]{1,0:T(8,128)S(1)}) fusion(f32[512,1024]{1,0:T(8,128)} %fusion.133, bf16[512,2048]{0,1:T(8,128)(2,1)} %all-gather.11.cloned.1.call-done, bf16[1024,2048]{1,0:T(8,128)(2,1)} %copy-done.32), kind=kOutput, calls=%fused_computation.37 | convolution fusion | flops 2185232384 | bytes 11534336 | tf_op jit(solution)/shard_map/dot_general | solution.py:19
  323.4 5.8 fusion.130
  337.1 6.4 %copy.106 = bf16[1024,2048]{0,1:T(8,128)(2,1)} copy(bf16[1024,2048]{1,0:T(8,128)(2,1)} %bitcast.166) | data formatting | bytes 8388608 | tf_op jit(solution)/shard_map/reshape | solution.py:258
  349.2 6.3 %collective-permute-done.38 = bf16[64,2048]{1,0:T(8,128)(2,1)S(1)} collective-permute-done((bf16[64,2048]{1,0:T(8,128)(2,1)S(1)}, bf16[64,2048]{1,0:T(8,128)(2,1)S(1)}, u32[]{:S(2)}, u32[]{:S(2)}) %collective-permute-start.38) | collective-permute-done | bytes 262176 | tf_op jit(solution)/shard_map/ppermute | solution.py:23
  357.9 11.4 %collective-permute-done.39 = bf16[128,2048]{1,0:T(8,128)(2,1)S(1)} collective-permute-done((bf16[128,2048]{1,0:T(8,128)(2,1)S(1)}, bf16[128,2048]{1,0:T(8,128)(2,1)S(1)}, u32[]{:S(2)}, u32[]{:S(2)}) %collective-permute-start.39) | collective-permute-done | bytes 524320 | tf_op jit(solution)/shard_map/ppermute | solution.py:23
  377.6 20.3 %collective-permute-done.40 = bf16[128,2048]{1,0:T(8,128)(2,1)S(1)} collective-permute-done((bf16[128,2048]{1,0:T(8,128)(2,1)S(1)}, bf16[128,2048]{1,0:T(8,128)(2,1)S(1)}, u32[]{:S(2)}, u32[]{:S(2)}) %collective-permute-start.40) | collective-permute-done | bytes 524320 | tf_op jit(solution)/shard_map/ppermute | solution.py:23
  427.3 6.1 convolution_convert_fusion
  433.4 7.4 %fusion.134 = f32[1024,2048]{1,0:T(8,128)S(1)} fusion(bf16[1024,1024]{1,0:T(8,128)(2,1)} %bitcast.198, bf16[1024,2048]{1,0:T(8,128)(2,1)} %all-gather.7.cloned.1.call-done), kind=kOutput, calls=%fused_computation.310 | convolution fusion | flops 4294967296 | bytes 14680064 | tf_op jit(solution)/shard_map/dot_general | solution.py:19
  454.4 5.7 collective-permute-done.61
  462.5 5.3 collective-permute-done.53
  471.6 5.5 collective-permute-done.62
  477.1 5.6 collective-permute-done.59
  490.3 6.8 %all-to-all-done.5 = bf16[4,128,512]{2,1,0:T(8,128)(2,1)S(1)} async-done(((bf16[4,128,512]{2,1,0:T(8,128)(2,1)}), bf16[4,128,512]{2,1,0:T(8,128)(2,1)S(1)}, u32[]{:S(2)}, u32[]{:S(2)}) %all-to-all-start.5) | async-done | bytes 524320 | tf_op jit(solution)/shard_map/all_to_all | solution.py:75
  497.1 11.2 %all_to_all.52 = bf16[4,128,512]{1,2,0:T(8,128)(2,1)S(1)} all-to-all(bf16[4,128,512]{1,2,0:T(8,128)(2,1)S(1)} %bitcast.209), channel_id=1, replica_groups=mesh['x'=2,'k'=2,'z'=4,'y'=2] {'x','k'}, dimensions={0} | all-to-all | bytes 1048576 | tf_op jit(solution)/shard_map/all_to_all | solution.py:75
  514.7 5.9 all-to-all-done.7
  527.4 5.7 all-to-all-done.4
  542.6 13.0 %collective-permute-done.64 = f32[4,2048]{1,0:T(4,128)S(1)} collective-permute-done((f32[4,2048]{1,0:T(4,128)S(1)}, f32[4,2048]{1,0:T(4,128)S(1)}, u32[]{:S(2)}, u32[]{:S(2)}) %collective-permute-start.64) | collective-permute-done | bytes 32800 | tf_op jit(solution)/shard_map/ppermute | solution.py:23
  568.3 11.2 %reduce-scatter.4.cloned.1.call-done = bf16[256,2048]{1,0:T(8,128)(2,1)} async-done(((bf16[1024,2048]{1,0:T(8,128)(2,1)}), bf16[256,2048]{1,0:T(8,128)(2,1)}) %reduce-scatter.4.cloned.1.call-update) | async-done | bytes 1048592 | tf_op jit(solution)/shard_map/reduce_scatter | solution.py:259
  598.1 9.5 %all-to-all-done.9 = bf16[8,128,512]{2,1,0:T(8,128)(2,1)} async-done(((bf16[8,128,512]{2,1,0:T(8,128)(2,1)}), bf16[8,128,512]{2,1,0:T(8,128)(2,1)}, u32[]{:S(2)}, u32[]{:S(2)}) %all-to-all-start.9) | async-done | bytes 1048608 | tf_op jit(solution)/shard_map/all_to_all | solution.py:306
  (461 shorter events, 252.8 us)
Async XLA Ops:
  7.2 126.7 %all-gather.7.cloned.1.call-start = ((), (), s32[]{:S(2)}) async-start(), calls=%async_computation.14 | async-start | bytes 5242880 | tf_op jit(solution)/shard_map/all_gather | solution.py:159
  36.2 162.7 %all-gather.5.cloned.1.call-start = ((), (), s32[]{:S(2)}) async-start(), calls=%async_computation.13 | async-start | bytes 5242880 | tf_op jit(solution)/shard_map/all_gather | solution.py:159
  86.3 26.1 %collective-permute-start.6 = (bf16[128,2048]{1,0:T(8,128)(2,1)}, bf16[128,2048]{1,0:T(8,128)(2,1)}, u32[]{:S(2)}, u32[]{:S(2)}) collective-permute-start(bf16[128,2048]{1,0:T(8,128)(2,1)} %get-tuple-element.109), channel_id=1, source_target_pairs={{0,16},{1,17},{8,24},{9,25},{16,0},{17,1},{24,8},{25,9},{2,18},{3,... | collective-permute-start | bytes 1572872 | tf_op jit(solution)/shard_map/ppermute | solution.py:23
  88.0 24.4 %collective-permute-start.3 = (bf16[128,2048]{1,0:T(8,128)(2,1)}, bf16[128,2048]{1,0:T(8,128)(2,1)}, u32[]{:S(2)}, u32[]{:S(2)}) collective-permute-start(bf16[128,2048]{1,0:T(8,128)(2,1)} %get-tuple-element.109), channel_id=1, source_target_pairs={{0,1},{1,0},{8,9},{9,8},{16,17},{17,16},{24,25},{25,24},{2,3},{3,2... | collective-permute-start | bytes 1572872 | tf_op jit(solution)/shard_map/ppermute | solution.py:23
  90.0 24.8 %collective-permute-start.4 = (bf16[128,2048]{1,0:T(8,128)(2,1)}, bf16[128,2048]{1,0:T(8,128)(2,1)S(1)}, u32[]{:S(2)}, u32[]{:S(2)}) collective-permute-start(bf16[128,2048]{1,0:T(8,128)(2,1)} %get-tuple-element.109), channel_id=1, source_target_pairs={{0,8},{1,9},{8,0},{9,1},{16,24},{17,25},{24,16},{25,17},{2,10},{3,... | collective-permute-start | bytes 1572872 | tf_op jit(solution)/shard_map/ppermute | solution.py:23
  92.5 29.8 %all-to-all-start.3 = ((bf16[4,2,128,512]{3,2,1,0:T(8,128)(2,1)}), bf16[4,2,128,512]{3,2,1,0:T(8,128)(2,1)S(1)}, u32[]{:S(2)}, u32[]{:S(2)}) async-start(bf16[4,2,128,512]{3,2,1,0:T(8,128)(2,1)} %copy.93), calls=%async_computation.3 | async-start | bytes 2097152 | tf_op jit(solution)/shard_map/all_to_all | solution.py:75
  96.0 204.8 %all-gather.9.cloned.1.call-start = ((), (), s32[]{:S(2)}) async-start(), calls=%async_computation.15 | async-start | bytes 2621440 | tf_op jit(solution)/shard_map/all_gather | solution.py:159
  102.4 29.6 %collective-permute-start.9 = (bf16[128,2048]{1,0:T(8,128)(2,1)}, bf16[128,2048]{1,0:T(8,128)(2,1)}, u32[]{:S(2)}, u32[]{:S(2)}) collective-permute-start(bf16[128,2048]{1,0:T(8,128)(2,1)} %collective-permute-done.7), channel_id=1, source_target_pairs={{0,8},{1,9},{8,0},{9,1},{16,24},{17,25},{24,16},{25,17},{2,10},{3,... | collective-permute-start | bytes 1572872 | tf_op jit(solution)/shard_map/ppermute | solution.py:23
  124.0 183.3 %all-gather.11.cloned.1.call-start = ((), (), s32[]{:S(2)}) async-start(), calls=%async_computation.16 | async-start | bytes 2621440 | tf_op jit(solution)/shard_map/all_gather | solution.py:159
  210.8 26.1 %collective-permute-start.25 = (bf16[128,2048]{1,0:T(8,128)(2,1)S(1)}, bf16[128,2048]{1,0:T(8,128)(2,1)}, u32[]{:S(2)}, u32[]{:S(2)}) collective-permute-start(bf16[128,2048]{1,0:T(8,128)(2,1)S(1)} %bitcast.181), channel_id=1, source_target_pairs={{0,1},{1,0},{8,9},{9,8},{16,17},{17,16},{24,25},{25,24},{2,3},{3,2... | collective-permute-start | bytes 1572872 | tf_op jit(solution)/shard_map/ppermute | solution.py:23
  214.5 27.6 %collective-permute-start.13 = (bf16[64,2048]{1,0:T(8,128)(2,1)}, bf16[64,2048]{1,0:T(8,128)(2,1)}, u32[]{:S(2)}, u32[]{:S(2)}) collective-permute-start(bf16[64,2048]{1,0:T(8,128)(2,1)} %get-tuple-element.167), channel_id=1, source_target_pairs={{0,1},{1,0},{8,9},{9,8},{16,17},{17,16},{24,25},{25,24},{2,3},{3,2... | collective-permute-start | bytes 786440 | tf_op jit(solution)/shard_map/ppermute | solution.py:23
  216.0 272.2 %reduce-scatter.8.cloned.1.call-start = ((), (), s32[]{:S(2)}) async-start(), calls=%async_computation.19 | async-start | bytes 5242880 | tf_op jit(solution)/shard_map/reduce_scatter | solution.py:259
  216.5 33.7 %collective-permute-start.29 = (bf16[128,2048]{1,0:T(8,128)(2,1)S(1)}, bf16[128,2048]{1,0:T(8,128)(2,1)S(1)}, u32[]{:S(2)}, u32[]{:S(2)}) collective-permute-start(bf16[128,2048]{1,0:T(8,128)(2,1)S(1)} %bitcast.182), channel_id=1, source_target_pairs={{0,17},{1,16},{8,25},{9,24},{16,1},{17,0},{24,9},{25,8},{2,19},{3,... | collective-permute-start | bytes 1572872 | tf_op jit(solution)/shard_map/ppermute | solution.py:23
  218.0 36.4 %collective-permute-start.28 = (bf16[128,2048]{1,0:T(8,128)(2,1)S(1)}, bf16[128,2048]{1,0:T(8,128)(2,1)S(1)}, u32[]{:S(2)}, u32[]{:S(2)}) collective-permute-start(bf16[128,2048]{1,0:T(8,128)(2,1)S(1)} %bitcast.183), channel_id=1, source_target_pairs={{0,16},{1,17},{8,24},{9,25},{16,0},{17,1},{24,8},{25,9},{2,18},{3,... | collective-permute-start | bytes 1572872 | tf_op jit(solution)/shard_map/ppermute | solution.py:23
  218.5 33.3 %collective-permute-start.26 = (bf16[128,2048]{1,0:T(8,128)(2,1)S(1)}, bf16[128,2048]{1,0:T(8,128)(2,1)S(1)}, u32[]{:S(2)}, u32[]{:S(2)}) collective-permute-start(bf16[128,2048]{1,0:T(8,128)(2,1)S(1)} %bitcast.184), channel_id=1, source_target_pairs={{0,8},{1,9},{8,0},{9,1},{16,24},{17,25},{24,16},{25,17},{2,10},{3,... | collective-permute-start | bytes 1572872 | tf_op jit(solution)/shard_map/ppermute | solution.py:23
  254.5 39.1 %collective-permute-start.31 = (bf16[128,2048]{1,0:T(8,128)(2,1)S(1)}, bf16[128,2048]{1,0:T(8,128)(2,1)S(1)}, u32[]{:S(2)}, u32[]{:S(2)}) collective-permute-start(bf16[128,2048]{1,0:T(8,128)(2,1)S(1)} %collective-permute-done.29), channel_id=1, source_target_pairs={{0,8},{1,9},{8,0},{9,1},{16,24},{17,25},{24,16},{25,17},{2,10},{3,... | collective-permute-start | bytes 1572872 | tf_op jit(solution)/shard_map/ppermute | solution.py:23
  268.9 24.6 %collective-permute-start.18 = (bf16[128,2048]{1,0:T(8,128)(2,1)S(1)}, bf16[128,2048]{1,0:T(8,128)(2,1)S(1)}, u32[]{:S(2)}, u32[]{:S(2)}) collective-permute-start(bf16[128,2048]{1,0:T(8,128)(2,1)S(1)} %get-tuple-element.105), channel_id=1, source_target_pairs={{0,1},{1,0},{8,9},{9,8},{16,17},{17,16},{24,25},{25,24},{2,3},{3,2... | collective-permute-start | bytes 1572872 | tf_op jit(solution)/shard_map/ppermute | solution.py:23
  269.5 24.1 %collective-permute-start.22 = (bf16[128,2048]{1,0:T(8,128)(2,1)S(1)}, bf16[128,2048]{1,0:T(8,128)(2,1)S(1)}, u32[]{:S(2)}, u32[]{:S(2)}) collective-permute-start(bf16[128,2048]{1,0:T(8,128)(2,1)S(1)} %get-tuple-element.105), channel_id=1, source_target_pairs={{0,17},{1,16},{8,25},{9,24},{16,1},{17,0},{24,9},{25,8},{2,19},{3,... | collective-permute-start | bytes 1572872 | tf_op jit(solution)/shard_map/ppermute | solution.py:23
  272.0 22.9 %collective-permute-start.21 = (bf16[128,2048]{1,0:T(8,128)(2,1)S(1)}, bf16[128,2048]{1,0:T(8,128)(2,1)S(1)}, u32[]{:S(2)}, u32[]{:S(2)}) collective-permute-start(bf16[128,2048]{1,0:T(8,128)(2,1)S(1)} %get-tuple-element.105), channel_id=1, source_target_pairs={{0,16},{1,17},{8,24},{9,25},{16,0},{17,1},{24,8},{25,9},{2,18},{3,... | collective-permute-start | bytes 1572872 | tf_op jit(solution)/shard_map/ppermute | solution.py:23
  272.6 23.1 %collective-permute-start.19 = (bf16[128,2048]{1,0:T(8,128)(2,1)S(1)}, bf16[128,2048]{1,0:T(8,128)(2,1)S(1)}, u32[]{:S(2)}, u32[]{:S(2)}) collective-permute-start(bf16[128,2048]{1,0:T(8,128)(2,1)S(1)} %get-tuple-element.105), channel_id=1, source_target_pairs={{0,8},{1,9},{8,0},{9,1},{16,24},{17,25},{24,16},{25,17},{2,10},{3,... | collective-permute-start | bytes 1572872 | tf_op jit(solution)/shard_map/ppermute | solution.py:23
  343.5 189.6 %reduce-scatter.6.cloned.1.call-start = ((), (), s32[]{:S(2)}) async-start(), calls=%async_computation.18 | async-start | bytes 5242880 | tf_op jit(solution)/shard_map/reduce_scatter | solution.py:259
  374.1 23.8 %collective-permute-start.40 = (bf16[128,2048]{1,0:T(8,128)(2,1)S(1)}, bf16[128,2048]{1,0:T(8,128)(2,1)S(1)}, u32[]{:S(2)}, u32[]{:S(2)}) collective-permute-start(bf16[128,2048]{1,0:T(8,128)(2,1)S(1)} %get-tuple-element.99), channel_id=1, source_target_pairs={{0,1},{1,0},{8,9},{9,8},{16,17},{17,16},{24,25},{25,24},{2,3},{3,2... | collective-permute-start | bytes 1572872 | tf_op jit(solution)/shard_map/ppermute | solution.py:23
  374.7 23.2 %collective-permute-start.44 = (bf16[128,2048]{1,0:T(8,128)(2,1)S(1)}, bf16[128,2048]{1,0:T(8,128)(2,1)S(1)}, u32[]{:S(2)}, u32[]{:S(2)}) collective-permute-start(bf16[128,2048]{1,0:T(8,128)(2,1)S(1)} %get-tuple-element.99), channel_id=1, source_target_pairs={{0,17},{1,16},{8,25},{9,24},{16,1},{17,0},{24,9},{25,8},{2,19},{3,... | collective-permute-start | bytes 1572872 | tf_op jit(solution)/shard_map/ppermute | solution.py:23
  376.1 23.0 %collective-permute-start.43 = (bf16[128,2048]{1,0:T(8,128)(2,1)S(1)}, bf16[128,2048]{1,0:T(8,128)(2,1)S(1)}, u32[]{:S(2)}, u32[]{:S(2)}) collective-permute-start(bf16[128,2048]{1,0:T(8,128)(2,1)S(1)} %get-tuple-element.99), channel_id=1, source_target_pairs={{0,16},{1,17},{8,24},{9,25},{16,0},{17,1},{24,8},{25,9},{2,18},{3,... | collective-permute-start | bytes 1572872 | tf_op jit(solution)/shard_map/ppermute | solution.py:23
  377.6 21.6 %collective-permute-start.41 = (bf16[128,2048]{1,0:T(8,128)(2,1)S(1)}, bf16[128,2048]{1,0:T(8,128)(2,1)S(1)}, u32[]{:S(2)}, u32[]{:S(2)}) collective-permute-start(bf16[128,2048]{1,0:T(8,128)(2,1)S(1)} %get-tuple-element.99), channel_id=1, source_target_pairs={{0,8},{1,9},{8,0},{9,1},{16,24},{17,25},{24,16},{25,17},{2,10},{3,... | collective-permute-start | bytes 1572872 | tf_op jit(solution)/shard_map/ppermute | solution.py:23
  413.5 166.0 %reduce-scatter.4.cloned.1.call-start = ((), (), s32[]{:S(2)}) async-start(), calls=%async_computation.17 | async-start | bytes 5242880 | tf_op jit(solution)/shard_map/reduce_scatter | solution.py:259
  443.6 27.2 %collective-permute-start.55 = (bf16[128,2048]{1,0:T(8,128)(2,1)S(1)}, bf16[128,2048]{1,0:T(8,128)(2,1)S(1)}, u32[]{:S(2)}, u32[]{:S(2)}) collective-permute-start(bf16[128,2048]{1,0:T(8,128)(2,1)S(1)} %get-tuple-element.123), channel_id=1, source_target_pairs={{0,8},{1,9},{8,0},{9,1},{16,24},{17,25},{24,16},{25,17},{2,10},{3,... | collective-permute-start | bytes 1572872 | tf_op jit(solution)/shard_map/ppermute | solution.py:23
  448.4 63.4 %collective-permute-start.47 = (bf16[128,2048]{1,0:T(8,128)(2,1)}, bf16[128,2048]{1,0:T(8,128)(2,1)}, u32[]{:S(2)}, u32[]{:S(2)}) collective-permute-start(bf16[128,2048]{1,0:T(8,128)(2,1)} %get-tuple-element.127), channel_id=1, source_target_pairs={{0,8},{1,9},{8,0},{9,1},{16,24},{17,25},{24,16},{25,17},{2,10},{3,... | collective-permute-start | bytes 1572872 | tf_op jit(solution)/shard_map/ppermute | solution.py:23
  468.5 43.3 %collective-permute-start.54 = (bf16[128,2048]{1,0:T(8,128)(2,1)S(1)}, bf16[128,2048]{1,0:T(8,128)(2,1)}, u32[]{:S(2)}, u32[]{:S(2)}) collective-permute-start(bf16[128,2048]{1,0:T(8,128)(2,1)S(1)} %pad_maximum_fusion.15), channel_id=1, source_target_pairs={{0,1},{1,0},{8,9},{9,8},{16,17},{17,16},{24,25},{25,24},{2,3},{3,2... | collective-permute-start | bytes 1572872 | tf_op jit(solution)/shard_map/ppermute | solution.py:23
  470.9 41.0 %collective-permute-start.51 = (bf16[128,2048]{1,0:T(8,128)(2,1)}, bf16[128,2048]{1,0:T(8,128)(2,1)}, u32[]{:S(2)}, u32[]{:S(2)}) collective-permute-start(bf16[128,2048]{1,0:T(8,128)(2,1)} %pad_maximum_fusion.14), channel_id=1, source_target_pairs={{0,16},{1,17},{8,24},{9,25},{16,0},{17,1},{24,8},{25,9},{2,18},{3,... | collective-permute-start | bytes 1572872 | tf_op jit(solution)/shard_map/ppermute | solution.py:23
  537.0 42.5 %all-to-all-start.8 = ((bf16[8,128,512]{2,1,0:T(8,128)(2,1)}), bf16[8,128,512]{2,1,0:T(8,128)(2,1)S(1)}, u32[]{:S(2)}, u32[]{:S(2)}) async-start(bf16[8,128,512]{2,1,0:T(8,128)(2,1)} %bitcast.189), calls=%async_computation.11 | async-start | bytes 2097152 | tf_op jit(solution)/shard_map/all_to_all | solution.py:306
  588.8 18.8 %all-to-all-start.9 = ((bf16[8,128,512]{2,1,0:T(8,128)(2,1)}), bf16[8,128,512]{2,1,0:T(8,128)(2,1)}, u32[]{:S(2)}, u32[]{:S(2)}) async-start(bf16[8,128,512]{2,1,0:T(8,128)(2,1)} %bitcast.190), calls=%async_computation.12 | async-start | bytes 2097152 | tf_op jit(solution)/shard_map/all_to_all | solution.py:306
  (107 other events, 835.2 us)
Sparse Core Ops, SparseCore 0:
  36.3 81.0 all-gather.6
  119.5 79.2 all-gather.4
  201.0 44.7 all-gather.8
  247.7 44.4 all-gather.10
  343.6 74.5 reduce-scatter.7
  420.5 77.2 reduce-scatter.5
  500.1 79.3 reduce-scatter.3

commit v3 on v2

v3 whole, which is shorter than its diff:
```python
import functools
import math

import jax
import jax.numpy as jnp
import numpy as np
from jax import lax
from jax.experimental import pallas as pl
from jax.experimental.pallas import tpu as pltpu
from jax.sharding import Mesh
from jax.sharding import PartitionSpec as P

HEADS = 8
EPS_NORM = 1e-05
EPS_GROUP = 0.25

ROW = ("x", "k")
GROUP = ("x", "k", "y")
EVERY = ("x", "k", "z", "y")
F32 = jnp.float32
BF16 = jnp.bfloat16


def dot(left, right, over):
    return lax.dot_general(left, right, (over, ((), ())), preferred_element_type=F32)


def swap(value, mask):
    return lax.ppermute(value, GROUP, [(i, i ^ mask) for i in range(8)])


def group_gather(part, *others):
    near = [part, swap(part, 1), swap(part, 4), swap(part, 5)]
    far = [swap(after(block, *others), 2) for block in near]
    return near[:2] + far[:2] + near[2:] + far[2:]


def reduce_pairs(total):
    height = total.shape[0] // 8

    def pair(j):
        kept = total[j * height : (j + 1) * height]
        return kept.astype(F32) + swap(total[(j + 2) * height : (j + 3) * height], 2).astype(F32)

    return pair(5).astype(BF16), pair(4), pair(1), pair(0)


def reduce_relay(state):
    across, over_x, over_y, own = state
    half = across.shape[0] // 2
    top, low = swap(across[:half], 1).astype(F32), swap(across[half:], 4).astype(F32)
    over_x = jnp.concatenate([over_x[:half] + top, over_x[half:]], axis=0).astype(BF16)
    over_y = jnp.concatenate([over_y[:half], over_y[half:] + low], axis=0).astype(BF16)
    return over_x, over_y, own


def reduce_last(state):
    over_x, over_y, own = state
    return own + swap(over_x, 4).astype(F32) + swap(over_y, 1).astype(F32)


def group_reduce(total):
    return reduce_last(reduce_relay(reduce_pairs(total)))


def after(value, *others):
    return lax.optimization_barrier((value,) + others)[0]


def total_over_all(value):
    value = value + swap(value, 2)
    value = value + swap(value, 1) + swap(value, 4) + swap(value, 5)
    depth = lax.axis_size("z")
    if depth > 4:
        return lax.psum(value, "z")
    own = value
    for step in range(1, depth):
        value = value + lax.ppermute(own, "z", [(i, (i + step) % depth) for i in range(depth)])
    return value


def row_gather(value):
    got = [value, swap(value, 2), swap(value, 4), swap(value, 6)]
    own = lax.axis_index(ROW)
    rows = []
    for i in range(4):
        picks = [jnp.where((own ^ j) == i, got[j], 0.0) for j in range(4)]
        rows.append(picks[0] + picks[1] + picks[2] + picks[3])
    return jnp.stack(rows)


def row_exchange(parts):
    return lax.all_to_all(parts, ROW, split_axis=0, concat_axis=0, tiled=True)


def to_wide(*parts):
    height, width = parts[0].shape
    moved = row_exchange(jnp.stack([p.reshape(4, -1, width) for p in parts], axis=1))
    moved = moved.transpose(1, 2, 0, 3).reshape(len(parts), height // 4, 4 * width)
    return [moved[i] for i in range(len(parts))]


def from_wide(*parts):
    height, width = parts[0].shape
    moved = row_exchange(
        jnp.stack(parts).reshape(len(parts), height, 4, width // 4).transpose(2, 0, 1, 3)
    )
    moved = moved.transpose(1, 0, 2, 3).reshape(len(parts), 4 * height, width // 4)
    return [moved[i] for i in range(len(parts))]


def head_order(count):
    units = count // HEADS
    j = lax.iota(jnp.int32, count)
    target = (j % HEADS) * units + j // HEADS
    return (target[:, None] == lax.iota(jnp.int32, count)[None, :]).astype(BF16)


def layernorm(value, gain, bias):
    mean = jnp.mean(value, axis=1, keepdims=True)
    centered = value - mean
    inverse = lax.rsqrt(jnp.mean(centered * centered, axis=1, keepdims=True) + EPS_NORM)
    hat = centered * inverse
    return hat, inverse, (hat * gain + bias).astype(BF16)


def layernorm_back(grad, hat, inverse, gain):
    scaled = grad * gain
    first = jnp.mean(scaled, axis=1, keepdims=True)
    second = jnp.mean(scaled * hat, axis=1, keepdims=True)
    return (
        inverse * (scaled - first - hat * second),
        jnp.sum(grad * hat, axis=0),
        jnp.sum(grad, axis=0),
    )


TILE = 256
WIDE = 512
LIMIT = 58 * 1024 * 1024


def spans(total, tile, step):
    def once(i, carry):
        step(pl.ds(pl.multiple_of(i * tile, tile), tile))
        return carry

    lax.fori_loop(0, total // tile, once, 0)


def kernel_call(body, outs, scratch, flops, *args, copies=0):
    moved = sum(a.size * a.dtype.itemsize for a in args)
    moved += sum(math.prod(shape) * jnp.dtype(kind).itemsize for shape, kind in outs)
    whole = pl.BlockSpec(memory_space=pl.ANY if copies else pltpu.VMEM)
    return pl.pallas_call(
        body,
        out_shape=[jax.ShapeDtypeStruct(shape, kind) for shape, kind in outs],
        in_specs=[whole] * len(args),
        out_specs=[whole] * len(outs),
        scratch_shapes=[pltpu.VMEM(shape, kind) for shape, kind in scratch]
        + [pltpu.SemaphoreType.DMA((copies,))] * bool(copies),
        compiler_params=pltpu.CompilerParams(vmem_limit_bytes=LIMIT),
        cost_estimate=pl.CostEstimate(flops=flops, bytes_accessed=moved, transcendentals=0),
    )(*args)


def unpack(source, first, second, depth):
    half = source.shape[0] // (2 * depth)
    for i in range(depth):
        at = 2 * i * half
        if first is not None:
            first[i * half : (i + 1) * half, :] = source[at : at + half, :]
        if second is not None:
            second[i * half : (i + 1) * half, :] = source[at + half : at + 2 * half, :]


def pack(target, columns, first, second, depth):
    half = first.shape[0] // depth
    for i in range(depth):
        at = 2 * i * half
        target[at : at + half, columns] = first[i * half : (i + 1) * half]
        target[at + half : at + 2 * half, columns] = second[i * half : (i + 1) * half]


def decayed(raw, spot, segs, grow, fall, rows):
    inside = (spot[0][rows, :] >= spot[1][...]) & (segs[0][rows, :] == segs[1][...])
    return jnp.where(inside, raw * (grow[rows, :] * fall[...]), 0.0).astype(BF16)


def retention_forward(depth, w, x, pc, pr, sc, sr, grow, fall, q, k, v, weights, normed, inv):
    seq = x.shape[0]
    part = q.shape[0] // depth
    width = v.shape[0] // depth
    group = 2 * part + width

    def project(at):
        out = dot(w[...], x[at, :], ((1,), (1,))).astype(BF16)
        for i in range(depth):
            z = i * group
            q[i * part : (i + 1) * part, at] = out[z : z + part]
            k[i * part : (i + 1) * part, at] = out[z + part : z + 2 * part]
            v[i * width : (i + 1) * width, at] = out[z + 2 * part : z + group]

    def attend(at):
        raw = dot(q[:, at], k[...], ((0,), (0,)))
        low = decayed(raw, (pc, pr), (sc, sr), grow, fall, at)
        weights[at, :] = low
        kept = dot(v[...], low, ((1,), (1,)))
        centered = kept - jnp.mean(kept, axis=0, keepdims=True)
        scale = lax.rsqrt(jnp.mean(centered * centered, axis=0, keepdims=True) + EPS_GROUP)
        normed[:, at] = centered * scale
        inv[:, at] = scale

    spans(seq, TILE, project)
    spans(seq, TILE, attend)


def gated_forward(depth, w, x, normed, gate, hidden, out, wg, wo):
    unpack(w, wg, wo, depth)

    def step(at):
        g = dot(wg[...], x[at, :], ((1,), (1,)))
        gate[:, at] = g
        low = normed[:, at].astype(BF16).astype(F32)
        h = (g * jax.nn.sigmoid(g) * low).astype(BF16)
        hidden[:, at] = h
        out[at, :] = dot(h, wo[...], ((0,), (0,))).astype(BF16)

    spans(x.shape[0], TILE, step)


class Mover:
    def __init__(self, semaphores):
        self.semaphores = semaphores
        self.count = 0

    def start(self, source, target):
        copy = pltpu.make_async_copy(source, target, self.semaphores.at[self.count])
        self.count += 1
        copy.start()
        return copy

    def rows(self, sources, target):
        height = sources[0].shape[0]
        return [
            self.start(source, target.at[pl.ds(i * height, height)])
            for i, source in enumerate(sources)
        ]

    def kind(self, source, target, which, depth):
        half = (source if which[0] == "from" else target).shape[0] // (2 * depth)
        moved = []
        for i in range(depth):
            mixed = pl.ds((2 * i + which[1]) * half, half)
            plain = pl.ds(i * half, half)
            if which[0] == "from":
                moved.append(self.start(source.at[mixed], target.at[plain]))
            else:
                moved.append(self.start(source.at[plain], target.at[mixed]))
        return moved


def wait(copies):
    for copy in copies:
        copy.wait()


def feedforward(depth, w, *refs):
    x_blocks, cot_blocks = refs[:8], refs[8:16]
    act_out, back_out, grads_out = refs[16:19]
    wu, wd, x, cot, act, gp, back, gu, gd, semaphores = refs[19:]
    move = Mover(semaphores)
    seq, rows = x.shape[0], x_blocks[0].shape[0]
    weights = move.kind(w, wu, ("from", 0), depth) + move.kind(w, wd, ("from", 1), depth)
    x_copies, cot_copies = move.rows(x_blocks, x), move.rows(cot_blocks, cot)
    wait(weights)
    for tile in range(seq // TILE):
        mine = slice(tile * TILE // rows, (tile + 1) * TILE // rows)
        wait(x_copies[mine] + cot_copies[mine])
        at = pl.ds(tile * TILE, TILE)
        pre = dot(wu[...], x[at, :], ((1,), (1,)))
        grad = dot(wd[...], cot[at, :], ((1,), (1,)))
        half = 0.5 * (1.0 + lax.erf(pre * np.float32(0.5**0.5)))
        act[:, at] = (pre * half).astype(BF16)
        bell = jnp.exp(-0.5 * pre * pre) * np.float32((2 * math.pi) ** -0.5)
        gp[:, at] = (grad * (half + pre * bell)).astype(BF16)
    sent = [move.start(act, act_out)]

    def up_step(at):
        gu[:, at] = dot(gp[...], x[:, at], ((1,), (0,))).astype(BF16)

    def down_step(at):
        gd[:, at] = dot(act[...], cot[:, at], ((1,), (0,))).astype(BF16)

    spans(x.shape[1], WIDE, up_step)
    sent += move.kind(gu, grads_out, ("to", 0), depth)
    spans(x.shape[1], WIDE, down_step)
    sent += move.kind(gd, grads_out, ("to", 1), depth)
    for tile in range(seq // TILE):
        at = pl.ds(tile * TILE, TILE)
        back[at, :] = dot(gp[:, at], wu[...], ((0,), (0,))).astype(BF16)
        sent.append(move.start(back.at[at], back_out.at[at]))
    wait(sent)


def down_forward(depth, w, act, out, wd):
    unpack(w, None, wd, depth)

    def step(at):
        out[at, :] = dot(act[:, at], wd[...], ((0,), (0,))).astype(BF16)

    spans(act.shape[1], TILE, step)


def gated_backward(depth, w, x_in, *refs):
    mid_blocks = refs[:8]
    gate_in, normed_in, inv_in, hidden_in, ggate_out, gret_out, grads_out = refs[8:15]
    wo, x, mid, gate, normed, inv, hidden, ggate, gret, gg, go, semaphores = refs[15:]
    move = Mover(semaphores)
    seq, rows = x.shape[0], mid_blocks[0].shape[0]
    first = move.kind(w, wo, ("from", 1), depth)
    mid_copies = move.rows(mid_blocks[:2], mid.at[pl.ds(0, 2 * rows)])
    first += [move.start(inv_in, inv), move.start(gate_in, gate), move.start(normed_in, normed)]
    mid_copies += move.rows(mid_blocks[2:], mid.at[pl.ds(2 * rows, seq - 2 * rows)])
    late = [move.start(x_in, x), move.start(hidden_in, hidden)]
    wait(first)
    for tile in range(seq // TILE):
        wait(mid_copies[tile * TILE // rows : (tile + 1) * TILE // rows])
        at = pl.ds(tile * TILE, TILE)
        up = dot(wo[...], mid[at, :], ((1,), (1,)))
        g = gate[:, at]
        s = jax.nn.sigmoid(g)
        full = normed[:, at]
        low = full.astype(BF16).astype(F32)
        ggate[:, at] = (up * low * (s * (1.0 + g * (1.0 - s)))).astype(BF16)
        gn = (up * (g * s)).astype(BF16).astype(F32)
        mean = jnp.mean(gn, axis=0, keepdims=True)
        slope = jnp.mean(gn * full, axis=0, keepdims=True)
        gret[:, at] = (inv[:, at] * (gn - mean - full * slope)).astype(BF16)
    sent = [move.start(ggate, ggate_out), move.start(gret, gret_out)]
    wait(late)

    def gate_step(at):
        gg[:, at] = dot(ggate[...], x[:, at], ((1,), (0,))).astype(BF16)

    def out_step(at):
        go[:, at] = dot(hidden[...], mid[:, at], ((1,), (0,))).astype(BF16)

    spans(x.shape[1], WIDE, gate_step)
    sent += move.kind(gg, grads_out, ("to", 0), depth)
    spans(x.shape[1], WIDE, out_step)
    sent += move.kind(go, grads_out, ("to", 1), depth)
    wait(sent)


def retention_backward(
    depth, q, k, v, weights, gret, x, pc, pr, sc, sr, grow, fall, packed, grads, scores
):
    seq = x.shape[0]
    part = q.shape[0] // depth
    width = v.shape[0] // depth
    group = 2 * part + width

    def place(value, at, offset, height):
        for i in range(depth):
            z = i * group + offset
            packed[z : z + height, at] = value[i * height : (i + 1) * height]

    def query_step(at):
        raw = dot(gret[:, at], v[...], ((0,), (0,)))
        low = decayed(raw, (pc, pr), (sc, sr), grow, fall, at)
        scores[at, :] = low
        place(dot(k[...], low, ((1,), (1,))).astype(BF16), at, 0, part)

    def key_step(at):
        place(dot(q[...], scores[:, at], ((1,), (0,))).astype(BF16), at, part, part)
        place(dot(gret[...], weights[:, at], ((1,), (0,))).astype(BF16), at, 2 * part, width)

    def grad_step(at):
        grads[:, at] = dot(packed[...], x[:, at], ((1,), (0,))).astype(BF16)

    spans(seq, TILE, query_step)
    spans(seq, TILE, key_step)
    spans(x.shape[1], WIDE, grad_step)


def input_backward(depth, packed, w, ggate, wgo, out, wg):
    unpack(wgo, wg, None, depth)

    def step(at):
        total = dot(packed[:, at], w[...], ((0,), (0,)))
        out[at, :] = (total + dot(ggate[:, at], wg[...], ((0,), (0,)))).astype(BF16)

    spans(packed.shape[1], TILE, step)


def body(
    block_in,
    cotangent,
    segments,
    w_query,
    w_key,
    w_value,
    w_gate,
    w_out,
    w_up,
    w_down,
    retention_norm_gain,
    retention_norm_bias,
    feedforward_norm_gain,
    feedforward_norm_bias,
):
    depth = lax.axis_size("z")
    part = block_in.shape[1]
    width = 4 * part
    own = lax.axis_index(GROUP)
    plane = lax.axis_index("z")
    tokens = block_in.shape[0] // 4
    seq = 8 * tokens

    kq = w_query.shape[1] // HEADS
    kv = w_value.shape[1] // HEADS
    order_q = head_order(w_query.shape[1])
    order_v = head_order(w_value.shape[1])

    def by_head(weight, order):
        return dot(order, weight, ((0,), (1,))).astype(BF16).reshape(HEADS, -1, part)

    def to_heads(send):
        got = lax.all_to_all(send, GROUP, split_axis=0, concat_axis=0, tiled=True)
        got = got.reshape(4, 2, send.shape[1], part).transpose(1, 2, 0, 3)
        return got.reshape(2, send.shape[1], width)

    split = 2 if kq % 16 == 0 else 1
    blocks = depth * split

    def regroup(rows, *counts):
        if split == 2:
            return rows.reshape(-1, width)
        cuts = np.cumsum((0,) + counts)
        return jnp.concatenate(
            [rows[:, cuts[i] : cuts[i + 1]].reshape(-1, width) for i in range(len(counts))]
        )

    def ungroup(rows, *counts):
        if split == 2:
            return rows.reshape(2, -1, width)
        cuts = 2 * np.cumsum((0,) + counts)
        return jnp.concatenate(
            [rows[cuts[i] : cuts[i + 1]].reshape(2, -1, width) for i in range(len(counts))], axis=1
        )

    def planes(mine):
        return lax.all_gather(mine, "z", axis=0, tiled=True)

    got_qkv = to_heads(
        jnp.concatenate(
            [by_head(w_query, order_q), by_head(w_key, order_q), by_head(w_value, order_v)], axis=1
        )
    )
    mine_qkv = regroup(got_qkv, kq, kq, kv)
    all_qkv = planes(mine_qkv)
    send_go = jnp.concatenate(
        [
            by_head(w_gate, order_v),
            dot(order_v, w_out, ((0,), (0,))).astype(BF16).reshape(HEADS, -1, part),
        ],
        axis=1,
    )
    got_go = to_heads(after(send_go, mine_qkv))
    mine_go = regroup(got_go, kv, kv)
    all_go = planes(mine_go)

    small = jnp.concatenate(
        [
            retention_norm_gain,
            retention_norm_bias,
            feedforward_norm_gain,
            feedforward_norm_bias,
            segments.astype(F32),
        ]
    )
    small = row_gather(after(small, mine_qkv))
    params = small[:, : 4 * part].reshape(4, 4, part).transpose(1, 0, 2).reshape(4, width)
    segs = small[:, 4 * part :].astype(jnp.int32).reshape(depth, 8, tokens)
    block_in, cotangent = after(block_in, got_go), after(cotangent, got_go)
    stream_low, cot_own = to_wide(block_in, cotangent)
    mine_up, mine_down = to_wide(after(w_up, stream_low).T, after(w_down, stream_low))
    all_ud = planes(after(jnp.concatenate([mine_up, mine_down], axis=0), mine_go))
    stream = stream_low.astype(F32)
    hat_one, inv_one, norm_one = layernorm(stream, params[0], params[1])
    x_one = jnp.concatenate(group_gather(norm_one), axis=0)

    ids = lax.iota(jnp.int32, 8) ^ own
    ids = (ids % 2) * 4 + ids // 2
    picked = (ids[:, None] == lax.iota(jnp.int32, 8)[None, :])[:, :, None]
    here = (lax.iota(jnp.int32, depth) == plane)[:, None, None]
    seg_plane = jnp.sum(jnp.where(here, segs, 0), axis=0)
    seg = jnp.sum(jnp.where(picked, seg_plane[None], 0), axis=1).reshape(seq)
    pos = (ids[:, None] * tokens + lax.iota(jnp.int32, tokens)[None, :]).reshape(seq)

    loggam = jnp.log1p(-jnp.exp2(-5.0 - own.astype(F32)))
    lag = (pos - seq // 2).astype(F32) * loggam
    grow = jnp.exp(lag) * np.float32((kq * 2 * depth) ** (-0.5))
    where = (pos[:, None], pos[None, :], seg[:, None], seg[None, :])
    where = where + (grow[:, None], jnp.exp(-lag)[None, :])

    x_one = after(x_one, mine_up, mine_down)
    keys_all, values_all = kq * 2 * depth, kv * 2 * depth
    square = 2 * seq * seq
    query, keys, values, weights, normed, inv_group = kernel_call(
        functools.partial(retention_forward, blocks),
        [
            ((keys_all, seq), BF16),
            ((keys_all, seq), BF16),
            ((values_all, seq), BF16),
            ((seq, seq), BF16),
            ((values_all, seq), F32),
            ((1, seq), F32),
        ],
        [],
        2 * seq * width * all_qkv.shape[0] + square * (keys_all + values_all),
        all_qkv,
        x_one,
        *where,
    )
    cot = group_gather(after(cot_own, x_one))
    wide = 2 * seq * width * values_all
    gate, hidden, attn = kernel_call(
        functools.partial(gated_forward, blocks),
        [((values_all, seq), F32), ((values_all, seq), BF16), ((seq, width), BF16)],
        [((values_all, width), BF16), ((values_all, width), BF16)],
        2 * wide,
        all_go,
        x_one,
        after(normed, cot),
    )
    middle = stream + group_reduce(attn)

    hat_two, inv_two, norm_two = layernorm(middle, params[2], params[3])
    x_two = group_gather(norm_two, all_ud)
    hidden_all = all_ud.shape[0] // 2
    wide_ff = 2 * seq * width * hidden_all
    narrow, broad = ((hidden_all, seq), BF16), ((hidden_all, width), BF16)
    tall = ((seq, width), BF16)
    act, two_part, full_ud = kernel_call(
        functools.partial(feedforward, depth),
        [narrow, tall, (all_ud.shape, BF16)],
        [broad, broad, tall, tall, narrow, narrow, tall, broad, broad],
        5 * wide_ff,
        all_ud,
        *x_two,
        *cot,
        copies=4 * depth + 17 + seq // TILE,
    )
    grad_two = group_reduce(two_part)

    def home(full):
        return lax.psum_scatter(full, "z", scatter_dimension=0, tiled=True)

    def from_units(mine):
        send = mine.reshape(-1, 4, part).transpose(1, 0, 2)
        return row_exchange(send).reshape(-1, part)

    home_ud = home(full_ud)

    back_two, grad_ffn_gain, grad_ffn_bias = layernorm_back(grad_two, hat_two, inv_two, params[2])
    grad_mid = cot_own.astype(F32) + back_two
    x_mid = group_gather(grad_mid.astype(BF16))

    narrow, broad = ((values_all, seq), BF16), ((values_all, width), BF16)
    plain = ((values_all, seq), F32)
    grad_gate, grad_ret, full_go = kernel_call(
        functools.partial(gated_backward, blocks),
        [narrow, narrow, (all_go.shape, BF16)],
        [broad, tall, tall, plain, plain, ((1, seq), F32), narrow, narrow, narrow, broad, broad],
        3 * wide,
        all_go,
        x_one,
        *x_mid,
        gate,
        normed,
        inv_group,
        hidden,
        copies=3 * blocks + 15,
    )
    home_go = home(full_go)
    grad_qkv, full_qkv = kernel_call(
        functools.partial(retention_backward, blocks),
        [((all_qkv.shape[0], seq), BF16), (all_qkv.shape, BF16)],
        [((seq, seq), BF16)],
        2 * seq * width * all_qkv.shape[0] + 2 * square * (keys_all + values_all),
        query,
        keys,
        values,
        weights,
        grad_ret,
        x_one,
        *where,
    )
    home_qkv = home(full_qkv)
    half = home_ud.shape[0] // 2
    grad_up, grad_down = from_wide(home_ud[:half], home_ud[half:])
    (one_part,) = kernel_call(
        functools.partial(input_backward, blocks),
        [((seq, width), BF16)],
        [((values_all, width), BF16)],
        2 * seq * width * all_qkv.shape[0] + wide,
        grad_qkv,
        all_qkv,
        after(grad_gate, full_qkv, grad_up),
        all_go,
    )
    grad_one = group_reduce(one_part)
    (ffn_part,) = kernel_call(
        functools.partial(down_forward, depth),
        [((seq, width), BF16)],
        [((hidden_all, width), BF16)],
        wide_ff,
        all_ud,
        after(act, one_part),
    )
    ffn = group_reduce(ffn_part)
    back_one, grad_attn_gain, grad_attn_bias = layernorm_back(grad_one, hat_one, inv_one, params[0])
    totals = total_over_all(
        jnp.stack([grad_attn_gain, grad_attn_bias, grad_ffn_gain, grad_ffn_bias])
    )
    totals = lax.dynamic_slice_in_dim(totals, lax.axis_index(ROW) * part, part, 1)
    grad_in, block_out = from_wide(
        (grad_mid + back_one).astype(BF16), (middle + ffn).astype(BF16)
    )
    grad_in = grad_in.astype(F32)

    def from_heads(mine):
        send = mine.reshape(2, -1, 4, part).transpose(2, 0, 1, 3).reshape(8, -1, part)
        return lax.all_to_all(send, GROUP, split_axis=0, concat_axis=0, tiled=True)

    def columns(grads, order):
        return dot(grads.reshape(-1, part), order, ((0,), (1,)))

    go = from_heads(ungroup(after(home_go, grad_in), kv, kv))
    back = from_heads(ungroup(after(home_qkv, go, totals), kq, kq, kv))
    grad_up, grad_down = grad_up.T.astype(F32), grad_down.astype(F32)
    out_gate = columns(go[:, :kv], order_v)
    out_out = dot(order_v, go[:, kv:].reshape(-1, part), ((1,), (0,)))
    out_query = columns(back[:, :kq], order_q)
    out_key = columns(back[:, kq : 2 * kq], order_q)
    out_value = columns(back[:, 2 * kq :], order_v)
    return (
        block_out,
        grad_in,
        out_query,
        out_key,
        out_value,
        out_gate,
        out_out,
        grad_up,
        grad_down,
        totals[0],
        totals[1],
        totals[2],
        totals[3],
    )


def solution(mesh):
    rows, cols = mesh.devices.shape
    fine = Mesh(mesh.devices.reshape(rows // 2, 2, cols // 2, 2), ("x", "k", "z", "y"))
    row, col = ("x", "k"), ("z", "y")
    tok, unit = P(col, row), P(row, col)
    return jax.shard_map(
        body,
        mesh=fine,
        in_specs=(tok, tok, P(row), unit, unit, unit, unit, tok, unit, tok)
        + (P(row),) * 4,
        out_specs=(tok, tok, unit, unit, unit, unit, tok, unit, tok) + (P(row),) * 4,
        check_vma=False,
    )
```

time: 631 us -> 579 us (0.918)
  Pallas kernels: 0 us -> 106 us
  matrix products: 91.3 us -> 11.4 us
  local copies, waits for them, and re-layouts: 77.4 us -> 46 us
  blocking collectives: 47.6 us -> 19.6 us
  waiting for transfers between devices: 280 us -> 266 us
  other arithmetic: 35.5 us -> 27.2 us
    pallas_call x0 -> x7, Pallas kernels: none -> 106 us  [kernel_call(): pl.pallas_call(body, out_shape=[jax.ShapeDtypeStruct(shape, kind) for sha...]
    dot_general x31 -> x10, matrix products: 91.3 us -> 11.4 us  [dot(): lax.dot_general(left, right, (over, ((), ())), preferred_element_type=F32)]
    ppermute x66 -> x67, waiting for transfers between devices: 162 us -> 131 us  [swap(): return lax.ppermute(value, GROUP, [(i, i ^ mask) for i in range(8)])]
    all_to_all x2 -> x1, blocking collectives: 36.4 us -> 19.6 us  [to_heads(): got = lax.all_to_all(send, GROUP, split_axis=0, concat_axis=0, tiled=True)]
    all_to_all x0 -> x1, waiting for transfers between devices: none -> 14.2 us  [to_heads(): got = lax.all_to_all(send, GROUP, split_axis=0, concat_axis=0, tiled=True)]
    all_to_all x1 -> x0, blocking collectives: 11.2 us -> none  [row_exchange(): return lax.all_to_all(parts, ROW, split_axis=0, concat_axis=0, tiled=True)]
    unnamed x143 -> x102, local copies, waits for them, and re-layouts: 27.9 us -> 17.7 us
    all_to_all x5 -> x4, waiting for transfers between devices: 39.3 us -> 29.6 us  [row_exchange(): return lax.all_to_all(parts, ROW, split_axis=0, concat_axis=0, tiled=True)]
  transfers between devices with their start and end apart: 83 -> 83, of which waited for: 38 -> 43; matrix products, arithmetic and copies ran while one was open for 24% -> 12% of each run, Pallas kernels for 0% -> 15%
where the time goes in v3:
time: 579 us; the launch traced here: 570 us
  waiting for transfers between devices  266 us (46%)
  Pallas kernels  106 us (18%)
  starting transfers between devices  78.1 us (13%)
  local copies, waits for them, and re-layouts  46 us (8%)
  other arithmetic  27.2 us (5%)
  blocking collectives  19.6 us (3%)
  between operations  15.9 us (3%)
  matrix products  11.4 us (2%)
    ppermute x67, waiting for transfers between devices, swap(): return lax.ppermute(value, GROUP, [(i, i ^ mask) for i in range(8)])  131 us
    pallas_call x7, Pallas kernels, kernel_call(): pl.pallas_call(body, out_shape=[jax.ShapeDtypeStruct(shape, kind) for sha...  106 us
    all_gather x3, waiting for transfers between devices, planes(): return lax.all_gather(mine, 'z', axis=0, tiled=True)  56 us
    ppermute x67, starting transfers between devices, swap(): return lax.ppermute(value, GROUP, [(i, i ^ mask) for i in range(8)])  48.6 us
    all_to_all x4, waiting for transfers between devices, row_exchange(): return lax.all_to_all(parts, ROW, split_axis=0, concat_axis=0, tiled=True)  29.6 us
    all_to_all x1, blocking collectives, to_heads(): got = lax.all_to_all(send, GROUP, split_axis=0, concat_axis=0, tiled=True)  19.6 us
    unnamed x102, local copies, waits for them, and re-layouts  17.7 us
    reduce_scatter x3, waiting for transfers between devices, home(): return lax.psum_scatter(full, 'z', scatter_dimension=0, tiled=True)  17.6 us
  transfers between devices with their start and end apart: 83, of which 43 were waited for; matrix products, arithmetic and copies ran while one was open for 12% of the time, Pallas kernels for 15%

profile of v3, /device:TPU:0, one launch (start us, length us, event | category | flops | bytes accessed | tf_op | source)
XLA Modules:
  0.0 570.1 jit_solution(11432253623674731871)
XLA Ops:
  10.7 19.6 %all_to_all.40 = bf16[8,128,512]{2,1,0:T(8,128)(2,1)S(1)} all-to-all(bf16[8,128,512]{2,1,0:T(8,128)(2,1)S(1)} %pad_maximum_fusion.1), channel_id=1, replica_groups=mesh['x'=2,'k'=2,'z'=4,'y'=2] {'x','k','y'}, dimensions={0} | all-to-all | bytes 2097152 | tf_op jit(solution)/shard_map/all_to_all | solution.py:430
  38.6 14.2 %all-to-all-done.1 = bf16[8,128,512]{2,1,0:T(8,128)(2,1)S(1)} async-done(((bf16[8,128,512]{2,1,0:T(8,128)(2,1)}), bf16[8,128,512]{2,1,0:T(8,128)(2,1)S(1)}, u32[]{:S(2)}, u32[]{:S(2)}) %all-to-all-start.1) | async-done | bytes 1048608 | tf_op jit(solution)/shard_map/all_to_all | solution.py:430
  64.9 14.3 %all-to-all-done.2 = bf16[4,2,128,512]{3,2,1,0:T(8,128)(2,1)S(1)} async-done(((bf16[4,2,128,512]{3,2,1,0:T(8,128)(2,1)}), bf16[4,2,128,512]{3,2,1,0:T(8,128)(2,1)S(1)}, u32[]{:S(2)}, u32[]{:S(2)}) %all-to-all-start.2) | async-done | bytes 1048608 | tf_op jit(solution)/shard_map/all_to_all | solution.py:93
  92.9 4.7 collective-permute-done.7
  97.6 10.1 %collective-permute-done.6 = bf16[128,2048]{1,0:T(8,128)(2,1)} collective-permute-done((bf16[128,2048]{1,0:T(8,128)(2,1)}, bf16[128,2048]{1,0:T(8,128)(2,1)}, u32[]{:S(2)}, u32[]{:S(2)}) %collective-permute-start.6) | collective-permute-done | bytes 524320 | tf_op jit(solution)/shard_map/ppermute | solution.py:29
  112.1 5.6 all-to-all-done.3
  134.3 9.9 %collective-permute-done.14.refs_13_ = bf16[128,2048]{1,0:T(8,128)(2,1)S(1)} collective-permute-done((bf16[128,2048]{1,0:T(8,128)(2,1)S(1)}, bf16[128,2048]{1,0:T(8,128)(2,1)S(1)}, u32[]{:S(2)}, u32[]{:S(2)}) %collective-permute-start.14) | collective-permute-done | bytes 524320 | tf_op jit(solution)/shard_map/ppermute | solution.py:29
  144.2 9.3 %collective-permute-done.13.refs_12_ = bf16[128,2048]{1,0:T(8,128)(2,1)S(1)} collective-permute-done((bf16[128,2048]{1,0:T(8,128)(2,1)S(1)}, bf16[128,2048]{1,0:T(8,128)(2,1)S(1)}, u32[]{:S(2)}, u32[]{:S(2)}) %collective-permute-start.13) | collective-permute-done | bytes 524320 | tf_op jit(solution)/shard_map/ppermute | solution.py:29
  154.0 15.4 %shard_map.237 = (bf16[256,1024]{1,0:T(8,128)(2,1)}, bf16[256,1024]{1,0:T(8,128)(2,1)}, bf16[512,1024]{1,0:T(8,128)(2,1)}, bf16[1024,1024]{1,0:T(8,128)(2,1)}, f32[512,1024]{1,0:T(8,128)}, /*index=5*/f32[1,1024]{1,0:T(1,128)}) custom-call(bf16[1024,2048]{1,0:T(8,128)(2,1)} %all-gather.6.cloned.1.call-done.w, ...), custom_call_target="tpu_custom_call" | custom-call | flops 5905580032 | bytes 14708736 | tf_op jit(solution)/shard_map/pallas_call | solution.py:155
  169.5 25.5 %all-gather.4.cloned.1.call-done.w.wgo = bf16[1024,2048]{1,0:T(8,128)(2,1)} async-done(((bf16[256,2048]{1,0:T(8,128)(2,1)}), bf16[1024,2048]{1,0:T(8,128)(2,1)}) %all-gather.4.cloned.1.call-update) | async-done | bytes 4194320 | tf_op jit(solution)/shard_map/all_gather | solution.py:454
  195.0 16.1 %shard_map.238 = (f32[512,1024]{1,0:T(8,128)}, bf16[512,1024]{1,0:T(8,128)(2,1)}, bf16[1024,2048]{1,0:T(8,128)(2,1)}) custom-call(bf16[1024,2048]{1,0:T(8,128)(2,1)} %all-gather.4.cloned.1.call-done.w.wgo, bf16[1024,2048]{1,0:T(8,128)(2,1)} %constant_dynamic-update-slice_fusion.1.x.x_in, f32[512,1024]{1,0:T(8,128)} %get-tuple-element.57.normed.refs_9_), custom_call_target="tpu_custom_call" | custom-call | flops 4294967296 | bytes 17825792 | tf_op jit(solution)/shard_map/pallas_call | solution.py:155
  220.2 5.2 collective-permute-done.23
  228.8 10.1 %collective-permute-done.24 = bf16[128,2048]{1,0:T(8,128)(2,1)S(1)} collective-permute-done((bf16[128,2048]{1,0:T(8,128)(2,1)S(1)}, bf16[128,2048]{1,0:T(8,128)(2,1)S(1)}, u32[]{:S(2)}, u32[]{:S(2)}) %collective-permute-start.24) | collective-permute-done | bytes 524320 | tf_op jit(solution)/shard_map/ppermute | solution.py:29
  245.9 30.5 %all-gather.8.cloned.1.call-done.w = bf16[1024,2048]{1,0:T(8,128)(2,1)} async-done(((bf16[256,2048]{1,0:T(8,128)(2,1)}), bf16[1024,2048]{1,0:T(8,128)(2,1)}) %all-gather.8.cloned.1.call-update) | async-done | bytes 4194320 | tf_op jit(solution)/shard_map/all_gather | solution.py:454
  282.2 18.9 %shard_map.239 = (bf16[512,1024]{1,0:T(8,128)(2,1)}, bf16[1024,2048]{1,0:T(8,128)(2,1)}, bf16[1024,2048]{1,0:T(8,128)(2,1)}) custom-call(bf16[1024,2048]{1,0:T(8,128)(2,1)} %all-gather.8.cloned.1.call-done.w, bf16[128,2048]{1,0:T(8,128)(2,1)} %copy-done.15, bf16[128,2048]{1,0:T(8,128)(2,1)} %collective-permute-done.25.refs_1_, bf16[128,2048]{1,0:T(8,128)(2,1)} %copy-done.35, ...), custom_call_target="tpu_custom_call" | custom-call | flops 10737418240 | bytes 22020096 | tf_op jit(solution)/shard_map/pallas_call | solution.py:155
  310.3 5.2 collective-permute-done.38
  318.9 10.1 %collective-permute-done.39 = bf16[128,2048]{1,0:T(8,128)(2,1)S(1)} collective-permute-done((bf16[128,2048]{1,0:T(8,128)(2,1)S(1)}, bf16[128,2048]{1,0:T(8,128)(2,1)S(1)}, u32[]{:S(2)}, u32[]{:S(2)}) %collective-permute-start.39) | collective-permute-done | bytes 524320 | tf_op jit(solution)/shard_map/ppermute | solution.py:29
  337.1 12.3 %collective-permute-done.44.refs_5_ = bf16[128,2048]{1,0:T(8,128)(2,1)S(1)} collective-permute-done((bf16[128,2048]{1,0:T(8,128)(2,1)S(1)}, bf16[128,2048]{1,0:T(8,128)(2,1)S(1)}, u32[]{:S(2)}, u32[]{:S(2)}) %collective-permute-start.44) | collective-permute-done | bytes 524320 | tf_op jit(solution)/shard_map/ppermute | solution.py:29
  349.5 9.3 %collective-permute-done.43.refs_4_ = bf16[128,2048]{1,0:T(8,128)(2,1)S(1)} collective-permute-done((bf16[128,2048]{1,0:T(8,128)(2,1)S(1)}, bf16[128,2048]{1,0:T(8,128)(2,1)S(1)}, u32[]{:S(2)}, u32[]{:S(2)}) %collective-permute-start.43) | collective-permute-done | bytes 524320 | tf_op jit(solution)/shard_map/ppermute | solution.py:29
  362.2 16.9 %shard_map.240 = (bf16[512,1024]{1,0:T(8,128)(2,1)}, bf16[512,1024]{1,0:T(8,128)(2,1)}, bf16[1024,2048]{1,0:T(8,128)(2,1)}) custom-call(bf16[1024,2048]{1,0:T(8,128)(2,1)} %all-gather.4.cloned.1.call-done.w.wgo, bf16[1024,2048]{1,0:T(8,128)(2,1)} %constant_dynamic-update-slice_fusion.1.x.x_in, bf16[128,2048]{1,0:T(8,128)(2,1)} %copy-done.16, ...), custom_call_target="tpu_custom_call" | custom-call | flops 6442450944 | bytes 24121344 | tf_op jit(solution)/shard_map/pallas_call | solution.py:155
  386.1 17.2 %shard_map.241 = (bf16[1024,1024]{1,0:T(8,128)(2,1)}, bf16[1024,2048]{1,0:T(8,128)(2,1)}) custom-call(bf16[256,1024]{1,0:T(8,128)(2,1)} %get-tuple-element.65.q, bf16[256,1024]{1,0:T(8,128)(2,1)} %get-tuple-element.66.k, bf16[512,1024]{1,0:T(8,128)(2,1)} %get-tuple-element.67.v, bf16[1024,1024]{1,0:T(8,128)(2,1)} %get-tuple-element.68.weights, ...), custom_call_target="tpu_custom_call" | custom-call | flops 7516192768 | bytes 15753216 | tf_op jit(solution)/shard_map/pallas_call | solution.py:155
  404.4 14.0 %shard_map.242 = bf16[1024,2048]{1,0:T(8,128)(2,1)} custom-call(bf16[1024,1024]{1,0:T(8,128)(2,1)} %get-tuple-element.73.packed, bf16[1024,2048]{1,0:T(8,128)(2,1)} %all-gather.6.cloned.1.call-done.w, bf16[512,1024]{1,0:T(8,128)(2,1)} %get-tuple-element.77.ggate, bf16[1024,2048]{1,0:T(8,128)(2,1)} %all-gather.4.cloned.1.call-done.w.wgo), custom_call_target="tpu_custom_call" | custom-call | flops 6442450944 | bytes 15728640 | tf_op jit(solution)/shard_map/pallas_call | solution.py:155
  418.4 7.7 %shard_map.243 = bf16[1024,2048]{1,0:T(8,128)(2,1)} custom-call(bf16[1024,2048]{1,0:T(8,128)(2,1)} %all-gather.8.cloned.1.call-done.w, bf16[512,1024]{1,0:T(8,128)(2,1)} %get-tuple-element.79.act), custom_call_target="tpu_custom_call" | custom-call | flops 2147483648 | bytes 9437184 | tf_op jit(solution)/shard_map/pallas_call | solution.py:155
  447.9 4.5 collective-permute-done.53
  457.4 4.1 collective-permute-done.62
  461.5 5.7 collective-permute-done.59
  468.1 4.3 collective-permute-done.54
  489.0 9.8 %all-to-all-done.5 = bf16[4,2,128,512]{3,2,1,0:T(8,128)(2,1)S(1)} async-done(((bf16[4,2,128,512]{3,2,1,0:T(8,128)(2,1)}), bf16[4,2,128,512]{3,2,1,0:T(8,128)(2,1)S(1)}, u32[]{:S(2)}, u32[]{:S(2)}) %all-to-all-start.5) | async-done | bytes 1048608 | tf_op jit(solution)/shard_map/all_to_all | solution.py:93
  503.8 3.8 all-to-all-start.6
  513.8 6.3 %collective-permute-done.68 = f32[4,2048]{1,0:T(4,128)S(1)} collective-permute-done((f32[4,2048]{1,0:T(4,128)S(1)}, f32[4,2048]{1,0:T(4,128)S(1)}, u32[]{:S(2)}, u32[]{:S(2)}) %collective-permute-start.68) | collective-permute-done | bytes 32800 | tf_op jit(solution)/shard_map/ppermute | solution.py:78
  520.1 17.6 %reduce-scatter.6.cloned.1.call-done = bf16[256,2048]{1,0:T(8,128)(2,1)} async-done(((bf16[1024,2048]{1,0:T(8,128)(2,1)}), bf16[256,2048]{1,0:T(8,128)(2,1)}) %reduce-scatter.6.cloned.1.call-update) | async-done | bytes 1048592 | tf_op jit(solution)/shard_map/reduce_scatter | solution.py:559
  548.1 10.8 %all-to-all-done.7 = bf16[8,128,512]{2,1,0:T(8,128)(2,1)S(1)} async-done(((bf16[8,128,512]{2,1,0:T(8,128)(2,1)}), bf16[8,128,512]{2,1,0:T(8,128)(2,1)S(1)}, u32[]{:S(2)}, u32[]{:S(2)}) %all-to-all-start.7) | async-done | bytes 1048608 | tf_op jit(solution)/shard_map/all_to_all | solution.py:636
  (379 shorter events, 185.3 us)
Async XLA Ops:
  7.2 146.8 %all-gather.6.cloned.1.call-start = ((), (), s32[]{:S(2)}) async-start(), calls=%async_computation.12 | async-start | bytes 5242880 | tf_op jit(solution)/shard_map/all_gather | solution.py:454
  34.6 18.2 %all-to-all-start.1 = ((bf16[8,128,512]{2,1,0:T(8,128)(2,1)}), bf16[8,128,512]{2,1,0:T(8,128)(2,1)S(1)}, u32[]{:S(2)}, u32[]{:S(2)}) async-start(bf16[8,128,512]{2,1,0:T(8,128)(2,1)} %pad_maximum_fusion), calls=%async_computation.1 | async-start | bytes 2097152 | tf_op jit(solution)/shard_map/all_to_all | solution.py:430
  38.3 156.6 %all-gather.4.cloned.1.call-start = ((), (), s32[]{:S(2)}) async-start(), calls=%async_computation.11 | async-start | bytes 5242880 | tf_op jit(solution)/shard_map/all_gather | solution.py:454
  81.7 26.1 %collective-permute-start.6 = (bf16[128,2048]{1,0:T(8,128)(2,1)}, bf16[128,2048]{1,0:T(8,128)(2,1)}, u32[]{:S(2)}, u32[]{:S(2)}) collective-permute-start(bf16[128,2048]{1,0:T(8,128)(2,1)} %get-tuple-element.98), channel_id=1, source_target_pairs={{0,16},{1,17},{8,24},{9,25},{16,0},{17,1},{24,8},{25,9},{2,18},{3,... | collective-permute-start | bytes 1572872 | tf_op jit(solution)/shard_map/ppermute | solution.py:29
  83.4 24.4 %collective-permute-start.3 = (bf16[128,2048]{1,0:T(8,128)(2,1)}, bf16[128,2048]{1,0:T(8,128)(2,1)}, u32[]{:S(2)}, u32[]{:S(2)}) collective-permute-start(bf16[128,2048]{1,0:T(8,128)(2,1)} %get-tuple-element.98), channel_id=1, source_target_pairs={{0,1},{1,0},{8,9},{9,8},{16,17},{17,16},{24,25},{25,24},{2,3},{3,2... | collective-permute-start | bytes 1572872 | tf_op jit(solution)/shard_map/ppermute | solution.py:29
  86.3 31.3 %all-to-all-start.3 = ((bf16[4,2,128,512]{3,2,1,0:T(8,128)(2,1)}), bf16[4,2,128,512]{3,2,1,0:T(8,128)(2,1)S(1)}, u32[]{:S(2)}, u32[]{:S(2)}) async-start(bf16[4,2,128,512]{3,2,1,0:T(8,128)(2,1)} %pad_maximum_fusion.3), calls=%async_computation.3 | async-start | bytes 2097152 | tf_op jit(solution)/shard_map/all_to_all | solution.py:93
  89.8 186.6 %all-gather.8.cloned.1.call-start = ((), (), s32[]{:S(2)}) async-start(), calls=%async_computation.13 | async-start | bytes 5242880 | tf_op jit(solution)/shard_map/all_gather | solution.py:454
  89.9 20.3 %collective-permute-start.4 = (bf16[128,2048]{1,0:T(8,128)(2,1)}, bf16[128,2048]{1,0:T(8,128)(2,1)}, u32[]{:S(2)}, u32[]{:S(2)}) collective-permute-start(bf16[128,2048]{1,0:T(8,128)(2,1)} %get-tuple-element.98), channel_id=1, source_target_pairs={{0,8},{1,9},{8,0},{9,1},{16,24},{17,25},{24,16},{25,17},{2,10},{3,... | collective-permute-start | bytes 1572872 | tf_op jit(solution)/shard_map/ppermute | solution.py:29
  97.6 28.9 %collective-permute-start.9 = (bf16[128,2048]{1,0:T(8,128)(2,1)}, bf16[128,2048]{1,0:T(8,128)(2,1)}, u32[]{:S(2)}, u32[]{:S(2)}) collective-permute-start(bf16[128,2048]{1,0:T(8,128)(2,1)} %collective-permute-done.7), channel_id=1, source_target_pairs={{0,8},{1,9},{8,0},{9,1},{16,24},{17,25},{24,16},{25,17},{2,10},{3,... | collective-permute-start | bytes 1572872 | tf_op jit(solution)/shard_map/ppermute | solution.py:29
  130.2 23.3 %collective-permute-start.13 = (bf16[128,2048]{1,0:T(8,128)(2,1)S(1)}, bf16[128,2048]{1,0:T(8,128)(2,1)S(1)}, u32[]{:S(2)}, u32[]{:S(2)}) collective-permute-start(bf16[128,2048]{1,0:T(8,128)(2,1)S(1)} %bitcast.126), channel_id=1, source_target_pairs={{0,16},{1,17},{8,24},{9,25},{16,0},{17,1},{24,8},{25,9},{2,18},{3,... | collective-permute-start | bytes 1572872 | tf_op jit(solution)/shard_map/ppermute | solution.py:29
  131.5 22.0 %collective-permute-start.10 = (bf16[128,2048]{1,0:T(8,128)(2,1)S(1)}, bf16[128,2048]{1,0:T(8,128)(2,1)}, u32[]{:S(2)}, u32[]{:S(2)}) collective-permute-start(bf16[128,2048]{1,0:T(8,128)(2,1)S(1)} %bitcast.127), channel_id=1, source_target_pairs={{0,1},{1,0},{8,9},{9,8},{16,17},{17,16},{24,25},{25,24},{2,3},{3,2... | collective-permute-start | bytes 1572872 | tf_op jit(solution)/shard_map/ppermute | solution.py:29
  134.2 245.0 %reduce-scatter.4.cloned.1.call-start = ((), (), s32[]{:S(2)}) async-start(), calls=%async_computation.14 | async-start | bytes 5242880 | tf_op jit(solution)/shard_map/reduce_scatter | solution.py:559
  134.2 35.2 %collective-permute-start.11 = (bf16[128,2048]{1,0:T(8,128)(2,1)S(1)}, bf16[128,2048]{1,0:T(8,128)(2,1)S(1)}, u32[]{:S(2)}, u32[]{:S(2)}) collective-permute-start(bf16[128,2048]{1,0:T(8,128)(2,1)S(1)} %bitcast.128), channel_id=1, source_target_pairs={{0,8},{1,9},{8,0},{9,1},{16,24},{17,25},{24,16},{25,17},{2,10},{3,... | collective-permute-start | bytes 1572872 | tf_op jit(solution)/shard_map/ppermute | solution.py:29
  144.2 25.3 %collective-permute-start.16 = (bf16[128,2048]{1,0:T(8,128)(2,1)S(1)}, bf16[128,2048]{1,0:T(8,128)(2,1)S(1)}, u32[]{:S(2)}, u32[]{:S(2)}) collective-permute-start(bf16[128,2048]{1,0:T(8,128)(2,1)S(1)} %collective-permute-done.14.refs_13_), channel_id=1, source_target_pairs={{0,8},{1,9},{8,0},{9,1},{16,24},{17,25},{24,16},{25,17},{2,10},{3,... | collective-permute-start | bytes 1572872 | tf_op jit(solution)/shard_map/ppermute | solution.py:29
  242.4 34.1 %collective-permute-start.29 = (bf16[128,2048]{1,0:T(8,128)(2,1)S(1)}, bf16[128,2048]{1,0:T(8,128)(2,1)S(1)}, u32[]{:S(2)}, u32[]{:S(2)}) collective-permute-start(bf16[128,2048]{1,0:T(8,128)(2,1)S(1)} %add_convert_fusion.4.refs_0_), channel_id=1, source_target_pairs={{0,17},{1,16},{8,25},{9,24},{16,1},{17,0},{24,9},{25,8},{2,19},{3,... | collective-permute-start | bytes 1572872 | tf_op jit(solution)/shard_map/ppermute | solution.py:29
  243.9 33.1 %collective-permute-start.28 = (bf16[128,2048]{1,0:T(8,128)(2,1)S(1)}, bf16[128,2048]{1,0:T(8,128)(2,1)S(1)}, u32[]{:S(2)}, u32[]{:S(2)}) collective-permute-start(bf16[128,2048]{1,0:T(8,128)(2,1)S(1)} %add_convert_fusion.4.refs_0_), channel_id=1, source_target_pairs={{0,16},{1,17},{8,24},{9,25},{16,0},{17,1},{24,8},{25,9},{2,18},{3,... | collective-permute-start | bytes 1572872 | tf_op jit(solution)/shard_map/ppermute | solution.py:29
  245.4 31.7 %collective-permute-start.25 = (bf16[128,2048]{1,0:T(8,128)(2,1)S(1)}, bf16[128,2048]{1,0:T(8,128)(2,1)}, u32[]{:S(2)}, u32[]{:S(2)}) collective-permute-start(bf16[128,2048]{1,0:T(8,128)(2,1)S(1)} %add_convert_fusion.4.refs_0_), channel_id=1, source_target_pairs={{0,1},{1,0},{8,9},{9,8},{16,17},{17,16},{24,25},{25,24},{2,3},{3,2... | collective-permute-start | bytes 1572872 | tf_op jit(solution)/shard_map/ppermute | solution.py:29
  301.1 199.6 %reduce-scatter.8.cloned.1.call-start = ((), (), s32[]{:S(2)}) async-start(), calls=%async_computation.16 | async-start | bytes 5242880 | tf_op jit(solution)/shard_map/reduce_scatter | solution.py:559
  335.1 23.6 %collective-permute-start.43 = (bf16[128,2048]{1,0:T(8,128)(2,1)S(1)}, bf16[128,2048]{1,0:T(8,128)(2,1)S(1)}, u32[]{:S(2)}, u32[]{:S(2)}) collective-permute-start(bf16[128,2048]{1,0:T(8,128)(2,1)S(1)} %get-tuple-element.92.refs_0_), channel_id=1, source_target_pairs={{0,16},{1,17},{8,24},{9,25},{16,0},{17,1},{24,8},{25,9},{2,18},{3,... | collective-permute-start | bytes 1572872 | tf_op jit(solution)/shard_map/ppermute | solution.py:29
  336.6 22.2 %collective-permute-start.40 = (bf16[128,2048]{1,0:T(8,128)(2,1)S(1)}, bf16[128,2048]{1,0:T(8,128)(2,1)S(1)}, u32[]{:S(2)}, u32[]{:S(2)}) collective-permute-start(bf16[128,2048]{1,0:T(8,128)(2,1)S(1)} %get-tuple-element.92.refs_0_), channel_id=1, source_target_pairs={{0,1},{1,0},{8,9},{9,8},{16,17},{17,16},{24,25},{25,24},{2,3},{3,2... | collective-permute-start | bytes 1572872 | tf_op jit(solution)/shard_map/ppermute | solution.py:29
  337.1 22.1 %collective-permute-start.41 = (bf16[128,2048]{1,0:T(8,128)(2,1)S(1)}, bf16[128,2048]{1,0:T(8,128)(2,1)S(1)}, u32[]{:S(2)}, u32[]{:S(2)}) collective-permute-start(bf16[128,2048]{1,0:T(8,128)(2,1)S(1)} %get-tuple-element.92.refs_0_), channel_id=1, source_target_pairs={{0,8},{1,9},{8,0},{9,1},{16,24},{17,25},{24,16},{25,17},{2,10},{3,... | collective-permute-start | bytes 1572872 | tf_op jit(solution)/shard_map/ppermute | solution.py:29
  382.5 20.8 %all-to-all-start.4 = ((bf16[4,2,128,512]{3,2,1,0:T(8,128)(2,1)}), bf16[4,2,128,512]{3,2,1,0:T(8,128)(2,1)S(1)}, u32[]{:S(2)}, u32[]{:S(2)}) async-start(bf16[4,2,128,512]{3,2,1,0:T(8,128)(2,1)} %maximum_bitcast_fusion), calls=%async_computation.5 | async-start | bytes 2097152 | tf_op jit(solution)/shard_map/all_to_all | solution.py:93
  386.0 151.6 %reduce-scatter.6.cloned.1.call-start = ((), (), s32[]{:S(2)}) async-start(), calls=%async_computation.15 | async-start | bytes 5242880 | tf_op jit(solution)/shard_map/reduce_scatter | solution.py:559
  429.7 27.0 %collective-permute-start.55 = (bf16[128,2048]{1,0:T(8,128)(2,1)S(1)}, bf16[128,2048]{1,0:T(8,128)(2,1)S(1)}, u32[]{:S(2)}, u32[]{:S(2)}) collective-permute-start(bf16[128,2048]{1,0:T(8,128)(2,1)S(1)} %get-tuple-element.106), channel_id=1, source_target_pairs={{0,8},{1,9},{8,0},{9,1},{16,24},{17,25},{24,16},{25,17},{2,10},{3,... | collective-permute-start | bytes 1572872 | tf_op jit(solution)/shard_map/ppermute | solution.py:29
  432.5 35.6 %collective-permute-start.47 = (bf16[128,2048]{1,0:T(8,128)(2,1)}, bf16[128,2048]{1,0:T(8,128)(2,1)}, u32[]{:S(2)}, u32[]{:S(2)}) collective-permute-start(bf16[128,2048]{1,0:T(8,128)(2,1)} %get-tuple-element.99), channel_id=1, source_target_pairs={{0,8},{1,9},{8,0},{9,1},{16,24},{17,25},{24,16},{25,17},{2,10},{3,... | collective-permute-start | bytes 1572872 | tf_op jit(solution)/shard_map/ppermute | solution.py:29
  456.7 19.3 %collective-permute-start.51 = (bf16[128,2048]{1,0:T(8,128)(2,1)}, bf16[128,2048]{1,0:T(8,128)(2,1)}, u32[]{:S(2)}, u32[]{:S(2)}) collective-permute-start(bf16[128,2048]{1,0:T(8,128)(2,1)} %pad_maximum_fusion.9), channel_id=1, source_target_pairs={{0,16},{1,17},{8,24},{9,25},{16,0},{17,1},{24,8},{25,9},{2,18},{3,... | collective-permute-start | bytes 1572872 | tf_op jit(solution)/shard_map/ppermute | solution.py:29
  480.3 18.4 %all-to-all-start.5 = ((bf16[4,2,128,512]{3,2,1,0:T(8,128)(2,1)}), bf16[4,2,128,512]{3,2,1,0:T(8,128)(2,1)S(1)}, u32[]{:S(2)}, u32[]{:S(2)}) async-start(bf16[4,2,128,512]{3,2,1,0:T(8,128)(2,1)} %maximum_bitcast_fusion.1), calls=%async_computation.6 | async-start | bytes 2097152 | tf_op jit(solution)/shard_map/all_to_all | solution.py:93
  485.4 23.4 %collective-permute-start.65 = (f32[4,2048]{1,0:T(4,128)S(1)}, f32[4,2048]{1,0:T(4,128)S(1)}, u32[]{:S(2)}, u32[]{:S(2)}) collective-permute-start(f32[4,2048]{1,0:T(4,128)S(1)} %fusion.61), channel_id=1, source_target_pairs={{0,16},{1,17},{8,24},{9,25},{16,0},{17,1},{24,8},{25,9},{2,18},{3,... | collective-permute-start | bytes 98312 | tf_op jit(solution)/shard_map/ppermute | solution.py:29
  487.2 21.5 %collective-permute-start.66 = (f32[4,2048]{1,0:T(4,128)S(1)}, f32[4,2048]{1,0:T(4,128)S(1)}, u32[]{:S(2)}, u32[]{:S(2)}) collective-permute-start(f32[4,2048]{1,0:T(4,128)S(1)} %fusion.61), channel_id=1, source_target_pairs={{0,17},{1,16},{8,25},{9,24},{16,1},{17,0},{24,9},{25,8},{2,19},{3,... | collective-permute-start | bytes 98312 | tf_op jit(solution)/shard_map/ppermute | solution.py:29
  488.3 20.4 %collective-permute-start.64 = (f32[4,2048]{1,0:T(4,128)S(1)}, f32[4,2048]{1,0:T(4,128)S(1)}, u32[]{:S(2)}, u32[]{:S(2)}) collective-permute-start(f32[4,2048]{1,0:T(4,128)S(1)} %fusion.61), channel_id=1, source_target_pairs={{0,1},{1,0},{8,9},{9,8},{16,17},{17,16},{24,25},{25,24},{2,3},{3,2... | collective-permute-start | bytes 98312 | tf_op jit(solution)/shard_map/ppermute | solution.py:29
  503.8 33.8 %all-to-all-start.6 = ((bf16[8,128,512]{2,1,0:T(8,128)(2,1)}), bf16[8,128,512]{2,1,0:T(8,128)(2,1)S(1)}, u32[]{:S(2)}, u32[]{:S(2)}) async-start(bf16[8,128,512]{2,1,0:T(8,128)(2,1)} %bitcast.41), calls=%async_computation.9 | async-start | bytes 2097152 | tf_op jit(solution)/shard_map/all_to_all | solution.py:636
  540.7 18.2 %all-to-all-start.7 = ((bf16[8,128,512]{2,1,0:T(8,128)(2,1)}), bf16[8,128,512]{2,1,0:T(8,128)(2,1)S(1)}, u32[]{:S(2)}, u32[]{:S(2)}) async-start(bf16[8,128,512]{2,1,0:T(8,128)(2,1)} %bitcast.109), calls=%async_computation.10 | async-start | bytes 2097152 | tf_op jit(solution)/shard_map/all_to_all | solution.py:636
  (94 other events, 1057.7 us)
Sparse Core Ops, SparseCore 0:
  32.5 81.0 all-gather.5
  115.7 79.2 all-gather.3
  197.1 79.2 all-gather.7
  301.3 75.2 reduce-scatter.3
  379.3 76.8 reduce-scatter.7
  458.3 79.3 reduce-scatter.5

commit v4 on v3

--- a/solution.py
+++ b/solution.py
@@ -137,6 +137,7 @@
 
 TILE = 256
 WIDE = 512
+TALL = 512
 LIMIT = 58 * 1024 * 1024
 
 
@@ -268,22 +269,24 @@
 def feedforward(depth, w, *refs):
     x_blocks, cot_blocks = refs[:8], refs[8:16]
     act_out, back_out, grads_out = refs[16:19]
-    wu, wd, x, cot, act, gp, back, gu, gd, semaphores = refs[19:]
+    wu, wd, x, cot, act, gp, turned, back, gu, gd, semaphores = refs[19:]
     move = Mover(semaphores)
     seq, rows = x.shape[0], x_blocks[0].shape[0]
     weights = move.kind(w, wu, ("from", 0), depth) + move.kind(w, wd, ("from", 1), depth)
     x_copies, cot_copies = move.rows(x_blocks, x), move.rows(cot_blocks, cot)
     wait(weights)
-    for tile in range(seq // TILE):
-        mine = slice(tile * TILE // rows, (tile + 1) * TILE // rows)
+    for tile in range(seq // TALL):
+        mine = slice(tile * TALL // rows, (tile + 1) * TALL // rows)
         wait(x_copies[mine] + cot_copies[mine])
-        at = pl.ds(tile * TILE, TILE)
+        at = pl.ds(tile * TALL, TALL)
         pre = dot(wu[...], x[at, :], ((1,), (1,)))
         grad = dot(wd[...], cot[at, :], ((1,), (1,)))
         half = 0.5 * (1.0 + lax.erf(pre * np.float32(0.5**0.5)))
         act[:, at] = (pre * half).astype(BF16)
         bell = jnp.exp(-0.5 * pre * pre) * np.float32((2 * math.pi) ** -0.5)
-        gp[:, at] = (grad * (half + pre * bell)).astype(BF16)
+        low = grad * (half + pre * bell)
+        gp[:, at] = low.astype(BF16)
+        turned[at, :] = low.T.astype(BF16)
     sent = [move.start(act, act_out)]
 
     def up_step(at):
@@ -296,10 +299,10 @@
     sent += move.kind(gu, grads_out, ("to", 0), depth)
     spans(x.shape[1], WIDE, down_step)
     sent += move.kind(gd, grads_out, ("to", 1), depth)
-    for tile in range(seq // TILE):
-        at = pl.ds(tile * TILE, TILE)
-        back[at, :] = dot(gp[:, at], wu[...], ((0,), (0,))).astype(BF16)
-        sent.append(move.start(back.at[at], back_out.at[at]))
+    for tile in range(x.shape[1] // WIDE):
+        at = pl.ds(tile * WIDE, WIDE)
+        back[:, at] = dot(turned[...], wu[:, at], ((1,), (0,))).astype(BF16)
+        sent.append(move.start(back.at[:, at], back_out.at[:, at]))
     wait(sent)
 
 
@@ -319,14 +322,14 @@
     move = Mover(semaphores)
     seq, rows = x.shape[0], mid_blocks[0].shape[0]
     first = move.kind(w, wo, ("from", 1), depth)
-    mid_copies = move.rows(mid_blocks[:2], mid.at[pl.ds(0, 2 * rows)])
+    mid_copies = move.rows(mid_blocks[:4], mid.at[pl.ds(0, 4 * rows)])
     first += [move.start(inv_in, inv), move.start(gate_in, gate), move.start(normed_in, normed)]
-    mid_copies += move.rows(mid_blocks[2:], mid.at[pl.ds(2 * rows, seq - 2 * rows)])
+    mid_copies += move.rows(mid_blocks[4:], mid.at[pl.ds(4 * rows, seq - 4 * rows)])
     late = [move.start(x_in, x), move.start(hidden_in, hidden)]
     wait(first)
-    for tile in range(seq // TILE):
-        wait(mid_copies[tile * TILE // rows : (tile + 1) * TILE // rows])
-        at = pl.ds(tile * TILE, TILE)
+    for tile in range(seq // TALL):
+        wait(mid_copies[tile * TALL // rows : (tile + 1) * TALL // rows])
+        at = pl.ds(tile * TALL, TALL)
         up = dot(wo[...], mid[at, :], ((1,), (1,)))
         g = gate[:, at]
         s = jax.nn.sigmoid(g)
@@ -376,12 +379,25 @@
         place(dot(q[...], scores[:, at], ((1,), (0,))).astype(BF16), at, part, part)
         place(dot(gret[...], weights[:, at], ((1,), (0,))).astype(BF16), at, 2 * part, width)
 
-    def grad_step(at):
-        grads[:, at] = dot(packed[...], x[:, at], ((1,), (0,))).astype(BF16)
-
     spans(seq, TILE, query_step)
     spans(seq, TILE, key_step)
-    spans(x.shape[1], WIDE, grad_step)
+    if len(grads.shape) == 2:
+
+        def grad_step(at):
+            grads[:, at] = dot(packed[...], x[:, at], ((1,), (0,))).astype(BF16)
+
+        spans(x.shape[1], WIDE, grad_step)
+        return
+
+    def home_step(row, carry):
+        columns = grads.shape[3]
+        at = pl.ds(pl.multiple_of(row * columns, columns), columns)
+        full = dot(packed[...], x[:, at], ((1,), (0,))).astype(BF16)
+        for i in range(depth):
+            grads[i // 2, 2 * row + i % 2, :, :] = full[i * group : (i + 1) * group]
+        return carry
+
+    lax.fori_loop(0, 4, home_step, 0)
 
 
 def input_backward(depth, packed, w, ggate, wgo, out, wg):
@@ -538,7 +554,8 @@
     middle = stream + group_reduce(attn)
 
     hat_two, inv_two, norm_two = layernorm(middle, params[2], params[3])
-    x_two = group_gather(norm_two, all_ud)
+    x_two = group_gather(norm_two)
+    token = swap(after(norm_two[:8, :128], all_ud), 2)
     hidden_all = all_ud.shape[0] // 2
     wide_ff = 2 * seq * width * hidden_all
     narrow, broad = ((hidden_all, seq), BF16), ((hidden_all, width), BF16)
@@ -546,12 +563,13 @@
     act, two_part, full_ud = kernel_call(
         functools.partial(feedforward, depth),
         [narrow, tall, (all_ud.shape, BF16)],
-        [broad, broad, tall, tall, narrow, narrow, tall, broad, broad],
+        [broad, broad, tall, tall, narrow, narrow, ((seq, hidden_all), BF16), tall, broad, broad],
         5 * wide_ff,
         all_ud,
         *x_two,
-        *cot,
-        copies=4 * depth + 17 + seq // TILE,
+        after(cot[0], token),
+        *cot[1:],
+        copies=4 * depth + 17 + width // WIDE,
     )
     grad_two = group_reduce(two_part)
 
@@ -585,9 +603,10 @@
         copies=3 * blocks + 15,
     )
     home_go = home(full_go)
+    home_shape = (depth, 8, 2 * kq + kv, part) if split == 2 else all_qkv.shape
     grad_qkv, full_qkv = kernel_call(
         functools.partial(retention_backward, blocks),
-        [((all_qkv.shape[0], seq), BF16), (all_qkv.shape, BF16)],
+        [((all_qkv.shape[0], seq), BF16), (home_shape, BF16)],
         [((seq, seq), BF16)],
         2 * seq * width * all_qkv.shape[0] + 2 * square * (keys_all + values_all),
         query,
@@ -639,7 +658,12 @@
         return dot(grads.reshape(-1, part), order, ((0,), (1,)))
 
     go = from_heads(ungroup(after(home_go, grad_in), kv, kv))
-    back = from_heads(ungroup(after(home_qkv, go, totals), kq, kq, kv))
+    home_qkv = after(home_qkv, go, totals)
+    if split == 2:
+        home_qkv = home_qkv.reshape(8, 2 * kq + kv, part)
+        back = lax.all_to_all(home_qkv, GROUP, split_axis=0, concat_axis=0, tiled=True)
+    else:
+        back = from_heads(ungroup(home_qkv, kq, kq, kv))
     grad_up, grad_down = grad_up.T.astype(F32), grad_down.astype(F32)
     out_gate = columns(go[:, :kv], order_v)
     out_out = dot(order_v, go[:, kv:].reshape(-1, part), ((1,), (0,)))

time: 579 us -> 570 us (0.984)
  waiting for transfers between devices: 266 us -> 259 us
    all_gather x3, waiting for transfers between devices: 56 us -> 34.3 us  [planes(): return lax.all_gather(mine, 'z', axis=0, tiled=True)]
    ppermute x67, waiting for transfers between devices: 131 us -> 149 us  [swap(): return lax.ppermute(value, GROUP, [(i, i ^ mask) for i in range(8)])]
    all_to_all x0 -> x1, waiting for transfers between devices: none -> 10.8 us  [body(): lax.all_to_all(home_qkv, GROUP, split_axis=0, concat_axis=0, tiled=True)]
    all_to_all x2 -> x1, waiting for transfers between devices: 10.8 us -> 0.01 us  [from_heads(): return lax.all_to_all(send, GROUP, split_axis=0, concat_axis=0, tiled=True)]
    unnamed x102 -> x94, local copies, waits for them, and re-layouts: 17.7 us -> 15.4 us
  transfers between devices with their start and end apart: 83 -> 83, of which waited for: 43 -> 43; matrix products, arithmetic and copies ran while one was open for 12% -> 13% of each run, Pallas kernels for 15% -> 15%
where the time goes in v4:
time: 570 us; the launch traced here: 561 us
  waiting for transfers between devices  259 us (45%)
  Pallas kernels  104 us (18%)
  starting transfers between devices  79.4 us (14%)
  local copies, waits for them, and re-layouts  42.7 us (7%)
  other arithmetic  29 us (5%)
  blocking collectives  19.6 us (3%)
  between operations  15.8 us (3%)
  matrix products  11.4 us (2%)
    ppermute x67, waiting for transfers between devices, swap(): return lax.ppermute(value, GROUP, [(i, i ^ mask) for i in range(8)])  149 us
    pallas_call x7, Pallas kernels, kernel_call(): pl.pallas_call(body, out_shape=[jax.ShapeDtypeStruct(shape, kind) for sha...  104 us
    ppermute x67, starting transfers between devices, swap(): return lax.ppermute(value, GROUP, [(i, i ^ mask) for i in range(8)])  48.3 us
    all_gather x3, waiting for transfers between devices, planes(): return lax.all_gather(mine, 'z', axis=0, tiled=True)  34.3 us
    all_to_all x4, waiting for transfers between devices, row_exchange(): return lax.all_to_all(parts, ROW, split_axis=0, concat_axis=0, tiled=True)  29.6 us
    all_to_all x1, blocking collectives, to_heads(): got = lax.all_to_all(send, GROUP, split_axis=0, concat_axis=0, tiled=True)  19.6 us
    reduce_scatter x3, waiting for transfers between devices, home(): return lax.psum_scatter(full, 'z', scatter_dimension=0, tiled=True)  16.5 us
    unnamed x94, local copies, waits for them, and re-layouts  15.4 us
  transfers between devices with their start and end apart: 83, of which 43 were waited for; matrix products, arithmetic and copies ran while one was open for 13% of the time, Pallas kernels for 15%

profile of v4, /device:TPU:0, one launch (start us, length us, event | category | flops | bytes accessed | tf_op | source)
XLA Modules:
  0.0 561.1 jit_solution(6365217134632865459)
XLA Ops:
  10.7 19.6 %all_to_all.40 = bf16[8,128,512]{2,1,0:T(8,128)(2,1)S(1)} all-to-all(bf16[8,128,512]{2,1,0:T(8,128)(2,1)S(1)} %pad_maximum_fusion.1), channel_id=1, replica_groups=mesh['x'=2,'k'=2,'z'=4,'y'=2] {'x','k','y'}, dimensions={0} | all-to-all | bytes 2097152 | tf_op jit(solution)/shard_map/all_to_all | solution.py:446
  38.6 14.2 %all-to-all-done.1 = bf16[8,128,512]{2,1,0:T(8,128)(2,1)S(1)} async-done(((bf16[8,128,512]{2,1,0:T(8,128)(2,1)}), bf16[8,128,512]{2,1,0:T(8,128)(2,1)S(1)}, u32[]{:S(2)}, u32[]{:S(2)}) %all-to-all-start.1) | async-done | bytes 1048608 | tf_op jit(solution)/shard_map/all_to_all | solution.py:446
  64.9 14.3 %all-to-all-done.2 = bf16[4,2,128,512]{3,2,1,0:T(8,128)(2,1)S(1)} async-done(((bf16[4,2,128,512]{3,2,1,0:T(8,128)(2,1)}), bf16[4,2,128,512]{3,2,1,0:T(8,128)(2,1)S(1)}, u32[]{:S(2)}, u32[]{:S(2)}) %all-to-all-start.2) | async-done | bytes 1048608 | tf_op jit(solution)/shard_map/all_to_all | solution.py:93
  92.1 5.5 collective-permute-done.7
  97.6 10.1 %collective-permute-done.6 = bf16[128,2048]{1,0:T(8,128)(2,1)} collective-permute-done((bf16[128,2048]{1,0:T(8,128)(2,1)}, bf16[128,2048]{1,0:T(8,128)(2,1)}, u32[]{:S(2)}, u32[]{:S(2)}) %collective-permute-start.6) | collective-permute-done | bytes 524320 | tf_op jit(solution)/shard_map/ppermute | solution.py:29
  112.0 5.6 all-to-all-done.3
  134.8 9.4 %collective-permute-done.14.refs_13_ = bf16[128,2048]{1,0:T(8,128)(2,1)S(1)} collective-permute-done((bf16[128,2048]{1,0:T(8,128)(2,1)S(1)}, bf16[128,2048]{1,0:T(8,128)(2,1)S(1)}, u32[]{:S(2)}, u32[]{:S(2)}) %collective-permute-start.14) | collective-permute-done | bytes 524320 | tf_op jit(solution)/shard_map/ppermute | solution.py:29
  144.2 9.3 %collective-permute-done.13.refs_12_ = bf16[128,2048]{1,0:T(8,128)(2,1)S(1)} collective-permute-done((bf16[128,2048]{1,0:T(8,128)(2,1)S(1)}, bf16[128,2048]{1,0:T(8,128)(2,1)S(1)}, u32[]{:S(2)}, u32[]{:S(2)}) %collective-permute-start.13) | collective-permute-done | bytes 524320 | tf_op jit(solution)/shard_map/ppermute | solution.py:29
  154.1 15.0 %shard_map.237 = (bf16[256,1024]{1,0:T(8,128)(2,1)}, bf16[256,1024]{1,0:T(8,128)(2,1)}, bf16[512,1024]{1,0:T(8,128)(2,1)}, bf16[1024,1024]{1,0:T(8,128)(2,1)}, f32[512,1024]{1,0:T(8,128)}, /*index=5*/f32[1,1024]{1,0:T(1,128)}) custom-call(bf16[1024,2048]{1,0:T(8,128)(2,1)} %all-gather.6.cloned.1.call-done.w, ...), custom_call_target="tpu_custom_call" | custom-call | flops 5905580032 | bytes 14708736 | tf_op jit(solution)/shard_map/pallas_call | solution.py:156
  169.1 25.9 %all-gather.4.cloned.1.call-done.w.wgo = bf16[1024,2048]{1,0:T(8,128)(2,1)} async-done(((bf16[256,2048]{1,0:T(8,128)(2,1)}), bf16[1024,2048]{1,0:T(8,128)(2,1)}) %all-gather.4.cloned.1.call-update) | async-done | bytes 4194320 | tf_op jit(solution)/shard_map/all_gather | solution.py:470
  195.0 16.1 %shard_map.238 = (f32[512,1024]{1,0:T(8,128)}, bf16[512,1024]{1,0:T(8,128)(2,1)}, bf16[1024,2048]{1,0:T(8,128)(2,1)}) custom-call(bf16[1024,2048]{1,0:T(8,128)(2,1)} %all-gather.4.cloned.1.call-done.w.wgo, bf16[1024,2048]{1,0:T(8,128)(2,1)} %constant_dynamic-update-slice_fusion.1.x.x_in, f32[512,1024]{1,0:T(8,128)} %get-tuple-element.53.normed.refs_9_), custom_call_target="tpu_custom_call" | custom-call | flops 4294967296 | bytes 17825792 | tf_op jit(solution)/shard_map/pallas_call | solution.py:156
  220.2 5.2 collective-permute-done.23
  228.8 10.1 %collective-permute-done.24 = bf16[128,2048]{1,0:T(8,128)(2,1)S(1)} collective-permute-done((bf16[128,2048]{1,0:T(8,128)(2,1)S(1)}, bf16[128,2048]{1,0:T(8,128)(2,1)S(1)}, u32[]{:S(2)}, u32[]{:S(2)}) %collective-permute-start.24) | collective-permute-done | bytes 524320 | tf_op jit(solution)/shard_map/ppermute | solution.py:29
  246.0 12.3 %collective-permute-done.29.refs_5_ = bf16[128,2048]{1,0:T(8,128)(2,1)S(1)} collective-permute-done((bf16[128,2048]{1,0:T(8,128)(2,1)S(1)}, bf16[128,2048]{1,0:T(8,128)(2,1)S(1)}, u32[]{:S(2)}, u32[]{:S(2)}) %collective-permute-start.29) | collective-permute-done | bytes 524320 | tf_op jit(solution)/shard_map/ppermute | solution.py:29
  258.3 9.3 %collective-permute-done.28.refs_4_ = bf16[128,2048]{1,0:T(8,128)(2,1)S(1)} collective-permute-done((bf16[128,2048]{1,0:T(8,128)(2,1)S(1)}, bf16[128,2048]{1,0:T(8,128)(2,1)S(1)}, u32[]{:S(2)}, u32[]{:S(2)}) %collective-permute-start.28) | collective-permute-done | bytes 524320 | tf_op jit(solution)/shard_map/ppermute | solution.py:29
  268.1 8.4 %all-gather.8.cloned.1.call-done.w = bf16[1024,2048]{1,0:T(8,128)(2,1)} async-done(((bf16[256,2048]{1,0:T(8,128)(2,1)}), bf16[1024,2048]{1,0:T(8,128)(2,1)}) %all-gather.8.cloned.1.call-update) | async-done | bytes 4194320 | tf_op jit(solution)/shard_map/all_gather | solution.py:470
  276.5 18.6 %shard_map.239 = (bf16[512,1024]{1,0:T(8,128)(2,1)}, bf16[1024,2048]{1,0:T(8,128)(2,1)}, bf16[1024,2048]{1,0:T(8,128)(2,1)}) custom-call(bf16[1024,2048]{1,0:T(8,128)(2,1)} %all-gather.8.cloned.1.call-done.w, bf16[128,2048]{1,0:T(8,128)(2,1)} %copy-done.15, bf16[128,2048]{1,0:T(8,128)(2,1)} %collective-permute-done.25.refs_1_, ...), custom_call_target="tpu_custom_call" | custom-call | flops 10737418240 | bytes 22020096 | tf_op jit(solution)/shard_map/pallas_call | solution.py:156
  304.3 5.2 collective-permute-done.38
  312.9 10.1 %collective-permute-done.39 = bf16[128,2048]{1,0:T(8,128)(2,1)S(1)} collective-permute-done((bf16[128,2048]{1,0:T(8,128)(2,1)S(1)}, bf16[128,2048]{1,0:T(8,128)(2,1)S(1)}, u32[]{:S(2)}, u32[]{:S(2)}) %collective-permute-start.39) | collective-permute-done | bytes 524320 | tf_op jit(solution)/shard_map/ppermute | solution.py:29
  331.1 12.3 %collective-permute-done.44.refs_5_ = bf16[128,2048]{1,0:T(8,128)(2,1)S(1)} collective-permute-done((bf16[128,2048]{1,0:T(8,128)(2,1)S(1)}, bf16[128,2048]{1,0:T(8,128)(2,1)S(1)}, u32[]{:S(2)}, u32[]{:S(2)}) %collective-permute-start.44) | collective-permute-done | bytes 524320 | tf_op jit(solution)/shard_map/ppermute | solution.py:29
  343.5 9.3 %collective-permute-done.43.refs_4_ = bf16[128,2048]{1,0:T(8,128)(2,1)S(1)} collective-permute-done((bf16[128,2048]{1,0:T(8,128)(2,1)S(1)}, bf16[128,2048]{1,0:T(8,128)(2,1)S(1)}, u32[]{:S(2)}, u32[]{:S(2)}) %collective-permute-start.43) | collective-permute-done | bytes 524320 | tf_op jit(solution)/shard_map/ppermute | solution.py:29
  356.2 15.1 %shard_map.240 = (bf16[512,1024]{1,0:T(8,128)(2,1)}, bf16[512,1024]{1,0:T(8,128)(2,1)}, bf16[1024,2048]{1,0:T(8,128)(2,1)}) custom-call(bf16[1024,2048]{1,0:T(8,128)(2,1)} %all-gather.4.cloned.1.call-done.w.wgo, bf16[1024,2048]{1,0:T(8,128)(2,1)} %constant_dynamic-update-slice_fusion.1.x.x_in, bf16[128,2048]{1,0:T(8,128)(2,1)} %copy-done.16, ...), custom_call_target="tpu_custom_call" | custom-call | flops 6442450944 | bytes 24121344 | tf_op jit(solution)/shard_map/pallas_call | solution.py:156
  378.2 18.0 %shard_map.241 = (bf16[1024,1024]{1,0:T(8,128)(2,1)}, bf16[4,8,128,512]{3,2,1,0:T(8,128)(2,1)}) custom-call(bf16[256,1024]{1,0:T(8,128)(2,1)} %get-tuple-element.57.q, bf16[256,1024]{1,0:T(8,128)(2,1)} %get-tuple-element.58.k, bf16[512,1024]{1,0:T(8,128)(2,1)} %get-tuple-element.59.v, bf16[1024,1024]{1,0:T(8,128)(2,1)} %get-tuple-element.60.weights, ...), custom_call_target="tpu_custom_call" | custom-call | flops 7516192768 | bytes 15753216 | tf_op jit(solution)/shard_map/pallas_call | solution.py:156
  397.3 13.9 %shard_map.242 = bf16[1024,2048]{1,0:T(8,128)(2,1)} custom-call(bf16[1024,1024]{1,0:T(8,128)(2,1)} %get-tuple-element.65.packed, bf16[1024,2048]{1,0:T(8,128)(2,1)} %all-gather.6.cloned.1.call-done.w, bf16[512,1024]{1,0:T(8,128)(2,1)} %get-tuple-element.69.ggate, bf16[1024,2048]{1,0:T(8,128)(2,1)} %all-gather.4.cloned.1.call-done.w.wgo), custom_call_target="tpu_custom_call" | custom-call | flops 6442450944 | bytes 15728640 | tf_op jit(solution)/shard_map/pallas_call | solution.py:156
  411.2 7.6 %shard_map.243 = bf16[1024,2048]{1,0:T(8,128)(2,1)} custom-call(bf16[1024,2048]{1,0:T(8,128)(2,1)} %all-gather.8.cloned.1.call-done.w, bf16[512,1024]{1,0:T(8,128)(2,1)} %get-tuple-element.71.act), custom_call_target="tpu_custom_call" | custom-call | flops 2147483648 | bytes 9437184 | tf_op jit(solution)/shard_map/pallas_call | solution.py:156
  440.7 4.3 collective-permute-done.53
  450.1 4.3 collective-permute-done.62
  454.4 5.4 collective-permute-done.59
  484.5 9.8 %all-to-all-done.5 = bf16[4,2,128,512]{3,2,1,0:T(8,128)(2,1)S(1)} async-done(((bf16[4,2,128,512]{3,2,1,0:T(8,128)(2,1)}), bf16[4,2,128,512]{3,2,1,0:T(8,128)(2,1)S(1)}, u32[]{:S(2)}, u32[]{:S(2)}) %all-to-all-start.5) | async-done | bytes 1048608 | tf_op jit(solution)/shard_map/all_to_all | solution.py:93
  499.4 3.8 all-to-all-start.6
  515.2 16.5 %reduce-scatter.6.cloned.1.call-done = bf16[1,8,128,512]{3,2,1,0:T(8,128)(2,1)} async-done(((bf16[4,8,128,512]{3,2,1,0:T(8,128)(2,1)}), bf16[1,8,128,512]{3,2,1,0:T(8,128)(2,1)}) %reduce-scatter.6.cloned.1.call-update) | async-done | bytes 1048592 | tf_op jit(solution)/shard_map/reduce_scatter | solution.py:577
  539.1 10.8 %all-to-all-done.7 = bf16[8,128,512]{2,1,0:T(8,128)(2,1)S(1)} async-done(((bf16[8,128,512]{2,1,0:T(8,128)(2,1)}), bf16[8,128,512]{2,1,0:T(8,128)(2,1)S(1)}, u32[]{:S(2)}, u32[]{:S(2)}) %all-to-all-start.7) | async-done | bytes 1048608 | tf_op jit(solution)/shard_map/all_to_all | solution.py:664
  (369 shorter events, 190.1 us)
Async XLA Ops:
  7.2 146.9 %all-gather.6.cloned.1.call-start = ((), (), s32[]{:S(2)}) async-start(), calls=%async_computation.12 | async-start | bytes 5242880 | tf_op jit(solution)/shard_map/all_gather | solution.py:470
  38.3 156.6 %all-gather.4.cloned.1.call-start = ((), (), s32[]{:S(2)}) async-start(), calls=%async_computation.11 | async-start | bytes 5242880 | tf_op jit(solution)/shard_map/all_gather | solution.py:470
  81.7 26.1 %collective-permute-start.6 = (bf16[128,2048]{1,0:T(8,128)(2,1)}, bf16[128,2048]{1,0:T(8,128)(2,1)}, u32[]{:S(2)}, u32[]{:S(2)}) collective-permute-start(bf16[128,2048]{1,0:T(8,128)(2,1)} %get-tuple-element.90), channel_id=1, source_target_pairs={{0,16},{1,17},{8,24},{9,25},{16,0},{17,1},{24,8},{25,9},{2,18},{3,... | collective-permute-start | bytes 1572872 | tf_op jit(solution)/shard_map/ppermute | solution.py:29
  83.4 24.4 %collective-permute-start.3 = (bf16[128,2048]{1,0:T(8,128)(2,1)}, bf16[128,2048]{1,0:T(8,128)(2,1)}, u32[]{:S(2)}, u32[]{:S(2)}) collective-permute-start(bf16[128,2048]{1,0:T(8,128)(2,1)} %get-tuple-element.90), channel_id=1, source_target_pairs={{0,1},{1,0},{8,9},{9,8},{16,17},{17,16},{24,25},{25,24},{2,3},{3,2... | collective-permute-start | bytes 1572872 | tf_op jit(solution)/shard_map/ppermute | solution.py:29
  86.3 31.3 %all-to-all-start.3 = ((bf16[4,2,128,512]{3,2,1,0:T(8,128)(2,1)}), bf16[4,2,128,512]{3,2,1,0:T(8,128)(2,1)S(1)}, u32[]{:S(2)}, u32[]{:S(2)}) async-start(bf16[4,2,128,512]{3,2,1,0:T(8,128)(2,1)} %pad_maximum_fusion.3), calls=%async_computation.3 | async-start | bytes 2097152 | tf_op jit(solution)/shard_map/all_to_all | solution.py:93
  89.8 186.6 %all-gather.8.cloned.1.call-start = ((), (), s32[]{:S(2)}) async-start(), calls=%async_computation.13 | async-start | bytes 5242880 | tf_op jit(solution)/shard_map/all_gather | solution.py:470
  89.9 20.3 %collective-permute-start.4 = (bf16[128,2048]{1,0:T(8,128)(2,1)}, bf16[128,2048]{1,0:T(8,128)(2,1)}, u32[]{:S(2)}, u32[]{:S(2)}) collective-permute-start(bf16[128,2048]{1,0:T(8,128)(2,1)} %get-tuple-element.90), channel_id=1, source_target_pairs={{0,8},{1,9},{8,0},{9,1},{16,24},{17,25},{24,16},{25,17},{2,10},{3,... | collective-permute-start | bytes 1572872 | tf_op jit(solution)/shard_map/ppermute | solution.py:29
  97.6 28.9 %collective-permute-start.9 = (bf16[128,2048]{1,0:T(8,128)(2,1)}, bf16[128,2048]{1,0:T(8,128)(2,1)}, u32[]{:S(2)}, u32[]{:S(2)}) collective-permute-start(bf16[128,2048]{1,0:T(8,128)(2,1)} %collective-permute-done.7), channel_id=1, source_target_pairs={{0,8},{1,9},{8,0},{9,1},{16,24},{17,25},{24,16},{25,17},{2,10},{3,... | collective-permute-start | bytes 1572872 | tf_op jit(solution)/shard_map/ppermute | solution.py:29
  130.3 23.3 %collective-permute-start.13 = (bf16[128,2048]{1,0:T(8,128)(2,1)S(1)}, bf16[128,2048]{1,0:T(8,128)(2,1)S(1)}, u32[]{:S(2)}, u32[]{:S(2)}) collective-permute-start(bf16[128,2048]{1,0:T(8,128)(2,1)S(1)} %bitcast.122), channel_id=1, source_target_pairs={{0,16},{1,17},{8,24},{9,25},{16,0},{17,1},{24,8},{25,9},{2,18},{3,... | collective-permute-start | bytes 1572872 | tf_op jit(solution)/shard_map/ppermute | solution.py:29
  131.6 22.0 %collective-permute-start.10 = (bf16[128,2048]{1,0:T(8,128)(2,1)S(1)}, bf16[128,2048]{1,0:T(8,128)(2,1)}, u32[]{:S(2)}, u32[]{:S(2)}) collective-permute-start(bf16[128,2048]{1,0:T(8,128)(2,1)S(1)} %bitcast.123), channel_id=1, source_target_pairs={{0,1},{1,0},{8,9},{9,8},{16,17},{17,16},{24,25},{25,24},{2,3},{3,2... | collective-permute-start | bytes 1572872 | tf_op jit(solution)/shard_map/ppermute | solution.py:29
  134.2 237.2 %reduce-scatter.4.cloned.1.call-start = ((), (), s32[]{:S(2)}) async-start(), calls=%async_computation.14 | async-start | bytes 5242880 | tf_op jit(solution)/shard_map/reduce_scatter | solution.py:577
  134.7 34.3 %collective-permute-start.11 = (bf16[128,2048]{1,0:T(8,128)(2,1)S(1)}, bf16[128,2048]{1,0:T(8,128)(2,1)S(1)}, u32[]{:S(2)}, u32[]{:S(2)}) collective-permute-start(bf16[128,2048]{1,0:T(8,128)(2,1)S(1)} %bitcast.124), channel_id=1, source_target_pairs={{0,8},{1,9},{8,0},{9,1},{16,24},{17,25},{24,16},{25,17},{2,10},{3,... | collective-permute-start | bytes 1572872 | tf_op jit(solution)/shard_map/ppermute | solution.py:29
  144.2 24.8 %collective-permute-start.16 = (bf16[128,2048]{1,0:T(8,128)(2,1)S(1)}, bf16[128,2048]{1,0:T(8,128)(2,1)S(1)}, u32[]{:S(2)}, u32[]{:S(2)}) collective-permute-start(bf16[128,2048]{1,0:T(8,128)(2,1)S(1)} %collective-permute-done.14.refs_13_), channel_id=1, source_target_pairs={{0,8},{1,9},{8,0},{9,1},{16,24},{17,25},{24,16},{25,17},{2,10},{3,... | collective-permute-start | bytes 1572872 | tf_op jit(solution)/shard_map/ppermute | solution.py:29
  243.9 23.6 %collective-permute-start.28 = (bf16[128,2048]{1,0:T(8,128)(2,1)S(1)}, bf16[128,2048]{1,0:T(8,128)(2,1)S(1)}, u32[]{:S(2)}, u32[]{:S(2)}) collective-permute-start(bf16[128,2048]{1,0:T(8,128)(2,1)S(1)} %add_convert_fusion.4.refs_0_), channel_id=1, source_target_pairs={{0,16},{1,17},{8,24},{9,25},{16,0},{17,1},{24,8},{25,9},{2,18},{3,... | collective-permute-start | bytes 1572872 | tf_op jit(solution)/shard_map/ppermute | solution.py:29
  245.4 22.2 %collective-permute-start.25 = (bf16[128,2048]{1,0:T(8,128)(2,1)S(1)}, bf16[128,2048]{1,0:T(8,128)(2,1)}, u32[]{:S(2)}, u32[]{:S(2)}) collective-permute-start(bf16[128,2048]{1,0:T(8,128)(2,1)S(1)} %add_convert_fusion.4.refs_0_), channel_id=1, source_target_pairs={{0,1},{1,0},{8,9},{9,8},{16,17},{17,16},{24,25},{25,24},{2,3},{3,2... | collective-permute-start | bytes 1572872 | tf_op jit(solution)/shard_map/ppermute | solution.py:29
  246.0 30.5 %collective-permute-start.26 = (bf16[128,2048]{1,0:T(8,128)(2,1)S(1)}, bf16[128,2048]{1,0:T(8,128)(2,1)}, u32[]{:S(2)}, u32[]{:S(2)}) collective-permute-start(bf16[128,2048]{1,0:T(8,128)(2,1)S(1)} %add_convert_fusion.4.refs_0_), channel_id=1, source_target_pairs={{0,8},{1,9},{8,0},{9,1},{16,24},{17,25},{24,16},{25,17},{2,10},{3,... | collective-permute-start | bytes 1572872 | tf_op jit(solution)/shard_map/ppermute | solution.py:29
  258.3 18.2 %collective-permute-start.31 = (bf16[128,2048]{1,0:T(8,128)(2,1)S(1)}, bf16[128,2048]{1,0:T(8,128)(2,1)}, u32[]{:S(2)}, u32[]{:S(2)}) collective-permute-start(bf16[128,2048]{1,0:T(8,128)(2,1)S(1)} %collective-permute-done.29.refs_5_), channel_id=1, source_target_pairs={{0,8},{1,9},{8,0},{9,1},{16,24},{17,25},{24,16},{25,17},{2,10},{3,... | collective-permute-start | bytes 1572872 | tf_op jit(solution)/shard_map/ppermute | solution.py:29
  295.1 201.1 %reduce-scatter.8.cloned.1.call-start = ((), (), s32[]{:S(2)}) async-start(), calls=%async_computation.16 | async-start | bytes 5242880 | tf_op jit(solution)/shard_map/reduce_scatter | solution.py:577
  329.1 23.6 %collective-permute-start.43 = (bf16[128,2048]{1,0:T(8,128)(2,1)S(1)}, bf16[128,2048]{1,0:T(8,128)(2,1)S(1)}, u32[]{:S(2)}, u32[]{:S(2)}) collective-permute-start(bf16[128,2048]{1,0:T(8,128)(2,1)S(1)} %get-tuple-element.84.refs_0_), channel_id=1, source_target_pairs={{0,16},{1,17},{8,24},{9,25},{16,0},{17,1},{24,8},{25,9},{2,18},{3,... | collective-permute-start | bytes 1572872 | tf_op jit(solution)/shard_map/ppermute | solution.py:29
  330.6 22.2 %collective-permute-start.40 = (bf16[128,2048]{1,0:T(8,128)(2,1)S(1)}, bf16[128,2048]{1,0:T(8,128)(2,1)S(1)}, u32[]{:S(2)}, u32[]{:S(2)}) collective-permute-start(bf16[128,2048]{1,0:T(8,128)(2,1)S(1)} %get-tuple-element.84.refs_0_), channel_id=1, source_target_pairs={{0,1},{1,0},{8,9},{9,8},{16,17},{17,16},{24,25},{25,24},{2,3},{3,2... | collective-permute-start | bytes 1572872 | tf_op jit(solution)/shard_map/ppermute | solution.py:29
  331.1 22.1 %collective-permute-start.41 = (bf16[128,2048]{1,0:T(8,128)(2,1)S(1)}, bf16[128,2048]{1,0:T(8,128)(2,1)S(1)}, u32[]{:S(2)}, u32[]{:S(2)}) collective-permute-start(bf16[128,2048]{1,0:T(8,128)(2,1)S(1)} %get-tuple-element.84.refs_0_), channel_id=1, source_target_pairs={{0,8},{1,9},{8,0},{9,1},{16,24},{17,25},{24,16},{25,17},{2,10},{3,... | collective-permute-start | bytes 1572872 | tf_op jit(solution)/shard_map/ppermute | solution.py:29
  374.7 21.5 %all-to-all-start.4 = ((bf16[4,2,128,512]{3,2,1,0:T(8,128)(2,1)}), bf16[4,2,128,512]{3,2,1,0:T(8,128)(2,1)S(1)}, u32[]{:S(2)}, u32[]{:S(2)}) async-start(bf16[4,2,128,512]{3,2,1,0:T(8,128)(2,1)} %maximum_bitcast_fusion), calls=%async_computation.5 | async-start | bytes 2097152 | tf_op jit(solution)/shard_map/all_to_all | solution.py:93
  378.2 153.5 %reduce-scatter.6.cloned.1.call-start = ((), (), s32[]{:S(2)}) async-start(), calls=%async_computation.15 | async-start | bytes 5242880 | tf_op jit(solution)/shard_map/reduce_scatter | solution.py:577
  422.5 27.0 %collective-permute-start.55 = (bf16[128,2048]{1,0:T(8,128)(2,1)S(1)}, bf16[128,2048]{1,0:T(8,128)(2,1)S(1)}, u32[]{:S(2)}, u32[]{:S(2)}) collective-permute-start(bf16[128,2048]{1,0:T(8,128)(2,1)S(1)} %get-tuple-element.98), channel_id=1, source_target_pairs={{0,8},{1,9},{8,0},{9,1},{16,24},{17,25},{24,16},{25,17},{2,10},{3,... | collective-permute-start | bytes 1572872 | tf_op jit(solution)/shard_map/ppermute | solution.py:29
  425.3 36.2 %collective-permute-start.47 = (bf16[128,2048]{1,0:T(8,128)(2,1)}, bf16[128,2048]{1,0:T(8,128)(2,1)}, u32[]{:S(2)}, u32[]{:S(2)}) collective-permute-start(bf16[128,2048]{1,0:T(8,128)(2,1)} %get-tuple-element.91), channel_id=1, source_target_pairs={{0,8},{1,9},{8,0},{9,1},{16,24},{17,25},{24,16},{25,17},{2,10},{3,... | collective-permute-start | bytes 1572872 | tf_op jit(solution)/shard_map/ppermute | solution.py:29
  449.6 19.1 %collective-permute-start.51 = (bf16[128,2048]{1,0:T(8,128)(2,1)}, bf16[128,2048]{1,0:T(8,128)(2,1)}, u32[]{:S(2)}, u32[]{:S(2)}) collective-permute-start(bf16[128,2048]{1,0:T(8,128)(2,1)} %pad_maximum_fusion.9), channel_id=1, source_target_pairs={{0,16},{1,17},{8,24},{9,25},{16,0},{17,1},{24,8},{25,9},{2,18},{3,... | collective-permute-start | bytes 1572872 | tf_op jit(solution)/shard_map/ppermute | solution.py:29
  475.8 18.4 %all-to-all-start.5 = ((bf16[4,2,128,512]{3,2,1,0:T(8,128)(2,1)}), bf16[4,2,128,512]{3,2,1,0:T(8,128)(2,1)S(1)}, u32[]{:S(2)}, u32[]{:S(2)}) async-start(bf16[4,2,128,512]{3,2,1,0:T(8,128)(2,1)} %maximum_bitcast_fusion.1), calls=%async_computation.6 | async-start | bytes 2097152 | tf_op jit(solution)/shard_map/all_to_all | solution.py:93
  480.9 23.4 %collective-permute-start.65 = (f32[4,2048]{1,0:T(4,128)S(1)}, f32[4,2048]{1,0:T(4,128)S(1)}, u32[]{:S(2)}, u32[]{:S(2)}) collective-permute-start(f32[4,2048]{1,0:T(4,128)S(1)} %fusion.61), channel_id=1, source_target_pairs={{0,16},{1,17},{8,24},{9,25},{16,0},{17,1},{24,8},{25,9},{2,18},{3,... | collective-permute-start | bytes 98312 | tf_op jit(solution)/shard_map/ppermute | solution.py:29
  482.8 21.5 %collective-permute-start.66 = (f32[4,2048]{1,0:T(4,128)S(1)}, f32[4,2048]{1,0:T(4,128)S(1)}, u32[]{:S(2)}, u32[]{:S(2)}) collective-permute-start(f32[4,2048]{1,0:T(4,128)S(1)} %fusion.61), channel_id=1, source_target_pairs={{0,17},{1,16},{8,25},{9,24},{16,1},{17,0},{24,9},{25,8},{2,19},{3,... | collective-permute-start | bytes 98312 | tf_op jit(solution)/shard_map/ppermute | solution.py:29
  483.8 20.5 %collective-permute-start.64 = (f32[4,2048]{1,0:T(4,128)S(1)}, f32[4,2048]{1,0:T(4,128)S(1)}, u32[]{:S(2)}, u32[]{:S(2)}) collective-permute-start(f32[4,2048]{1,0:T(4,128)S(1)} %fusion.61), channel_id=1, source_target_pairs={{0,1},{1,0},{8,9},{9,8},{16,17},{17,16},{24,25},{25,24},{2,3},{3,2... | collective-permute-start | bytes 98312 | tf_op jit(solution)/shard_map/ppermute | solution.py:29
  499.4 32.3 %all-to-all-start.6 = ((bf16[8,128,512]{2,1,0:T(8,128)(2,1)}), bf16[8,128,512]{2,1,0:T(8,128)(2,1)S(1)}, u32[]{:S(2)}, u32[]{:S(2)}) async-start(bf16[8,128,512]{2,1,0:T(8,128)(2,1)} %bitcast.41), calls=%async_computation.9 | async-start | bytes 2097152 | tf_op jit(solution)/shard_map/all_to_all | solution.py:655
  531.7 18.2 %all-to-all-start.7 = ((bf16[8,128,512]{2,1,0:T(8,128)(2,1)}), bf16[8,128,512]{2,1,0:T(8,128)(2,1)S(1)}, u32[]{:S(2)}, u32[]{:S(2)}) async-start(bf16[8,128,512]{2,1,0:T(8,128)(2,1)} %bitcast.127), calls=%async_computation.10 | async-start | bytes 2097152 | tf_op jit(solution)/shard_map/all_to_all | solution.py:664
  (90 other events, 1142.1 us)
Sparse Core Ops, SparseCore 0:
  32.5 81.0 all-gather.5
  115.7 79.2 all-gather.3
  197.1 79.2 all-gather.7
  295.3 75.2 reduce-scatter.3
  372.8 77.2 reduce-scatter.7
  452.3 79.3 reduce-scatter.5

commit v5 on v4

--- a/solution.py
+++ b/solution.py
@@ -165,22 +165,13 @@
     )(*args)
 
 
-def unpack(source, first, second, depth):
-    half = source.shape[0] // (2 * depth)
+def unpack(source, targets, depth):
+    height = source.shape[0] // (len(targets) * depth)
     for i in range(depth):
-        at = 2 * i * half
-        if first is not None:
-            first[i * half : (i + 1) * half, :] = source[at : at + half, :]
-        if second is not None:
-            second[i * half : (i + 1) * half, :] = source[at + half : at + 2 * half, :]
-
-
-def pack(target, columns, first, second, depth):
-    half = first.shape[0] // depth
-    for i in range(depth):
-        at = 2 * i * half
-        target[at : at + half, columns] = first[i * half : (i + 1) * half]
-        target[at + half : at + 2 * half, columns] = second[i * half : (i + 1) * half]
+        for j, target in enumerate(targets):
+            at = (i * len(targets) + j) * height
+            if target is not None:
+                target[i * height : (i + 1) * height, :] = source[at : at + height, :]
 
 
 def decayed(raw, spot, segs, grow, fall, rows):
@@ -188,45 +179,45 @@
     return jnp.where(inside, raw * (grow[rows, :] * fall[...]), 0.0).astype(BF16)
 
 
-def retention_forward(depth, w, x, pc, pr, sc, sr, grow, fall, q, k, v, weights, normed, inv):
+def retention_scores(depth, w, x, pc, pr, sc, sr, grow, fall, q, k, weights):
     seq = x.shape[0]
     part = q.shape[0] // depth
-    width = v.shape[0] // depth
-    group = 2 * part + width
 
     def project(at):
         out = dot(w[...], x[at, :], ((1,), (1,))).astype(BF16)
         for i in range(depth):
-            z = i * group
+            z = 2 * i * part
             q[i * part : (i + 1) * part, at] = out[z : z + part]
             k[i * part : (i + 1) * part, at] = out[z + part : z + 2 * part]
-            v[i * width : (i + 1) * width, at] = out[z + 2 * part : z + group]
 
     def attend(at):
         raw = dot(q[:, at], k[...], ((0,), (0,)))
-        low = decayed(raw, (pc, pr), (sc, sr), grow, fall, at)
-        weights[at, :] = low
-        kept = dot(v[...], low, ((1,), (1,)))
+        weights[at, :] = decayed(raw, (pc, pr), (sc, sr), grow, fall, at)
+
+    spans(seq, TILE, project)
+    spans(seq, TILE, attend)
+
+
+def gated_forward(depth, w, x, weights, gate, hidden, out, v, normed, inv, wv, wg, wo):
+    unpack(w, (wv, wg, wo), depth)
+
+    def project(at):
+        v[:, at] = dot(wv[...], x[at, :], ((1,), (1,))).astype(BF16)
+
+    def step(at):
+        kept = dot(v[...], weights[at, :], ((1,), (1,)))
         centered = kept - jnp.mean(kept, axis=0, keepdims=True)
         scale = lax.rsqrt(jnp.mean(centered * centered, axis=0, keepdims=True) + EPS_GROUP)
-        normed[:, at] = centered * scale
+        full = centered * scale
+        normed[:, at] = full
         inv[:, at] = scale
-
-    spans(seq, TILE, project)
-    spans(seq, TILE, attend)
-
-
-def gated_forward(depth, w, x, normed, gate, hidden, out, wg, wo):
-    unpack(w, wg, wo, depth)
-
-    def step(at):
         g = dot(wg[...], x[at, :], ((1,), (1,)))
         gate[:, at] = g
-        low = normed[:, at].astype(BF16).astype(F32)
-        h = (g * jax.nn.sigmoid(g) * low).astype(BF16)
+        h = (g * jax.nn.sigmoid(g) * full.astype(BF16).astype(F32)).astype(BF16)
         hidden[:, at] = h
         out[at, :] = dot(h, wo[...], ((0,), (0,))).astype(BF16)
 
+    spans(x.shape[0], TILE, project)
     spans(x.shape[0], TILE, step)
 
 
@@ -249,12 +240,13 @@
         ]
 
     def kind(self, source, target, which, depth):
-        half = (source if which[0] == "from" else target).shape[0] // (2 * depth)
+        way, index, kinds = which
+        height = (source if way == "from" else target).shape[0] // (kinds * depth)
         moved = []
         for i in range(depth):
-            mixed = pl.ds((2 * i + which[1]) * half, half)
-            plain = pl.ds(i * half, half)
-            if which[0] == "from":
+            mixed = pl.ds((kinds * i + index) * height, height)
+            plain = pl.ds(i * height, height)
+            if way == "from":
                 moved.append(self.start(source.at[mixed], target.at[plain]))
             else:
                 moved.append(self.start(source.at[plain], target.at[mixed]))
@@ -272,7 +264,7 @@
     wu, wd, x, cot, act, gp, turned, back, gu, gd, semaphores = refs[19:]
     move = Mover(semaphores)
     seq, rows = x.shape[0], x_blocks[0].shape[0]
-    weights = move.kind(w, wu, ("from", 0), depth) + move.kind(w, wd, ("from", 1), depth)
+    weights = move.kind(w, wu, ("from", 0, 2), depth) + move.kind(w, wd, ("from", 1, 2), depth)
     x_copies, cot_copies = move.rows(x_blocks, x), move.rows(cot_blocks, cot)
     wait(weights)
     for tile in range(seq // TALL):
@@ -296,9 +288,9 @@
         gd[:, at] = dot(act[...], cot[:, at], ((1,), (0,))).astype(BF16)
 
     spans(x.shape[1], WIDE, up_step)
-    sent += move.kind(gu, grads_out, ("to", 0), depth)
+    sent += move.kind(gu, grads_out, ("to", 0, 2), depth)
     spans(x.shape[1], WIDE, down_step)
-    sent += move.kind(gd, grads_out, ("to", 1), depth)
+    sent += move.kind(gd, grads_out, ("to", 1, 2), depth)
     for tile in range(x.shape[1] // WIDE):
         at = pl.ds(tile * WIDE, WIDE)
         back[:, at] = dot(turned[...], wu[:, at], ((1,), (0,))).astype(BF16)
@@ -307,7 +299,7 @@
 
 
 def down_forward(depth, w, act, out, wd):
-    unpack(w, None, wd, depth)
+    unpack(w, (None, wd), depth)
 
     def step(at):
         out[at, :] = dot(act[:, at], wd[...], ((0,), (0,))).astype(BF16)
@@ -321,7 +313,7 @@
     wo, x, mid, gate, normed, inv, hidden, ggate, gret, gg, go, semaphores = refs[15:]
     move = Mover(semaphores)
     seq, rows = x.shape[0], mid_blocks[0].shape[0]
-    first = move.kind(w, wo, ("from", 1), depth)
+    first = move.kind(w, wo, ("from", 2, 3), depth)
     mid_copies = move.rows(mid_blocks[:4], mid.at[pl.ds(0, 4 * rows)])
     first += [move.start(inv_in, inv), move.start(gate_in, gate), move.start(normed_in, normed)]
     mid_copies += move.rows(mid_blocks[4:], mid.at[pl.ds(4 * rows, seq - 4 * rows)])
@@ -350,9 +342,9 @@
         go[:, at] = dot(hidden[...], mid[:, at], ((1,), (0,))).astype(BF16)
 
     spans(x.shape[1], WIDE, gate_step)
-    sent += move.kind(gg, grads_out, ("to", 0), depth)
+    sent += move.kind(gg, grads_out, ("to", 0, 2), depth)
     spans(x.shape[1], WIDE, out_step)
-    sent += move.kind(go, grads_out, ("to", 1), depth)
+    sent += move.kind(go, grads_out, ("to", 1, 2), depth)
     wait(sent)
 
 
@@ -362,29 +354,35 @@
     seq = x.shape[0]
     part = q.shape[0] // depth
     width = v.shape[0] // depth
-    group = 2 * part + width
-
-    def place(value, at, offset, height):
+    pairs = 2 * part * depth
+
+    def place(value, at, offset):
         for i in range(depth):
-            z = i * group + offset
-            packed[z : z + height, at] = value[i * height : (i + 1) * height]
+            z = 2 * i * part + offset
+            packed[z : z + part, at] = value[i * part : (i + 1) * part]
 
     def query_step(at):
         raw = dot(gret[:, at], v[...], ((0,), (0,)))
         low = decayed(raw, (pc, pr), (sc, sr), grow, fall, at)
         scores[at, :] = low
-        place(dot(k[...], low, ((1,), (1,))).astype(BF16), at, 0, part)
+        place(dot(k[...], low, ((1,), (1,))).astype(BF16), at, 0)
 
     def key_step(at):
-        place(dot(q[...], scores[:, at], ((1,), (0,))).astype(BF16), at, part, part)
-        place(dot(gret[...], weights[:, at], ((1,), (0,))).astype(BF16), at, 2 * part, width)
+        place(dot(q[...], scores[:, at], ((1,), (0,))).astype(BF16), at, part)
+        packed[pairs:, at] = dot(gret[...], weights[:, at], ((1,), (0,))).astype(BF16)
 
     spans(seq, TILE, query_step)
     spans(seq, TILE, key_step)
     if len(grads.shape) == 2:
 
         def grad_step(at):
-            grads[:, at] = dot(packed[...], x[:, at], ((1,), (0,))).astype(BF16)
+            full = dot(packed[...], x[:, at], ((1,), (0,))).astype(BF16)
+            for i in range(depth):
+                z = i * (2 * part + width)
+                grads[z : z + 2 * part, at] = full[2 * i * part : 2 * (i + 1) * part]
+                grads[z + 2 * part : z + 2 * part + width, at] = full[
+                    pairs + i * width : pairs + (i + 1) * width
+                ]
 
         spans(x.shape[1], WIDE, grad_step)
         return
@@ -394,17 +392,23 @@
         at = pl.ds(pl.multiple_of(row * columns, columns), columns)
         full = dot(packed[...], x[:, at], ((1,), (0,))).astype(BF16)
         for i in range(depth):
-            grads[i // 2, 2 * row + i % 2, :, :] = full[i * group : (i + 1) * group]
+            there = (i // 2, 2 * row + i % 2)
+            grads[(*there, slice(0, 2 * part))] = full[2 * i * part : 2 * (i + 1) * part]
+            grads[(*there, slice(2 * part, 2 * part + width))] = full[
+                pairs + i * width : pairs + (i + 1) * width
+            ]
         return carry
 
     lax.fori_loop(0, 4, home_step, 0)
 
 
-def input_backward(depth, packed, w, ggate, wgo, out, wg):
-    unpack(wgo, wg, None, depth)
+def input_backward(depth, packed, w, ggate, vgo, out, wv, wg):
+    unpack(vgo, (wv, wg, None), depth)
+    pairs = w.shape[0]
 
     def step(at):
-        total = dot(packed[:, at], w[...], ((0,), (0,)))
+        total = dot(packed[:pairs, at], w[...], ((0,), (0,)))
+        total = total + dot(packed[pairs:, at], wv[...], ((0,), (0,)))
         out[at, :] = (total + dot(ggate[:, at], wg[...], ((0,), (0,)))).astype(BF16)
 
     spans(packed.shape[1], TILE, step)
@@ -469,23 +473,22 @@
     def planes(mine):
         return lax.all_gather(mine, "z", axis=0, tiled=True)
 
-    got_qkv = to_heads(
-        jnp.concatenate(
-            [by_head(w_query, order_q), by_head(w_key, order_q), by_head(w_value, order_v)], axis=1
-        )
-    )
-    mine_qkv = regroup(got_qkv, kq, kq, kv)
-    all_qkv = planes(mine_qkv)
-    send_go = jnp.concatenate(
+    got_qk = to_heads(
+        jnp.concatenate([by_head(w_query, order_q), by_head(w_key, order_q)], axis=1)
+    )
+    mine_qk = regroup(got_qk, kq, kq)
+    all_qk = planes(mine_qk)
+    send_vgo = jnp.concatenate(
         [
+            by_head(w_value, order_v),
             by_head(w_gate, order_v),
             dot(order_v, w_out, ((0,), (0,))).astype(BF16).reshape(HEADS, -1, part),
         ],
         axis=1,
     )
-    got_go = to_heads(after(send_go, mine_qkv))
-    mine_go = regroup(got_go, kv, kv)
-    all_go = planes(mine_go)
+    got_vgo = to_heads(after(send_vgo, mine_qk))
+    mine_vgo = regroup(got_vgo, kv, kv, kv)
+    all_vgo = planes(mine_vgo)
 
     small = jnp.concatenate(
         [
@@ -496,13 +499,13 @@
             segments.astype(F32),
         ]
     )
-    small = row_gather(after(small, mine_qkv))
+    small = row_gather(after(small, mine_qk))
     params = small[:, : 4 * part].reshape(4, 4, part).transpose(1, 0, 2).reshape(4, width)
     segs = small[:, 4 * part :].astype(jnp.int32).reshape(depth, 8, tokens)
-    block_in, cotangent = after(block_in, got_go), after(cotangent, got_go)
+    block_in, cotangent = after(block_in, got_vgo), after(cotangent, got_vgo)
     stream_low, cot_own = to_wide(block_in, cotangent)
     mine_up, mine_down = to_wide(after(w_up, stream_low).T, after(w_down, stream_low))
-    all_ud = planes(after(jnp.concatenate([mine_up, mine_down], axis=0), mine_go))
+    all_ud = planes(after(jnp.concatenate([mine_up, mine_down], axis=0), mine_vgo))
     stream = stream_low.astype(F32)
     hat_one, inv_one, norm_one = layernorm(stream, params[0], params[1])
     x_one = jnp.concatenate(group_gather(norm_one), axis=0)
@@ -524,32 +527,28 @@
     x_one = after(x_one, mine_up, mine_down)
     keys_all, values_all = kq * 2 * depth, kv * 2 * depth
     square = 2 * seq * seq
-    query, keys, values, weights, normed, inv_group = kernel_call(
-        functools.partial(retention_forward, blocks),
-        [
-            ((keys_all, seq), BF16),
-            ((keys_all, seq), BF16),
-            ((values_all, seq), BF16),
-            ((seq, seq), BF16),
-            ((values_all, seq), F32),
-            ((1, seq), F32),
-        ],
+    qkv_shape = (2 * keys_all + values_all, width)
+    query, keys, weights = kernel_call(
+        functools.partial(retention_scores, blocks),
+        [((keys_all, seq), BF16), ((keys_all, seq), BF16), ((seq, seq), BF16)],
         [],
-        2 * seq * width * all_qkv.shape[0] + square * (keys_all + values_all),
-        all_qkv,
+        2 * seq * width * all_qk.shape[0] + square * keys_all,
+        all_qk,
         x_one,
         *where,
     )
     cot = group_gather(after(cot_own, x_one))
     wide = 2 * seq * width * values_all
-    gate, hidden, attn = kernel_call(
+    narrow, broad = ((values_all, seq), BF16), ((values_all, width), BF16)
+    plain = ((values_all, seq), F32)
+    gate, hidden, attn, values, normed, inv_group = kernel_call(
         functools.partial(gated_forward, blocks),
-        [((values_all, seq), F32), ((values_all, seq), BF16), ((seq, width), BF16)],
-        [((values_all, width), BF16), ((values_all, width), BF16)],
-        2 * wide,
-        all_go,
+        [plain, narrow, ((seq, width), BF16), narrow, plain, ((1, seq), F32)],
+        [broad, broad, broad],
+        3 * wide + square * values_all,
+        all_vgo,
         x_one,
-        after(normed, cot),
+        after(weights, cot),
     )
     middle = stream + group_reduce(attn)
 
@@ -590,10 +589,10 @@
     plain = ((values_all, seq), F32)
     grad_gate, grad_ret, full_go = kernel_call(
         functools.partial(gated_backward, blocks),
-        [narrow, narrow, (all_go.shape, BF16)],
+        [narrow, narrow, ((2 * values_all, width), BF16)],
         [broad, tall, tall, plain, plain, ((1, seq), F32), narrow, narrow, narrow, broad, broad],
         3 * wide,
-        all_go,
+        all_vgo,
         x_one,
         *x_mid,
         gate,
@@ -603,12 +602,12 @@
         copies=3 * blocks + 15,
     )
     home_go = home(full_go)
-    home_shape = (depth, 8, 2 * kq + kv, part) if split == 2 else all_qkv.shape
+    home_shape = (depth, 8, 2 * kq + kv, part) if split == 2 else qkv_shape
     grad_qkv, full_qkv = kernel_call(
         functools.partial(retention_backward, blocks),
-        [((all_qkv.shape[0], seq), BF16), (home_shape, BF16)],
+        [((qkv_shape[0], seq), BF16), (home_shape, BF16)],
         [((seq, seq), BF16)],
-        2 * seq * width * all_qkv.shape[0] + 2 * square * (keys_all + values_all),
+        2 * seq * width * qkv_shape[0] + 2 * square * (keys_all + values_all),
         query,
         keys,
         values,
@@ -623,12 +622,12 @@
     (one_part,) = kernel_call(
         functools.partial(input_backward, blocks),
         [((seq, width), BF16)],
-        [((values_all, width), BF16)],
-        2 * seq * width * all_qkv.shape[0] + wide,
+        [broad, broad],
+        2 * seq * width * qkv_shape[0] + wide,
         grad_qkv,
-        all_qkv,
+        all_qk,
         after(grad_gate, full_qkv, grad_up),
-        all_go,
+        all_vgo,
     )
     grad_one = group_reduce(one_part)
     (ffn_part,) = kernel_call(

time: 570 us -> 562 us (0.986)
  waiting for transfers between devices: 259 us -> 240 us
  blocking collectives: 19.6 us -> 36.4 us
    all_to_all x1 -> x2, blocking collectives: 19.6 us -> 36.4 us  [to_heads(): got = lax.all_to_all(send, GROUP, split_axis=0, concat_axis=0, tiled=True)]
    all_to_all x1 -> x0, waiting for transfers between devices: 14.2 us -> none  [to_heads(): got = lax.all_to_all(send, GROUP, split_axis=0, concat_axis=0, tiled=True)]
    all_gather x3, waiting for transfers between devices: 34.3 us -> 28.6 us  [planes(): return lax.all_gather(mine, 'z', axis=0, tiled=True)]
    unnamed x94 -> x84, local copies, waits for them, and re-layouts: 15.4 us -> 14.2 us
  transfers between devices with their start and end apart: 83 -> 82, of which waited for: 43 -> 42; matrix products, arithmetic and copies ran while one was open for 13% -> 13% of each run, Pallas kernels for 15% -> 15%
where the time goes in v5:
time: 562 us; the launch traced here: 553 us
  waiting for transfers between devices  240 us (43%)
  Pallas kernels  102 us (18%)
  starting transfers between devices  76.1 us (14%)
  local copies, waits for them, and re-layouts  41.5 us (7%)
  blocking collectives  36.4 us (6%)
  other arithmetic  29.1 us (5%)
  between operations  15.9 us (3%)
  matrix products  11.5 us (2%)
    ppermute x67, waiting for transfers between devices, swap(): return lax.ppermute(value, GROUP, [(i, i ^ mask) for i in range(8)])  150 us
    pallas_call x7, Pallas kernels, kernel_call(): pl.pallas_call(body, out_shape=[jax.ShapeDtypeStruct(shape, kind) for sha...  102 us
    ppermute x67, starting transfers between devices, swap(): return lax.ppermute(value, GROUP, [(i, i ^ mask) for i in range(8)])  48.7 us
    all_to_all x2, blocking collectives, to_heads(): got = lax.all_to_all(send, GROUP, split_axis=0, concat_axis=0, tiled=True)  36.4 us
    all_to_all x4, waiting for transfers between devices, row_exchange(): return lax.all_to_all(parts, ROW, split_axis=0, concat_axis=0, tiled=True)  29.5 us
    all_gather x3, waiting for transfers between devices, planes(): return lax.all_gather(mine, 'z', axis=0, tiled=True)  28.6 us
    reduce_scatter x3, waiting for transfers between devices, home(): return lax.psum_scatter(full, 'z', scatter_dimension=0, tiled=True)  16.5 us
    all_to_all x4, starting transfers between devices, row_exchange(): return lax.all_to_all(parts, ROW, split_axis=0, concat_axis=0, tiled=True)  14.5 us
  transfers between devices with their start and end apart: 82, of which 42 were waited for; matrix products, arithmetic and copies ran while one was open for 13% of the time, Pallas kernels for 15%

profile of v5, /device:TPU:0, one launch (start us, length us, event | category | flops | bytes accessed | tf_op | source)
XLA Modules:
  0.0 553.1 jit_solution(9572540692401688537)
XLA Ops:
  10.1 13.8 %all_to_all.40 = bf16[8,64,512]{2,1,0:T(8,128)(2,1)S(1)} all-to-all(bf16[8,64,512]{2,1,0:T(8,128)(2,1)S(1)} %pad_maximum_fusion.4), channel_id=1, replica_groups=mesh['x'=2,'k'=2,'z'=4,'y'=2] {'x','k','y'}, dimensions={0} | all-to-all | bytes 1048576 | tf_op jit(solution)/shard_map/all_to_all | solution.py:450
  27.4 22.6 %all_to_all.41 = bf16[8,192,512]{2,1,0:T(8,128)(2,1)S(1)} all-to-all(bf16[8,192,512]{2,1,0:T(8,128)(2,1)S(1)} %pad_maximum_fusion), channel_id=1, replica_groups=mesh['x'=2,'k'=2,'z'=4,'y'=2] {'x','k','y'}, dimensions={0} | all-to-all | bytes 3145728 | tf_op jit(solution)/shard_map/all_to_all | solution.py:450
  63.1 14.3 %all-to-all-done.2 = bf16[4,2,128,512]{3,2,1,0:T(8,128)(2,1)S(1)} async-done(((bf16[4,2,128,512]{3,2,1,0:T(8,128)(2,1)}), bf16[4,2,128,512]{3,2,1,0:T(8,128)(2,1)S(1)}, u32[]{:S(2)}, u32[]{:S(2)}) %all-to-all-start.2) | async-done | bytes 1048608 | tf_op jit(solution)/shard_map/all_to_all | solution.py:93
  90.8 4.8 collective-permute-done.7
  95.7 10.1 %collective-permute-done.6 = bf16[128,2048]{1,0:T(8,128)(2,1)} collective-permute-done((bf16[128,2048]{1,0:T(8,128)(2,1)}, bf16[128,2048]{1,0:T(8,128)(2,1)}, u32[]{:S(2)}, u32[]{:S(2)}) %collective-permute-start.6) | collective-permute-done | bytes 524320 | tf_op jit(solution)/shard_map/ppermute | solution.py:29
  110.1 5.5 all-to-all-done.3
  130.1 10.9 %collective-permute-done.14.refs_13_ = bf16[128,2048]{1,0:T(8,128)(2,1)} collective-permute-done((bf16[128,2048]{1,0:T(8,128)(2,1)S(1)}, bf16[128,2048]{1,0:T(8,128)(2,1)}, u32[]{:S(2)}, u32[]{:S(2)}) %collective-permute-start.14) | collective-permute-done | bytes 524320 | tf_op jit(solution)/shard_map/ppermute | solution.py:29
  141.1 9.4 %collective-permute-done.13.refs_12_ = bf16[128,2048]{1,0:T(8,128)(2,1)} collective-permute-done((bf16[128,2048]{1,0:T(8,128)(2,1)S(1)}, bf16[128,2048]{1,0:T(8,128)(2,1)}, u32[]{:S(2)}, u32[]{:S(2)}) %collective-permute-start.13) | collective-permute-done | bytes 524320 | tf_op jit(solution)/shard_map/ppermute | solution.py:29
  153.7 9.3 %shard_map.237 = (bf16[256,1024]{1,0:T(8,128)(2,1)}, bf16[256,1024]{1,0:T(8,128)(2,1)}, bf16[1024,1024]{1,0:T(8,128)(2,1)}) custom-call(bf16[512,2048]{1,0:T(8,128)(2,1)} %all-gather.6.cloned.1.call-done.w, bf16[1024,2048]{1,0:T(8,128)(2,1)} %constant_dynamic-update-slice_fusion.1.x.x_in, s32[1024,1]{1,0:T(8,128)} %copy-done.6, s32[1,1024]{1,0:T(1,128)} %bitcast.170, ...), custom_call_target="tpu_custom_call" | custom-call | flops 2684354560 | bytes 9461760 | tf_op jit(solution)/shard_map/pallas_call | solution.py:156
  163.0 24.2 %all-gather.4.cloned.1.call-done.w.vgo = bf16[1536,2048]{1,0:T(8,128)(2,1)} async-done(((bf16[384,2048]{1,0:T(8,128)(2,1)}), bf16[1536,2048]{1,0:T(8,128)(2,1)}) %all-gather.4.cloned.1.call-update) | async-done | bytes 6291472 | tf_op jit(solution)/shard_map/all_gather | solution.py:474
  187.2 19.9 %shard_map.238 = (f32[512,1024]{1,0:T(8,128)}, bf16[512,1024]{1,0:T(8,128)(2,1)}, bf16[1024,2048]{1,0:T(8,128)(2,1)}, bf16[512,1024]{1,0:T(8,128)(2,1)}, f32[512,1024]{1,0:T(8,128)}, /*index=5*/f32[1,1024]{1,0:T(1,128)}) custom-call(bf16[1536,2048]{1,0:T(8,128)(2,1)} %all-gather.4.cloned.1.call-done.w.vgo, ...), custom_call_target="tpu_custom_call" | custom-call | flops 7516192768 | bytes 23072768 | tf_op jit(solution)/shard_map/pallas_call | solution.py:156
  216.3 5.3 collective-permute-done.23
  224.8 10.1 %collective-permute-done.24 = bf16[128,2048]{1,0:T(8,128)(2,1)S(1)} collective-permute-done((bf16[128,2048]{1,0:T(8,128)(2,1)S(1)}, bf16[128,2048]{1,0:T(8,128)(2,1)S(1)}, u32[]{:S(2)}, u32[]{:S(2)}) %collective-permute-start.24) | collective-permute-done | bytes 524320 | tf_op jit(solution)/shard_map/ppermute | solution.py:29
  242.0 12.3 %collective-permute-done.29.refs_5_ = bf16[128,2048]{1,0:T(8,128)(2,1)S(1)} collective-permute-done((bf16[128,2048]{1,0:T(8,128)(2,1)S(1)}, bf16[128,2048]{1,0:T(8,128)(2,1)S(1)}, u32[]{:S(2)}, u32[]{:S(2)}) %collective-permute-start.29) | collective-permute-done | bytes 524320 | tf_op jit(solution)/shard_map/ppermute | solution.py:29
  254.3 9.3 %collective-permute-done.28.refs_4_ = bf16[128,2048]{1,0:T(8,128)(2,1)S(1)} collective-permute-done((bf16[128,2048]{1,0:T(8,128)(2,1)S(1)}, bf16[128,2048]{1,0:T(8,128)(2,1)S(1)}, u32[]{:S(2)}, u32[]{:S(2)}) %collective-permute-start.28) | collective-permute-done | bytes 524320 | tf_op jit(solution)/shard_map/ppermute | solution.py:29
  264.1 4.3 all-gather.8.cloned.1.call-done.w
  268.5 18.6 %shard_map.239 = (bf16[512,1024]{1,0:T(8,128)(2,1)}, bf16[1024,2048]{1,0:T(8,128)(2,1)}, bf16[1024,2048]{1,0:T(8,128)(2,1)}) custom-call(bf16[1024,2048]{1,0:T(8,128)(2,1)} %all-gather.8.cloned.1.call-done.w, bf16[128,2048]{1,0:T(8,128)(2,1)} %copy-done.14, bf16[128,2048]{1,0:T(8,128)(2,1)} %collective-permute-done.25.refs_1_, ...), custom_call_target="tpu_custom_call" | custom-call | flops 10737418240 | bytes 22020096 | tf_op jit(solution)/shard_map/pallas_call | solution.py:156
  296.3 5.2 collective-permute-done.38
  304.8 10.1 %collective-permute-done.39 = bf16[128,2048]{1,0:T(8,128)(2,1)S(1)} collective-permute-done((bf16[128,2048]{1,0:T(8,128)(2,1)S(1)}, bf16[128,2048]{1,0:T(8,128)(2,1)S(1)}, u32[]{:S(2)}, u32[]{:S(2)}) %collective-permute-start.39) | collective-permute-done | bytes 524320 | tf_op jit(solution)/shard_map/ppermute | solution.py:29
  323.1 12.3 %collective-permute-done.44.refs_5_ = bf16[128,2048]{1,0:T(8,128)(2,1)S(1)} collective-permute-done((bf16[128,2048]{1,0:T(8,128)(2,1)S(1)}, bf16[128,2048]{1,0:T(8,128)(2,1)S(1)}, u32[]{:S(2)}, u32[]{:S(2)}) %collective-permute-start.44) | collective-permute-done | bytes 524320 | tf_op jit(solution)/shard_map/ppermute | solution.py:29
  335.4 9.3 %collective-permute-done.43.refs_4_ = bf16[128,2048]{1,0:T(8,128)(2,1)S(1)} collective-permute-done((bf16[128,2048]{1,0:T(8,128)(2,1)S(1)}, bf16[128,2048]{1,0:T(8,128)(2,1)S(1)}, u32[]{:S(2)}, u32[]{:S(2)}) %collective-permute-start.43) | collective-permute-done | bytes 524320 | tf_op jit(solution)/shard_map/ppermute | solution.py:29
  348.2 15.1 %shard_map.240 = (bf16[512,1024]{1,0:T(8,128)(2,1)}, bf16[512,1024]{1,0:T(8,128)(2,1)}, bf16[1024,2048]{1,0:T(8,128)(2,1)}) custom-call(bf16[1536,2048]{1,0:T(8,128)(2,1)} %all-gather.4.cloned.1.call-done.w.vgo, bf16[1024,2048]{1,0:T(8,128)(2,1)} %constant_dynamic-update-slice_fusion.1.x.x_in, bf16[128,2048]{1,0:T(8,128)(2,1)} %copy-done.15, ...), custom_call_target="tpu_custom_call" | custom-call | flops 6442450944 | bytes 26218496 | tf_op jit(solution)/shard_map/pallas_call | solution.py:156
  370.2 17.9 %shard_map.241 = (bf16[1024,1024]{1,0:T(8,128)(2,1)}, bf16[4,8,128,512]{3,2,1,0:T(8,128)(2,1)}) custom-call(bf16[256,1024]{1,0:T(8,128)(2,1)} %get-tuple-element.57.q, bf16[256,1024]{1,0:T(8,128)(2,1)} %get-tuple-element.58.k, bf16[512,1024]{1,0:T(8,128)(2,1)} %get-tuple-element.59.v, bf16[1024,1024]{1,0:T(8,128)(2,1)} %get-tuple-element.53.weights, ...), custom_call_target="tpu_custom_call" | custom-call | flops 7516192768 | bytes 15753216 | tf_op jit(solution)/shard_map/pallas_call | solution.py:156
  389.2 14.0 %shard_map.242 = bf16[1024,2048]{1,0:T(8,128)(2,1)} custom-call(bf16[1024,1024]{1,0:T(8,128)(2,1)} %get-tuple-element.65.packed, bf16[512,2048]{1,0:T(8,128)(2,1)} %all-gather.6.cloned.1.call-done.w, bf16[512,1024]{1,0:T(8,128)(2,1)} %get-tuple-element.69.ggate, bf16[1536,2048]{1,0:T(8,128)(2,1)} %all-gather.4.cloned.1.call-done.w.vgo), custom_call_target="tpu_custom_call" | custom-call | flops 6442450944 | bytes 15728640 | tf_op jit(solution)/shard_map/pallas_call | solution.py:156
  403.2 7.6 %shard_map.243 = bf16[1024,2048]{1,0:T(8,128)(2,1)} custom-call(bf16[1024,2048]{1,0:T(8,128)(2,1)} %all-gather.8.cloned.1.call-done.w, bf16[512,1024]{1,0:T(8,128)(2,1)} %get-tuple-element.71.act), custom_call_target="tpu_custom_call" | custom-call | flops 2147483648 | bytes 9437184 | tf_op jit(solution)/shard_map/pallas_call | solution.py:156
  432.7 4.3 collective-permute-done.53
  442.1 4.3 collective-permute-done.62
  446.4 5.4 collective-permute-done.59
  467.8 3.8 all-to-all-start.5
  476.7 9.8 %all-to-all-done.5 = bf16[4,2,128,512]{3,2,1,0:T(8,128)(2,1)S(1)} async-done(((bf16[4,2,128,512]{3,2,1,0:T(8,128)(2,1)}), bf16[4,2,128,512]{3,2,1,0:T(8,128)(2,1)S(1)}, u32[]{:S(2)}, u32[]{:S(2)}) %all-to-all-start.5) | async-done | bytes 1048608 | tf_op jit(solution)/shard_map/all_to_all | solution.py:93
  507.2 16.5 %reduce-scatter.6.cloned.1.call-done = bf16[1,8,128,512]{3,2,1,0:T(8,128)(2,1)} async-done(((bf16[4,8,128,512]{3,2,1,0:T(8,128)(2,1)}), bf16[1,8,128,512]{3,2,1,0:T(8,128)(2,1)}) %reduce-scatter.6.cloned.1.call-update) | async-done | bytes 1048592 | tf_op jit(solution)/shard_map/reduce_scatter | solution.py:576
  531.0 10.8 %all-to-all-done.7 = bf16[8,128,512]{2,1,0:T(8,128)(2,1)S(1)} async-done(((bf16[8,128,512]{2,1,0:T(8,128)(2,1)}), bf16[8,128,512]{2,1,0:T(8,128)(2,1)S(1)}, u32[]{:S(2)}, u32[]{:S(2)}) %all-to-all-start.7) | async-done | bytes 1048608 | tf_op jit(solution)/shard_map/all_to_all | solution.py:663
  (358 shorter events, 186.2 us)
Async XLA Ops:
  7.2 146.5 %all-gather.6.cloned.1.call-start = ((), (), s32[]{:S(2)}) async-start(), calls=%async_computation.12 | async-start | bytes 2621440 | tf_op jit(solution)/shard_map/all_gather | solution.py:474
  25.2 162.0 %all-gather.4.cloned.1.call-start = ((), (), s32[]{:S(2)}) async-start(), calls=%async_computation.11 | async-start | bytes 7864320 | tf_op jit(solution)/shard_map/all_gather | solution.py:474
  59.2 18.1 %all-to-all-start.2 = ((bf16[4,2,128,512]{3,2,1,0:T(8,128)(2,1)}), bf16[4,2,128,512]{3,2,1,0:T(8,128)(2,1)S(1)}, u32[]{:S(2)}, u32[]{:S(2)}) async-start(bf16[4,2,128,512]{3,2,1,0:T(8,128)(2,1)} %pad_maximum_fusion.1), calls=%async_computation.2 | async-start | bytes 2097152 | tf_op jit(solution)/shard_map/all_to_all | solution.py:93
  79.7 26.1 %collective-permute-start.6 = (bf16[128,2048]{1,0:T(8,128)(2,1)}, bf16[128,2048]{1,0:T(8,128)(2,1)}, u32[]{:S(2)}, u32[]{:S(2)}) collective-permute-start(bf16[128,2048]{1,0:T(8,128)(2,1)} %get-tuple-element.90), channel_id=1, source_target_pairs={{0,16},{1,17},{8,24},{9,25},{16,0},{17,1},{24,8},{25,9},{2,18},{3,... | collective-permute-start | bytes 1572872 | tf_op jit(solution)/shard_map/ppermute | solution.py:29
  81.4 24.4 %collective-permute-start.3 = (bf16[128,2048]{1,0:T(8,128)(2,1)}, bf16[128,2048]{1,0:T(8,128)(2,1)}, u32[]{:S(2)}, u32[]{:S(2)}) collective-permute-start(bf16[128,2048]{1,0:T(8,128)(2,1)} %get-tuple-element.90), channel_id=1, source_target_pairs={{0,1},{1,0},{8,9},{9,8},{16,17},{17,16},{24,25},{25,24},{2,3},{3,2... | collective-permute-start | bytes 1572872 | tf_op jit(solution)/shard_map/ppermute | solution.py:29
  85.5 30.0 %all-to-all-start.3 = ((bf16[4,2,128,512]{3,2,1,0:T(8,128)(2,1)}), bf16[4,2,128,512]{3,2,1,0:T(8,128)(2,1)S(1)}, u32[]{:S(2)}, u32[]{:S(2)}) async-start(bf16[4,2,128,512]{3,2,1,0:T(8,128)(2,1)} %pad_maximum_fusion.2), calls=%async_computation.3 | async-start | bytes 2097152 | tf_op jit(solution)/shard_map/all_to_all | solution.py:93
  89.1 179.3 %all-gather.8.cloned.1.call-start = ((), (), s32[]{:S(2)}) async-start(), calls=%async_computation.13 | async-start | bytes 5242880 | tf_op jit(solution)/shard_map/all_gather | solution.py:474
  89.1 19.1 %collective-permute-start.4 = (bf16[128,2048]{1,0:T(8,128)(2,1)}, bf16[128,2048]{1,0:T(8,128)(2,1)}, u32[]{:S(2)}, u32[]{:S(2)}) collective-permute-start(bf16[128,2048]{1,0:T(8,128)(2,1)} %get-tuple-element.90), channel_id=1, source_target_pairs={{0,8},{1,9},{8,0},{9,1},{16,24},{17,25},{24,16},{25,17},{2,10},{3,... | collective-permute-start | bytes 1572872 | tf_op jit(solution)/shard_map/ppermute | solution.py:29
  95.7 27.6 %collective-permute-start.9 = (bf16[128,2048]{1,0:T(8,128)(2,1)S(1)}, bf16[128,2048]{1,0:T(8,128)(2,1)}, u32[]{:S(2)}, u32[]{:S(2)}) collective-permute-start(bf16[128,2048]{1,0:T(8,128)(2,1)S(1)} %collective-permute-done.7), channel_id=1, source_target_pairs={{0,8},{1,9},{8,0},{9,1},{16,24},{17,25},{24,16},{25,17},{2,10},{3,... | collective-permute-start | bytes 1572872 | tf_op jit(solution)/shard_map/ppermute | solution.py:29
  127.0 23.4 %collective-permute-start.13 = (bf16[128,2048]{1,0:T(8,128)(2,1)S(1)}, bf16[128,2048]{1,0:T(8,128)(2,1)}, u32[]{:S(2)}, u32[]{:S(2)}) collective-permute-start(bf16[128,2048]{1,0:T(8,128)(2,1)S(1)} %bitcast.123), channel_id=1, source_target_pairs={{0,16},{1,17},{8,24},{9,25},{16,0},{17,1},{24,8},{25,9},{2,18},{3,... | collective-permute-start | bytes 1572872 | tf_op jit(solution)/shard_map/ppermute | solution.py:29
  128.4 22.0 %collective-permute-start.10 = (bf16[128,2048]{1,0:T(8,128)(2,1)S(1)}, bf16[128,2048]{1,0:T(8,128)(2,1)}, u32[]{:S(2)}, u32[]{:S(2)}) collective-permute-start(bf16[128,2048]{1,0:T(8,128)(2,1)S(1)} %bitcast.124), channel_id=1, source_target_pairs={{0,1},{1,0},{8,9},{9,8},{16,17},{17,16},{24,25},{25,24},{2,3},{3,2... | collective-permute-start | bytes 1572872 | tf_op jit(solution)/shard_map/ppermute | solution.py:29
  130.0 33.0 %collective-permute-start.11 = (bf16[128,2048]{1,0:T(8,128)(2,1)S(1)}, bf16[128,2048]{1,0:T(8,128)(2,1)}, u32[]{:S(2)}, u32[]{:S(2)}) collective-permute-start(bf16[128,2048]{1,0:T(8,128)(2,1)S(1)} %bitcast.125), channel_id=1, source_target_pairs={{0,8},{1,9},{8,0},{9,1},{16,24},{17,25},{24,16},{25,17},{2,10},{3,... | collective-permute-start | bytes 1572872 | tf_op jit(solution)/shard_map/ppermute | solution.py:29
  141.1 21.9 %collective-permute-start.16 = (bf16[128,2048]{1,0:T(8,128)(2,1)}, bf16[128,2048]{1,0:T(8,128)(2,1)}, u32[]{:S(2)}, u32[]{:S(2)}) collective-permute-start(bf16[128,2048]{1,0:T(8,128)(2,1)} %collective-permute-done.14.refs_13_), channel_id=1, source_target_pairs={{0,8},{1,9},{8,0},{9,1},{16,24},{17,25},{24,16},{25,17},{2,10},{3,... | collective-permute-start | bytes 1572872 | tf_op jit(solution)/shard_map/ppermute | solution.py:29
  153.2 210.2 %reduce-scatter.4.cloned.1.call-start = ((), (), s32[]{:S(2)}) async-start(), calls=%async_computation.14 | async-start | bytes 5242880 | tf_op jit(solution)/shard_map/reduce_scatter | solution.py:576
  240.0 23.6 %collective-permute-start.28 = (bf16[128,2048]{1,0:T(8,128)(2,1)S(1)}, bf16[128,2048]{1,0:T(8,128)(2,1)S(1)}, u32[]{:S(2)}, u32[]{:S(2)}) collective-permute-start(bf16[128,2048]{1,0:T(8,128)(2,1)S(1)} %add_convert_fusion.4.refs_0_), channel_id=1, source_target_pairs={{0,16},{1,17},{8,24},{9,25},{16,0},{17,1},{24,8},{25,9},{2,18},{3,... | collective-permute-start | bytes 1572872 | tf_op jit(solution)/shard_map/ppermute | solution.py:29
  241.4 22.2 %collective-permute-start.25 = (bf16[128,2048]{1,0:T(8,128)(2,1)S(1)}, bf16[128,2048]{1,0:T(8,128)(2,1)}, u32[]{:S(2)}, u32[]{:S(2)}) collective-permute-start(bf16[128,2048]{1,0:T(8,128)(2,1)S(1)} %add_convert_fusion.4.refs_0_), channel_id=1, source_target_pairs={{0,1},{1,0},{8,9},{9,8},{16,17},{17,16},{24,25},{25,24},{2,3},{3,2... | collective-permute-start | bytes 1572872 | tf_op jit(solution)/shard_map/ppermute | solution.py:29
  242.0 26.4 %collective-permute-start.26 = (bf16[128,2048]{1,0:T(8,128)(2,1)S(1)}, bf16[128,2048]{1,0:T(8,128)(2,1)}, u32[]{:S(2)}, u32[]{:S(2)}) collective-permute-start(bf16[128,2048]{1,0:T(8,128)(2,1)S(1)} %add_convert_fusion.4.refs_0_), channel_id=1, source_target_pairs={{0,8},{1,9},{8,0},{9,1},{16,24},{17,25},{24,16},{25,17},{2,10},{3,... | collective-permute-start | bytes 1572872 | tf_op jit(solution)/shard_map/ppermute | solution.py:29
  287.1 201.4 %reduce-scatter.8.cloned.1.call-start = ((), (), s32[]{:S(2)}) async-start(), calls=%async_computation.16 | async-start | bytes 5242880 | tf_op jit(solution)/shard_map/reduce_scatter | solution.py:576
  321.1 23.6 %collective-permute-start.43 = (bf16[128,2048]{1,0:T(8,128)(2,1)S(1)}, bf16[128,2048]{1,0:T(8,128)(2,1)S(1)}, u32[]{:S(2)}, u32[]{:S(2)}) collective-permute-start(bf16[128,2048]{1,0:T(8,128)(2,1)S(1)} %get-tuple-element.84.refs_0_), channel_id=1, source_target_pairs={{0,16},{1,17},{8,24},{9,25},{16,0},{17,1},{24,8},{25,9},{2,18},{3,... | collective-permute-start | bytes 1572872 | tf_op jit(solution)/shard_map/ppermute | solution.py:29
  322.5 22.2 %collective-permute-start.40 = (bf16[128,2048]{1,0:T(8,128)(2,1)S(1)}, bf16[128,2048]{1,0:T(8,128)(2,1)S(1)}, u32[]{:S(2)}, u32[]{:S(2)}) collective-permute-start(bf16[128,2048]{1,0:T(8,128)(2,1)S(1)} %get-tuple-element.84.refs_0_), channel_id=1, source_target_pairs={{0,1},{1,0},{8,9},{9,8},{16,17},{17,16},{24,25},{25,24},{2,3},{3,2... | collective-permute-start | bytes 1572872 | tf_op jit(solution)/shard_map/ppermute | solution.py:29
  323.1 22.1 %collective-permute-start.41 = (bf16[128,2048]{1,0:T(8,128)(2,1)S(1)}, bf16[128,2048]{1,0:T(8,128)(2,1)S(1)}, u32[]{:S(2)}, u32[]{:S(2)}) collective-permute-start(bf16[128,2048]{1,0:T(8,128)(2,1)S(1)} %get-tuple-element.84.refs_0_), channel_id=1, source_target_pairs={{0,8},{1,9},{8,0},{9,1},{16,24},{17,25},{24,16},{25,17},{2,10},{3,... | collective-permute-start | bytes 1572872 | tf_op jit(solution)/shard_map/ppermute | solution.py:29
  366.6 21.5 %all-to-all-start.4 = ((bf16[4,2,128,512]{3,2,1,0:T(8,128)(2,1)}), bf16[4,2,128,512]{3,2,1,0:T(8,128)(2,1)S(1)}, u32[]{:S(2)}, u32[]{:S(2)}) async-start(bf16[4,2,128,512]{3,2,1,0:T(8,128)(2,1)} %maximum_bitcast_fusion), calls=%async_computation.5 | async-start | bytes 2097152 | tf_op jit(solution)/shard_map/all_to_all | solution.py:93
  370.2 153.5 %reduce-scatter.6.cloned.1.call-start = ((), (), s32[]{:S(2)}) async-start(), calls=%async_computation.15 | async-start | bytes 5242880 | tf_op jit(solution)/shard_map/reduce_scatter | solution.py:576
  414.5 27.0 %collective-permute-start.55 = (bf16[128,2048]{1,0:T(8,128)(2,1)S(1)}, bf16[128,2048]{1,0:T(8,128)(2,1)S(1)}, u32[]{:S(2)}, u32[]{:S(2)}) collective-permute-start(bf16[128,2048]{1,0:T(8,128)(2,1)S(1)} %get-tuple-element.98), channel_id=1, source_target_pairs={{0,8},{1,9},{8,0},{9,1},{16,24},{17,25},{24,16},{25,17},{2,10},{3,... | collective-permute-start | bytes 1572872 | tf_op jit(solution)/shard_map/ppermute | solution.py:29
  417.3 36.2 %collective-permute-start.47 = (bf16[128,2048]{1,0:T(8,128)(2,1)}, bf16[128,2048]{1,0:T(8,128)(2,1)}, u32[]{:S(2)}, u32[]{:S(2)}) collective-permute-start(bf16[128,2048]{1,0:T(8,128)(2,1)} %get-tuple-element.91), channel_id=1, source_target_pairs={{0,8},{1,9},{8,0},{9,1},{16,24},{17,25},{24,16},{25,17},{2,10},{3,... | collective-permute-start | bytes 1572872 | tf_op jit(solution)/shard_map/ppermute | solution.py:29
  441.5 19.1 %collective-permute-start.51 = (bf16[128,2048]{1,0:T(8,128)(2,1)}, bf16[128,2048]{1,0:T(8,128)(2,1)}, u32[]{:S(2)}, u32[]{:S(2)}) collective-permute-start(bf16[128,2048]{1,0:T(8,128)(2,1)} %pad_maximum_fusion.9), channel_id=1, source_target_pairs={{0,16},{1,17},{8,24},{9,25},{16,0},{17,1},{24,8},{25,9},{2,18},{3,... | collective-permute-start | bytes 1572872 | tf_op jit(solution)/shard_map/ppermute | solution.py:29
  467.8 18.7 %all-to-all-start.5 = ((bf16[4,2,128,512]{3,2,1,0:T(8,128)(2,1)}), bf16[4,2,128,512]{3,2,1,0:T(8,128)(2,1)S(1)}, u32[]{:S(2)}, u32[]{:S(2)}) async-start(bf16[4,2,128,512]{3,2,1,0:T(8,128)(2,1)} %maximum_bitcast_fusion.1), calls=%async_computation.6 | async-start | bytes 2097152 | tf_op jit(solution)/shard_map/all_to_all | solution.py:93
  473.2 23.1 %collective-permute-start.65 = (f32[4,2048]{1,0:T(4,128)S(1)}, f32[4,2048]{1,0:T(4,128)S(1)}, u32[]{:S(2)}, u32[]{:S(2)}) collective-permute-start(f32[4,2048]{1,0:T(4,128)S(1)} %fusion.61), channel_id=1, source_target_pairs={{0,16},{1,17},{8,24},{9,25},{16,0},{17,1},{24,8},{25,9},{2,18},{3,... | collective-permute-start | bytes 98312 | tf_op jit(solution)/shard_map/ppermute | solution.py:29
  475.0 21.3 %collective-permute-start.66 = (f32[4,2048]{1,0:T(4,128)S(1)}, f32[4,2048]{1,0:T(4,128)S(1)}, u32[]{:S(2)}, u32[]{:S(2)}) collective-permute-start(f32[4,2048]{1,0:T(4,128)S(1)} %fusion.61), channel_id=1, source_target_pairs={{0,17},{1,16},{8,25},{9,24},{16,1},{17,0},{24,9},{25,8},{2,19},{3,... | collective-permute-start | bytes 98312 | tf_op jit(solution)/shard_map/ppermute | solution.py:29
  476.0 20.3 %collective-permute-start.64 = (f32[4,2048]{1,0:T(4,128)S(1)}, f32[4,2048]{1,0:T(4,128)S(1)}, u32[]{:S(2)}, u32[]{:S(2)}) collective-permute-start(f32[4,2048]{1,0:T(4,128)S(1)} %fusion.61), channel_id=1, source_target_pairs={{0,1},{1,0},{8,9},{9,8},{16,17},{17,16},{24,25},{25,24},{2,3},{3,2... | collective-permute-start | bytes 98312 | tf_op jit(solution)/shard_map/ppermute | solution.py:29
  491.6 32.1 %all-to-all-start.6 = ((bf16[8,128,512]{2,1,0:T(8,128)(2,1)}), bf16[8,128,512]{2,1,0:T(8,128)(2,1)S(1)}, u32[]{:S(2)}, u32[]{:S(2)}) async-start(bf16[8,128,512]{2,1,0:T(8,128)(2,1)} %bitcast.40), calls=%async_computation.9 | async-start | bytes 2097152 | tf_op jit(solution)/shard_map/all_to_all | solution.py:654
  523.7 18.2 %all-to-all-start.7 = ((bf16[8,128,512]{2,1,0:T(8,128)(2,1)}), bf16[8,128,512]{2,1,0:T(8,128)(2,1)S(1)}, u32[]{:S(2)}, u32[]{:S(2)}) async-start(bf16[8,128,512]{2,1,0:T(8,128)(2,1)} %bitcast.128), calls=%async_computation.10 | async-start | bytes 2097152 | tf_op jit(solution)/shard_map/all_to_all | solution.py:663
  (84 other events, 838.4 us)
Sparse Core Ops, SparseCore 0:
  25.3 46.1 all-gather.5
  73.1 114.0 all-gather.3
  189.4 78.9 all-gather.7
  287.2 75.2 reduce-scatter.3
  364.8 77.2 reduce-scatter.7
  444.3 79.3 reduce-scatter.5

commit v6 on v5

--- a/solution.py
+++ b/solution.py
@@ -264,13 +264,16 @@
     wu, wd, x, cot, act, gp, turned, back, gu, gd, semaphores = refs[19:]
     move = Mover(semaphores)
     seq, rows = x.shape[0], x_blocks[0].shape[0]
-    weights = move.kind(w, wu, ("from", 0, 2), depth) + move.kind(w, wd, ("from", 1, 2), depth)
-    x_copies, cot_copies = move.rows(x_blocks, x), move.rows(cot_blocks, cot)
-    wait(weights)
-    for tile in range(seq // TALL):
-        mine = slice(tile * TALL // rows, (tile + 1) * TALL // rows)
-        wait(x_copies[mine] + cot_copies[mine])
-        at = pl.ds(tile * TALL, TALL)
+    first = TALL // rows
+    wu_copies = move.kind(w, wu, ("from", 0, 2), depth)
+    x_copies = move.rows(x_blocks[:first], x.at[pl.ds(0, TALL)])
+    wd_copies = move.kind(w, wd, ("from", 1, 2), depth)
+    cot_copies = move.rows(cot_blocks[:first], cot.at[pl.ds(0, TALL)])
+    x_copies += move.rows(x_blocks[first:], x.at[pl.ds(TALL, seq - TALL)])
+    cot_copies += move.rows(cot_blocks[first:], cot.at[pl.ds(TALL, seq - TALL)])
+    wait(wu_copies + x_copies + wd_copies + cot_copies)
+
+    def step(at):
         pre = dot(wu[...], x[at, :], ((1,), (1,)))
         grad = dot(wd[...], cot[at, :], ((1,), (1,)))
         half = 0.5 * (1.0 + lax.erf(pre * np.float32(0.5**0.5)))
@@ -279,6 +282,8 @@
         low = grad * (half + pre * bell)
         gp[:, at] = low.astype(BF16)
         turned[at, :] = low.T.astype(BF16)
+
+    spans(seq, TALL, step)
     sent = [move.start(act, act_out)]
 
     def up_step(at):
@@ -291,10 +296,11 @@
     sent += move.kind(gu, grads_out, ("to", 0, 2), depth)
     spans(x.shape[1], WIDE, down_step)
     sent += move.kind(gd, grads_out, ("to", 1, 2), depth)
-    for tile in range(x.shape[1] // WIDE):
-        at = pl.ds(tile * WIDE, WIDE)
+    def back_step(at):
         back[:, at] = dot(turned[...], wu[:, at], ((1,), (0,))).astype(BF16)
-        sent.append(move.start(back.at[:, at], back_out.at[:, at]))
+
+    spans(x.shape[1], WIDE, back_step)
+    sent.append(move.start(back, back_out))
     wait(sent)
 
 
@@ -315,7 +321,7 @@
     seq, rows = x.shape[0], mid_blocks[0].shape[0]
     first = move.kind(w, wo, ("from", 2, 3), depth)
     mid_copies = move.rows(mid_blocks[:4], mid.at[pl.ds(0, 4 * rows)])
-    first += [move.start(inv_in, inv), move.start(gate_in, gate), move.start(normed_in, normed)]
+    second = [move.start(inv_in, inv), move.start(gate_in, gate), move.start(normed_in, normed)]
     mid_copies += move.rows(mid_blocks[4:], mid.at[pl.ds(4 * rows, seq - 4 * rows)])
     late = [move.start(x_in, x), move.start(hidden_in, hidden)]
     wait(first)
@@ -323,6 +329,8 @@
         wait(mid_copies[tile * TALL // rows : (tile + 1) * TALL // rows])
         at = pl.ds(tile * TALL, TALL)
         up = dot(wo[...], mid[at, :], ((1,), (1,)))
+        if tile == 0:
+            wait(second)
         g = gate[:, at]
         s = jax.nn.sigmoid(g)
         full = normed[:, at]
@@ -473,11 +481,8 @@
     def planes(mine):
         return lax.all_gather(mine, "z", axis=0, tiled=True)
 
-    got_qk = to_heads(
-        jnp.concatenate([by_head(w_query, order_q), by_head(w_key, order_q)], axis=1)
-    )
-    mine_qk = regroup(got_qk, kq, kq)
-    all_qk = planes(mine_qk)
+    send_qk = jnp.concatenate([by_head(w_query, order_q), by_head(w_key, order_q)], axis=1)
+    from_planes = planes(send_qk.reshape(-1, part)).reshape(depth, HEADS, -1, part)
     send_vgo = jnp.concatenate(
         [
             by_head(w_value, order_v),
@@ -486,7 +491,7 @@
         ],
         axis=1,
     )
-    got_vgo = to_heads(after(send_vgo, mine_qk))
+    got_vgo = to_heads(after(send_vgo, send_qk))
     mine_vgo = regroup(got_vgo, kv, kv, kv)
     all_vgo = planes(mine_vgo)
 
@@ -499,7 +504,7 @@
             segments.astype(F32),
         ]
     )
-    small = row_gather(after(small, mine_qk))
+    small = row_gather(after(small, send_qk))
     params = small[:, : 4 * part].reshape(4, 4, part).transpose(1, 0, 2).reshape(4, width)
     segs = small[:, 4 * part :].astype(jnp.int32).reshape(depth, 8, tokens)
     block_in, cotangent = after(block_in, got_vgo), after(cotangent, got_vgo)
@@ -524,6 +529,11 @@
     where = (pos[:, None], pos[None, :], seg[:, None], seg[None, :])
     where = where + (grow[:, None], jnp.exp(-lag)[None, :])
 
+    got_qk = lax.all_to_all(
+        from_planes.transpose(1, 0, 2, 3), GROUP, split_axis=0, concat_axis=0, tiled=True
+    ).reshape(4, 2, depth, 2, kq, part)
+    order = (2, 1, 3, 4, 0, 5) if split == 2 else (2, 3, 1, 4, 0, 5)
+    all_qk = got_qk.transpose(order).reshape(-1, width)
     x_one = after(x_one, mine_up, mine_down)
     keys_all, values_all = kq * 2 * depth, kv * 2 * depth
     square = 2 * seq * seq
@@ -568,7 +578,7 @@
         *x_two,
         after(cot[0], token),
         *cot[1:],
-        copies=4 * depth + 17 + width // WIDE,
+        copies=4 * depth + 18,
     )
     grad_two = group_reduce(two_part)
 

time: 562 us -> 556 us (0.989)
  blocking collectives: 36.4 us -> 25 us
    all_gather x3, waiting for transfers between devices: 28.6 us -> 0.19 us  [planes(): return lax.all_gather(mine, 'z', axis=0, tiled=True)]
    ppermute x67, waiting for transfers between devices: 150 us -> 171 us  [swap(): return lax.ppermute(value, GROUP, [(i, i ^ mask) for i in range(8)])]
    all_to_all x2 -> x1, blocking collectives: 36.4 us -> 25 us  [to_heads(): got = lax.all_to_all(send, GROUP, split_axis=0, concat_axis=0, tiled=True)]
    unnamed x84 -> x78, local copies, waits for them, and re-layouts: 14.2 us -> 16.6 us
  transfers between devices with their start and end apart: 82 -> 83, of which waited for: 42 -> 44; matrix products, arithmetic and copies ran while one was open for 13% -> 15% of each run, Pallas kernels for 15% -> 15%
where the time goes in v6:
time: 556 us; the launch traced here: 547 us
  waiting for transfers between devices  239 us (43%)
  Pallas kernels  103 us (19%)
  starting transfers between devices  75.1 us (14%)
  local copies, waits for them, and re-layouts  46.5 us (8%)
  other arithmetic  30.3 us (5%)
  blocking collectives  25 us (4%)
  between operations  15.6 us (3%)
  matrix products  12.5 us (2%)
    ppermute x67, waiting for transfers between devices, swap(): return lax.ppermute(value, GROUP, [(i, i ^ mask) for i in range(8)])  171 us
    pallas_call x7, Pallas kernels, kernel_call(): pl.pallas_call(body, out_shape=[jax.ShapeDtypeStruct(shape, kind) for sha...  103 us
    ppermute x67, starting transfers between devices, swap(): return lax.ppermute(value, GROUP, [(i, i ^ mask) for i in range(8)])  43.7 us
    all_to_all x4, waiting for transfers between devices, row_exchange(): return lax.all_to_all(parts, ROW, split_axis=0, concat_axis=0, tiled=True)  30.6 us
    all_to_all x1, blocking collectives, to_heads(): got = lax.all_to_all(send, GROUP, split_axis=0, concat_axis=0, tiled=True)  25 us
    reduce_scatter x3, waiting for transfers between devices, home(): return lax.psum_scatter(full, 'z', scatter_dimension=0, tiled=True)  19.7 us
    unnamed x78, local copies, waits for them, and re-layouts  16.6 us
    all_to_all x4, starting transfers between devices, row_exchange(): return lax.all_to_all(parts, ROW, split_axis=0, concat_axis=0, tiled=True)  14.5 us
  transfers between devices with their start and end apart: 83, of which 44 were waited for; matrix products, arithmetic and copies ran while one was open for 15% of the time, Pallas kernels for 15%

profile of v6, /device:TPU:0, one launch (start us, length us, event | category | flops | bytes accessed | tf_op | source)
XLA Modules:
  0.0 547.2 jit_solution(10333723417707562470)
XLA Ops:
  14.0 25.0 %all_to_all.40 = bf16[8,192,512]{2,1,0:T(8,128)(2,1)S(1)} all-to-all(bf16[8,192,512]{2,1,0:T(8,128)(2,1)S(1)} %pad_maximum_fusion), channel_id=1, replica_groups=mesh['x'=2,'k'=2,'z'=4,'y'=2] {'x','k','y'}, dimensions={0} | all-to-all | bytes 3145728 | tf_op jit(solution)/shard_map/all_to_all | solution.py:458
  52.0 14.3 %all-to-all-done.1 = bf16[4,2,128,512]{3,2,1,0:T(8,128)(2,1)S(1)} async-done(((bf16[4,2,128,512]{3,2,1,0:T(8,128)(2,1)}), bf16[4,2,128,512]{3,2,1,0:T(8,128)(2,1)S(1)}, u32[]{:S(2)}, u32[]{:S(2)}) %all-to-all-start.1) | async-done | bytes 1048608 | tf_op jit(solution)/shard_map/all_to_all | solution.py:93
  80.5 4.1 collective-permute-done.7
  84.6 10.1 %collective-permute-done.6 = bf16[128,2048]{1,0:T(8,128)(2,1)} collective-permute-done((bf16[128,2048]{1,0:T(8,128)(2,1)}, bf16[128,2048]{1,0:T(8,128)(2,1)}, u32[]{:S(2)}, u32[]{:S(2)}) %collective-permute-start.6) | collective-permute-done | bytes 524320 | tf_op jit(solution)/shard_map/ppermute | solution.py:29
  98.0 6.5 %all-to-all-done.2 = bf16[4,2,128,512]{3,2,1,0:T(8,128)(2,1)S(1)} async-done(((bf16[4,2,128,512]{3,2,1,0:T(8,128)(2,1)}), bf16[4,2,128,512]{3,2,1,0:T(8,128)(2,1)S(1)}, u32[]{:S(2)}, u32[]{:S(2)}) %all-to-all-start.2) | async-done | bytes 1048608 | tf_op jit(solution)/shard_map/all_to_all | solution.py:93
  127.4 25.0 %collective-permute-done.14.refs_13_ = bf16[128,2048]{1,0:T(8,128)(2,1)} collective-permute-done((bf16[128,2048]{1,0:T(8,128)(2,1)}, bf16[128,2048]{1,0:T(8,128)(2,1)}, u32[]{:S(2)}, u32[]{:S(2)}) %collective-permute-start.14) | collective-permute-done | bytes 524320 | tf_op jit(solution)/shard_map/ppermute | solution.py:29
  152.5 9.9 %collective-permute-done.13.refs_12_ = bf16[128,2048]{1,0:T(8,128)(2,1)} collective-permute-done((bf16[128,2048]{1,0:T(8,128)(2,1)}, bf16[128,2048]{1,0:T(8,128)(2,1)}, u32[]{:S(2)}, u32[]{:S(2)}) %collective-permute-start.13) | collective-permute-done | bytes 524320 | tf_op jit(solution)/shard_map/ppermute | solution.py:29
  170.6 9.2 %shard_map.237 = (bf16[256,1024]{1,0:T(8,128)(2,1)}, bf16[256,1024]{1,0:T(8,128)(2,1)}, bf16[1024,1024]{1,0:T(8,128)(2,1)}) custom-call(bf16[512,2048]{1,0:T(8,128)(2,1)} %bitcast.114, bf16[1024,2048]{1,0:T(8,128)(2,1)} %constant_dynamic-update-slice_fusion.1.x.x_in, s32[1024,1]{1,0:T(8,128)} %copy-done.6, s32[1,1024]{1,0:T(1,128)} %bitcast.171, ...), custom_call_target="tpu_custom_call" | custom-call | flops 2684354560 | bytes 9461760 | tf_op jit(solution)/shard_map/pallas_call | solution.py:156
  179.9 20.7 %shard_map.238 = (f32[512,1024]{1,0:T(8,128)}, bf16[512,1024]{1,0:T(8,128)(2,1)}, bf16[1024,2048]{1,0:T(8,128)(2,1)}, bf16[512,1024]{1,0:T(8,128)(2,1)}, f32[512,1024]{1,0:T(8,128)}, /*index=5*/f32[1,1024]{1,0:T(1,128)}) custom-call(bf16[1536,2048]{1,0:T(8,128)(2,1)} %all-gather.4.cloned.1.call-done.w.vgo, ...), custom_call_target="tpu_custom_call" | custom-call | flops 7516192768 | bytes 23072768 | tf_op jit(solution)/shard_map/pallas_call | solution.py:156
  208.3 6.6 %collective-permute-done.23 = bf16[64,2048]{1,0:T(8,128)(2,1)S(1)} collective-permute-done((bf16[64,2048]{1,0:T(8,128)(2,1)S(1)}, bf16[64,2048]{1,0:T(8,128)(2,1)S(1)}, u32[]{:S(2)}, u32[]{:S(2)}) %collective-permute-start.23) | collective-permute-done | bytes 262176 | tf_op jit(solution)/shard_map/ppermute | solution.py:29
  217.6 10.7 %collective-permute-done.24 = bf16[128,2048]{1,0:T(8,128)(2,1)S(1)} collective-permute-done((bf16[128,2048]{1,0:T(8,128)(2,1)S(1)}, bf16[128,2048]{1,0:T(8,128)(2,1)S(1)}, u32[]{:S(2)}, u32[]{:S(2)}) %collective-permute-start.24) | collective-permute-done | bytes 524320 | tf_op jit(solution)/shard_map/ppermute | solution.py:29
  234.7 12.3 %collective-permute-done.29.refs_5_ = bf16[128,2048]{1,0:T(8,128)(2,1)S(1)} collective-permute-done((bf16[128,2048]{1,0:T(8,128)(2,1)S(1)}, bf16[128,2048]{1,0:T(8,128)(2,1)S(1)}, u32[]{:S(2)}, u32[]{:S(2)}) %collective-permute-start.29) | collective-permute-done | bytes 524320 | tf_op jit(solution)/shard_map/ppermute | solution.py:29
  247.0 8.8 %collective-permute-done.28.refs_4_ = bf16[128,2048]{1,0:T(8,128)(2,1)S(1)} collective-permute-done((bf16[128,2048]{1,0:T(8,128)(2,1)S(1)}, bf16[128,2048]{1,0:T(8,128)(2,1)S(1)}, u32[]{:S(2)}, u32[]{:S(2)}) %collective-permute-start.28) | collective-permute-done | bytes 524320 | tf_op jit(solution)/shard_map/ppermute | solution.py:29
  258.8 20.4 %shard_map.239 = (bf16[512,1024]{1,0:T(8,128)(2,1)}, bf16[1024,2048]{1,0:T(8,128)(2,1)}, bf16[1024,2048]{1,0:T(8,128)(2,1)}) custom-call(bf16[1024,2048]{1,0:T(8,128)(2,1)} %all-gather.8.cloned.1.call-done.w, bf16[128,2048]{1,0:T(8,128)(2,1)} %copy-done.12, bf16[128,2048]{1,0:T(8,128)(2,1)} %collective-permute-done.25.refs_1_, ...), custom_call_target="tpu_custom_call" | custom-call | flops 10737418240 | bytes 22020096 | tf_op jit(solution)/shard_map/pallas_call | solution.py:156
  288.0 5.7 %collective-permute-done.38 = bf16[64,2048]{1,0:T(8,128)(2,1)S(1)} collective-permute-done((bf16[64,2048]{1,0:T(8,128)(2,1)S(1)}, bf16[64,2048]{1,0:T(8,128)(2,1)S(1)}, u32[]{:S(2)}, u32[]{:S(2)}) %collective-permute-start.38) | collective-permute-done | bytes 262176 | tf_op jit(solution)/shard_map/ppermute | solution.py:29
  296.6 10.6 %collective-permute-done.39 = bf16[128,2048]{1,0:T(8,128)(2,1)S(1)} collective-permute-done((bf16[128,2048]{1,0:T(8,128)(2,1)S(1)}, bf16[128,2048]{1,0:T(8,128)(2,1)S(1)}, u32[]{:S(2)}, u32[]{:S(2)}) %collective-permute-start.39) | collective-permute-done | bytes 524320 | tf_op jit(solution)/shard_map/ppermute | solution.py:29
  316.6 12.3 %collective-permute-done.44.refs_5_ = bf16[128,2048]{1,0:T(8,128)(2,1)S(1)} collective-permute-done((bf16[128,2048]{1,0:T(8,128)(2,1)S(1)}, bf16[128,2048]{1,0:T(8,128)(2,1)S(1)}, u32[]{:S(2)}, u32[]{:S(2)}) %collective-permute-start.44) | collective-permute-done | bytes 524320 | tf_op jit(solution)/shard_map/ppermute | solution.py:29
  328.9 8.6 %collective-permute-done.43.refs_4_ = bf16[128,2048]{1,0:T(8,128)(2,1)S(1)} collective-permute-done((bf16[128,2048]{1,0:T(8,128)(2,1)S(1)}, bf16[128,2048]{1,0:T(8,128)(2,1)S(1)}, u32[]{:S(2)}, u32[]{:S(2)}) %collective-permute-start.43) | collective-permute-done | bytes 524320 | tf_op jit(solution)/shard_map/ppermute | solution.py:29
  341.0 13.8 %shard_map.240 = (bf16[512,1024]{1,0:T(8,128)(2,1)}, bf16[512,1024]{1,0:T(8,128)(2,1)}, bf16[1024,2048]{1,0:T(8,128)(2,1)}) custom-call(bf16[1536,2048]{1,0:T(8,128)(2,1)} %all-gather.4.cloned.1.call-done.w.vgo, bf16[1024,2048]{1,0:T(8,128)(2,1)} %constant_dynamic-update-slice_fusion.1.x.x_in, bf16[128,2048]{1,0:T(8,128)(2,1)} %copy-done.13, ...), custom_call_target="tpu_custom_call" | custom-call | flops 6442450944 | bytes 26218496 | tf_op jit(solution)/shard_map/pallas_call | solution.py:156
  363.9 17.7 %shard_map.241 = (bf16[1024,1024]{1,0:T(8,128)(2,1)}, bf16[4,8,128,512]{3,2,1,0:T(8,128)(2,1)}) custom-call(bf16[256,1024]{1,0:T(8,128)(2,1)} %get-tuple-element.57.q, bf16[256,1024]{1,0:T(8,128)(2,1)} %get-tuple-element.58.k, bf16[512,1024]{1,0:T(8,128)(2,1)} %get-tuple-element.59.v, bf16[1024,1024]{1,0:T(8,128)(2,1)} %get-tuple-element.53.weights, ...), custom_call_target="tpu_custom_call" | custom-call | flops 7516192768 | bytes 15753216 | tf_op jit(solution)/shard_map/pallas_call | solution.py:156
  382.8 14.0 %shard_map.242 = bf16[1024,2048]{1,0:T(8,128)(2,1)} custom-call(bf16[1024,1024]{1,0:T(8,128)(2,1)} %get-tuple-element.65.packed, bf16[512,2048]{1,0:T(8,128)(2,1)} %bitcast.115, bf16[512,1024]{1,0:T(8,128)(2,1)} %get-tuple-element.69.ggate, bf16[1536,2048]{1,0:T(8,128)(2,1)} %all-gather.4.cloned.1.call-done.w.vgo), custom_call_target="tpu_custom_call" | custom-call | flops 6442450944 | bytes 15728640 | tf_op jit(solution)/shard_map/pallas_call | solution.py:156
  396.8 7.7 %shard_map.243 = bf16[1024,2048]{1,0:T(8,128)(2,1)} custom-call(bf16[1024,2048]{1,0:T(8,128)(2,1)} %all-gather.8.cloned.1.call-done.w, bf16[512,1024]{1,0:T(8,128)(2,1)} %get-tuple-element.71.act), custom_call_target="tpu_custom_call" | custom-call | flops 2147483648 | bytes 9437184 | tf_op jit(solution)/shard_map/pallas_call | solution.py:156
  419.9 3.9 collective-permute-done.61
  426.3 5.0 collective-permute-done.53
  436.0 4.4 collective-permute-done.62
  440.4 5.8 %collective-permute-done.59 = bf16[128,2048]{1,0:T(8,128)(2,1)S(1)} collective-permute-done((bf16[128,2048]{1,0:T(8,128)(2,1)S(1)}, bf16[128,2048]{1,0:T(8,128)(2,1)S(1)}, u32[]{:S(2)}, u32[]{:S(2)}) %collective-permute-start.59) | collective-permute-done | bytes 524320 | tf_op jit(solution)/shard_map/ppermute | solution.py:29
  450.8 4.2 collective-permute-done.51
  459.3 3.8 all-to-all-start.5
  468.2 9.8 %all-to-all-done.5 = bf16[4,2,128,512]{3,2,1,0:T(8,128)(2,1)S(1)} async-done(((bf16[4,2,128,512]{3,2,1,0:T(8,128)(2,1)}), bf16[4,2,128,512]{3,2,1,0:T(8,128)(2,1)S(1)}, u32[]{:S(2)}, u32[]{:S(2)}) %all-to-all-start.5) | async-done | bytes 1048608 | tf_op jit(solution)/shard_map/all_to_all | solution.py:93
  494.0 6.3 %collective-permute-done.68 = f32[4,2048]{1,0:T(4,128)S(1)} collective-permute-done((f32[4,2048]{1,0:T(4,128)S(1)}, f32[4,2048]{1,0:T(4,128)S(1)}, u32[]{:S(2)}, u32[]{:S(2)}) %collective-permute-start.68) | collective-permute-done | bytes 32800 | tf_op jit(solution)/shard_map/ppermute | solution.py:78
  500.3 17.6 %reduce-scatter.6.cloned.1.call-done = bf16[1,8,128,512]{3,2,1,0:T(8,128)(2,1)} async-done(((bf16[4,8,128,512]{3,2,1,0:T(8,128)(2,1)}), bf16[1,8,128,512]{3,2,1,0:T(8,128)(2,1)}) %reduce-scatter.6.cloned.1.call-update) | async-done | bytes 1048592 | tf_op jit(solution)/shard_map/reduce_scatter | solution.py:586
  525.3 10.8 %all-to-all-done.7 = bf16[8,128,512]{2,1,0:T(8,128)(2,1)S(1)} async-done(((bf16[8,128,512]{2,1,0:T(8,128)(2,1)}), bf16[8,128,512]{2,1,0:T(8,128)(2,1)S(1)}, u32[]{:S(2)}, u32[]{:S(2)}) %all-to-all-start.7) | async-done | bytes 1048608 | tf_op jit(solution)/shard_map/all_to_all | solution.py:673
  (354 shorter events, 186.1 us)
Async XLA Ops:
  7.2 100.0 %all-gather.6.cloned.1.call-start = ((), (), s32[]{:S(2)}) async-start(), calls=%async_computation.12 | async-start | bytes 2621440 | tf_op jit(solution)/shard_map/all_gather | solution.py:482
  10.8 169.1 %all-gather.4.cloned.1.call-start = ((), (), s32[]{:S(2)}) async-start(), calls=%async_computation.11 | async-start | bytes 7864320 | tf_op jit(solution)/shard_map/all_gather | solution.py:482
  68.7 26.1 %collective-permute-start.6 = (bf16[128,2048]{1,0:T(8,128)(2,1)}, bf16[128,2048]{1,0:T(8,128)(2,1)}, u32[]{:S(2)}, u32[]{:S(2)}) collective-permute-start(bf16[128,2048]{1,0:T(8,128)(2,1)} %get-tuple-element.90), channel_id=1, source_target_pairs={{0,16},{1,17},{8,24},{9,25},{16,0},{17,1},{24,8},{25,9},{2,18},{3,... | collective-permute-start | bytes 1572872 | tf_op jit(solution)/shard_map/ppermute | solution.py:29
  70.3 24.4 %collective-permute-start.3 = (bf16[128,2048]{1,0:T(8,128)(2,1)}, bf16[128,2048]{1,0:T(8,128)(2,1)}, u32[]{:S(2)}, u32[]{:S(2)}) collective-permute-start(bf16[128,2048]{1,0:T(8,128)(2,1)} %get-tuple-element.90), channel_id=1, source_target_pairs={{0,1},{1,0},{8,9},{9,8},{16,17},{17,16},{24,25},{25,24},{2,3},{3,2... | collective-permute-start | bytes 1572872 | tf_op jit(solution)/shard_map/ppermute | solution.py:29
  74.4 30.0 %all-to-all-start.2 = ((bf16[4,2,128,512]{3,2,1,0:T(8,128)(2,1)}), bf16[4,2,128,512]{3,2,1,0:T(8,128)(2,1)S(1)}, u32[]{:S(2)}, u32[]{:S(2)}) async-start(bf16[4,2,128,512]{3,2,1,0:T(8,128)(2,1)} %pad_maximum_fusion.2), calls=%async_computation.2 | async-start | bytes 2097152 | tf_op jit(solution)/shard_map/all_to_all | solution.py:93
  84.6 36.0 %collective-permute-start.9 = (bf16[128,2048]{1,0:T(8,128)(2,1)S(1)}, bf16[128,2048]{1,0:T(8,128)(2,1)}, u32[]{:S(2)}, u32[]{:S(2)}) collective-permute-start(bf16[128,2048]{1,0:T(8,128)(2,1)S(1)} %collective-permute-done.7), channel_id=1, source_target_pairs={{0,8},{1,9},{8,0},{9,1},{16,24},{17,25},{24,16},{25,17},{2,10},{3,... | collective-permute-start | bytes 1572872 | tf_op jit(solution)/shard_map/ppermute | solution.py:29
  94.7 24.0 %collective-permute-start.8 = (bf16[128,2048]{1,0:T(8,128)(2,1)}, bf16[128,2048]{1,0:T(8,128)(2,1)}, u32[]{:S(2)}, u32[]{:S(2)}) collective-permute-start(bf16[128,2048]{1,0:T(8,128)(2,1)} %collective-permute-done.6), channel_id=1, source_target_pairs={{0,8},{1,9},{8,0},{9,1},{16,24},{17,25},{24,16},{25,17},{2,10},{3,... | collective-permute-start | bytes 1572872 | tf_op jit(solution)/shard_map/ppermute | solution.py:29
  94.7 19.3 %collective-permute-start.5 = (bf16[128,2048]{1,0:T(8,128)(2,1)}, bf16[128,2048]{1,0:T(8,128)(2,1)}, u32[]{:S(2)}, u32[]{:S(2)}) collective-permute-start(bf16[128,2048]{1,0:T(8,128)(2,1)} %collective-permute-done.3), channel_id=1, source_target_pairs={{0,8},{1,9},{8,0},{9,1},{16,24},{17,25},{24,16},{25,17},{2,10},{3,... | collective-permute-start | bytes 1572872 | tf_op jit(solution)/shard_map/ppermute | solution.py:29
  110.4 56.4 %all-to-all-start.3 = ((bf16[8,4,64,512]{3,2,1,0:T(8,128)(2,1)}), bf16[8,4,64,512]{3,2,1,0:T(8,128)(2,1)S(1)}, u32[]{:S(2)}, u32[]{:S(2)}) async-start(bf16[8,4,64,512]{3,2,1,0:T(8,128)(2,1)} %copy.116), calls=%async_computation.3 | async-start | bytes 4194304 | tf_op jit(solution)/shard_map/all_to_all | solution.py:532
  114.0 142.4 %all-gather.8.cloned.1.call-start = ((), (), s32[]{:S(2)}) async-start(), calls=%async_computation.13 | async-start | bytes 5242880 | tf_op jit(solution)/shard_map/all_gather | solution.py:482
  122.5 30.0 %collective-permute-start.14 = (bf16[128,2048]{1,0:T(8,128)(2,1)}, bf16[128,2048]{1,0:T(8,128)(2,1)}, u32[]{:S(2)}, u32[]{:S(2)}) collective-permute-start(bf16[128,2048]{1,0:T(8,128)(2,1)} %bitcast.68.refs_8_), channel_id=1, source_target_pairs={{0,17},{1,16},{8,25},{9,24},{16,1},{17,0},{24,9},{25,8},{2,19},{3,... | collective-permute-start | bytes 1572872 | tf_op jit(solution)/shard_map/ppermute | solution.py:29
  125.3 37.0 %collective-permute-start.13 = (bf16[128,2048]{1,0:T(8,128)(2,1)}, bf16[128,2048]{1,0:T(8,128)(2,1)}, u32[]{:S(2)}, u32[]{:S(2)}) collective-permute-start(bf16[128,2048]{1,0:T(8,128)(2,1)} %bitcast.68.refs_8_), channel_id=1, source_target_pairs={{0,16},{1,17},{8,24},{9,25},{16,0},{17,1},{24,8},{25,9},{2,18},{3,... | collective-permute-start | bytes 1572872 | tf_op jit(solution)/shard_map/ppermute | solution.py:29
  125.8 36.5 %collective-permute-start.10 = (bf16[128,2048]{1,0:T(8,128)(2,1)}, bf16[128,2048]{1,0:T(8,128)(2,1)}, u32[]{:S(2)}, u32[]{:S(2)}) collective-permute-start(bf16[128,2048]{1,0:T(8,128)(2,1)} %bitcast.68.refs_8_), channel_id=1, source_target_pairs={{0,1},{1,0},{8,9},{9,8},{16,17},{17,16},{24,25},{25,24},{2,3},{3,2... | collective-permute-start | bytes 1572872 | tf_op jit(solution)/shard_map/ppermute | solution.py:29
  127.3 52.5 %collective-permute-start.11 = (bf16[128,2048]{1,0:T(8,128)(2,1)}, bf16[128,2048]{1,0:T(8,128)(2,1)}, u32[]{:S(2)}, u32[]{:S(2)}) collective-permute-start(bf16[128,2048]{1,0:T(8,128)(2,1)} %bitcast.68.refs_8_), channel_id=1, source_target_pairs={{0,8},{1,9},{8,0},{9,1},{16,24},{17,25},{24,16},{25,17},{2,10},{3,... | collective-permute-start | bytes 1572872 | tf_op jit(solution)/shard_map/ppermute | solution.py:29
  152.5 27.4 %collective-permute-start.16 = (bf16[128,2048]{1,0:T(8,128)(2,1)}, bf16[128,2048]{1,0:T(8,128)(2,1)}, u32[]{:S(2)}, u32[]{:S(2)}) collective-permute-start(bf16[128,2048]{1,0:T(8,128)(2,1)} %collective-permute-done.14.refs_13_), channel_id=1, source_target_pairs={{0,8},{1,9},{8,0},{9,1},{16,24},{17,25},{24,16},{25,17},{2,10},{3,... | collective-permute-start | bytes 1572872 | tf_op jit(solution)/shard_map/ppermute | solution.py:29
  166.3 190.6 %reduce-scatter.4.cloned.1.call-start = ((), (), s32[]{:S(2)}) async-start(), calls=%async_computation.14 | async-start | bytes 5242880 | tf_op jit(solution)/shard_map/reduce_scatter | solution.py:586
  233.3 22.5 %collective-permute-start.28 = (bf16[128,2048]{1,0:T(8,128)(2,1)S(1)}, bf16[128,2048]{1,0:T(8,128)(2,1)S(1)}, u32[]{:S(2)}, u32[]{:S(2)}) collective-permute-start(bf16[128,2048]{1,0:T(8,128)(2,1)S(1)} %add_convert_fusion.4.refs_0_), channel_id=1, source_target_pairs={{0,16},{1,17},{8,24},{9,25},{16,0},{17,1},{24,8},{25,9},{2,18},{3,... | collective-permute-start | bytes 1572872 | tf_op jit(solution)/shard_map/ppermute | solution.py:29
  233.6 22.4 %collective-permute-start.25 = (bf16[128,2048]{1,0:T(8,128)(2,1)S(1)}, bf16[128,2048]{1,0:T(8,128)(2,1)}, u32[]{:S(2)}, u32[]{:S(2)}) collective-permute-start(bf16[128,2048]{1,0:T(8,128)(2,1)S(1)} %add_convert_fusion.4.refs_0_), channel_id=1, source_target_pairs={{0,1},{1,0},{8,9},{9,8},{16,17},{17,16},{24,25},{25,24},{2,3},{3,2... | collective-permute-start | bytes 1572872 | tf_op jit(solution)/shard_map/ppermute | solution.py:29
  234.6 21.8 %collective-permute-start.26 = (bf16[128,2048]{1,0:T(8,128)(2,1)S(1)}, bf16[128,2048]{1,0:T(8,128)(2,1)}, u32[]{:S(2)}, u32[]{:S(2)}) collective-permute-start(bf16[128,2048]{1,0:T(8,128)(2,1)S(1)} %add_convert_fusion.4.refs_0_), channel_id=1, source_target_pairs={{0,8},{1,9},{8,0},{9,1},{16,24},{17,25},{24,16},{25,17},{2,10},{3,... | collective-permute-start | bytes 1572872 | tf_op jit(solution)/shard_map/ppermute | solution.py:29
  279.2 200.8 %reduce-scatter.8.cloned.1.call-start = ((), (), s32[]{:S(2)}) async-start(), calls=%async_computation.16 | async-start | bytes 5242880 | tf_op jit(solution)/shard_map/reduce_scatter | solution.py:586
  313.7 23.8 %collective-permute-start.43 = (bf16[128,2048]{1,0:T(8,128)(2,1)S(1)}, bf16[128,2048]{1,0:T(8,128)(2,1)S(1)}, u32[]{:S(2)}, u32[]{:S(2)}) collective-permute-start(bf16[128,2048]{1,0:T(8,128)(2,1)S(1)} %get-tuple-element.84.refs_0_), channel_id=1, source_target_pairs={{0,16},{1,17},{8,24},{9,25},{16,0},{17,1},{24,8},{25,9},{2,18},{3,... | collective-permute-start | bytes 1572872 | tf_op jit(solution)/shard_map/ppermute | solution.py:29
  315.4 22.8 %collective-permute-start.40 = (bf16[128,2048]{1,0:T(8,128)(2,1)S(1)}, bf16[128,2048]{1,0:T(8,128)(2,1)S(1)}, u32[]{:S(2)}, u32[]{:S(2)}) collective-permute-start(bf16[128,2048]{1,0:T(8,128)(2,1)S(1)} %get-tuple-element.84.refs_0_), channel_id=1, source_target_pairs={{0,1},{1,0},{8,9},{9,8},{16,17},{17,16},{24,25},{25,24},{2,3},{3,2... | collective-permute-start | bytes 1572872 | tf_op jit(solution)/shard_map/ppermute | solution.py:29
  316.6 21.7 %collective-permute-start.41 = (bf16[128,2048]{1,0:T(8,128)(2,1)S(1)}, bf16[128,2048]{1,0:T(8,128)(2,1)S(1)}, u32[]{:S(2)}, u32[]{:S(2)}) collective-permute-start(bf16[128,2048]{1,0:T(8,128)(2,1)S(1)} %get-tuple-element.84.refs_0_), channel_id=1, source_target_pairs={{0,8},{1,9},{8,0},{9,1},{16,24},{17,25},{24,16},{25,17},{2,10},{3,... | collective-permute-start | bytes 1572872 | tf_op jit(solution)/shard_map/ppermute | solution.py:29
  360.2 21.5 %all-to-all-start.4 = ((bf16[4,2,128,512]{3,2,1,0:T(8,128)(2,1)}), bf16[4,2,128,512]{3,2,1,0:T(8,128)(2,1)S(1)}, u32[]{:S(2)}, u32[]{:S(2)}) async-start(bf16[4,2,128,512]{3,2,1,0:T(8,128)(2,1)} %maximum_bitcast_fusion), calls=%async_computation.5 | async-start | bytes 2097152 | tf_op jit(solution)/shard_map/all_to_all | solution.py:93
  363.7 154.3 %reduce-scatter.6.cloned.1.call-start = ((), (), s32[]{:S(2)}) async-start(), calls=%async_computation.15 | async-start | bytes 5242880 | tf_op jit(solution)/shard_map/reduce_scatter | solution.py:586
  408.1 27.3 %collective-permute-start.55 = (bf16[128,2048]{1,0:T(8,128)(2,1)S(1)}, bf16[128,2048]{1,0:T(8,128)(2,1)S(1)}, u32[]{:S(2)}, u32[]{:S(2)}) collective-permute-start(bf16[128,2048]{1,0:T(8,128)(2,1)S(1)} %get-tuple-element.98), channel_id=1, source_target_pairs={{0,8},{1,9},{8,0},{9,1},{16,24},{17,25},{24,16},{25,17},{2,10},{3,... | collective-permute-start | bytes 1572872 | tf_op jit(solution)/shard_map/ppermute | solution.py:29
  410.8 36.2 %collective-permute-start.47 = (bf16[128,2048]{1,0:T(8,128)(2,1)}, bf16[128,2048]{1,0:T(8,128)(2,1)}, u32[]{:S(2)}, u32[]{:S(2)}) collective-permute-start(bf16[128,2048]{1,0:T(8,128)(2,1)} %get-tuple-element.91), channel_id=1, source_target_pairs={{0,8},{1,9},{8,0},{9,1},{16,24},{17,25},{24,16},{25,17},{2,10},{3,... | collective-permute-start | bytes 1572872 | tf_op jit(solution)/shard_map/ppermute | solution.py:29
  435.3 19.7 %collective-permute-start.51 = (bf16[128,2048]{1,0:T(8,128)(2,1)}, bf16[128,2048]{1,0:T(8,128)(2,1)}, u32[]{:S(2)}, u32[]{:S(2)}) collective-permute-start(bf16[128,2048]{1,0:T(8,128)(2,1)} %pad_maximum_fusion.9), channel_id=1, source_target_pairs={{0,16},{1,17},{8,24},{9,25},{16,0},{17,1},{24,8},{25,9},{2,18},{3,... | collective-permute-start | bytes 1572872 | tf_op jit(solution)/shard_map/ppermute | solution.py:29
  464.7 23.1 %collective-permute-start.65 = (f32[4,2048]{1,0:T(4,128)S(1)}, f32[4,2048]{1,0:T(4,128)S(1)}, u32[]{:S(2)}, u32[]{:S(2)}) collective-permute-start(f32[4,2048]{1,0:T(4,128)S(1)} %fusion.61), channel_id=1, source_target_pairs={{0,16},{1,17},{8,24},{9,25},{16,0},{17,1},{24,8},{25,9},{2,18},{3,... | collective-permute-start | bytes 98312 | tf_op jit(solution)/shard_map/ppermute | solution.py:29
  466.5 21.3 %collective-permute-start.66 = (f32[4,2048]{1,0:T(4,128)S(1)}, f32[4,2048]{1,0:T(4,128)S(1)}, u32[]{:S(2)}, u32[]{:S(2)}) collective-permute-start(f32[4,2048]{1,0:T(4,128)S(1)} %fusion.61), channel_id=1, source_target_pairs={{0,17},{1,16},{8,25},{9,24},{16,1},{17,0},{24,9},{25,8},{2,19},{3,... | collective-permute-start | bytes 98312 | tf_op jit(solution)/shard_map/ppermute | solution.py:29
  467.3 20.5 %collective-permute-start.64 = (f32[4,2048]{1,0:T(4,128)S(1)}, f32[4,2048]{1,0:T(4,128)S(1)}, u32[]{:S(2)}, u32[]{:S(2)}) collective-permute-start(f32[4,2048]{1,0:T(4,128)S(1)} %fusion.61), channel_id=1, source_target_pairs={{0,1},{1,0},{8,9},{9,8},{16,17},{17,16},{24,25},{25,24},{2,3},{3,2... | collective-permute-start | bytes 98312 | tf_op jit(solution)/shard_map/ppermute | solution.py:29
  483.1 34.9 %all-to-all-start.6 = ((bf16[8,128,512]{2,1,0:T(8,128)(2,1)}), bf16[8,128,512]{2,1,0:T(8,128)(2,1)S(1)}, u32[]{:S(2)}, u32[]{:S(2)}) async-start(bf16[8,128,512]{2,1,0:T(8,128)(2,1)} %bitcast.43), calls=%async_computation.9 | async-start | bytes 2097152 | tf_op jit(solution)/shard_map/all_to_all | solution.py:664
  (82 other events, 783.1 us)
Sparse Core Ops, SparseCore 0:
  10.9 48.6 all-gather.5
  61.2 114.0 all-gather.3
  177.4 78.9 all-gather.7
  279.3 77.4 reduce-scatter.3
  359.1 77.2 reduce-scatter.7
  438.6 79.3 reduce-scatter.5

commit v7 on v6

--- a/solution.py
+++ b/solution.py
@@ -296,12 +296,21 @@
     sent += move.kind(gu, grads_out, ("to", 0, 2), depth)
     spans(x.shape[1], WIDE, down_step)
     sent += move.kind(gd, grads_out, ("to", 1, 2), depth)
-    def back_step(at):
+    tiles, base = x.shape[1] // WIDE, move.count
+
+    def back_copy(i, at):
+        return pltpu.make_async_copy(
+            back.at[:, at], back_out.at[:, at], semaphores.at[base + i]
+        )
+
+    def back_step(i, carry):
+        at = pl.ds(pl.multiple_of(i * WIDE, WIDE), WIDE)
         back[:, at] = dot(turned[...], wu[:, at], ((1,), (0,))).astype(BF16)
-
-    spans(x.shape[1], WIDE, back_step)
-    sent.append(move.start(back, back_out))
-    wait(sent)
+        back_copy(i, at).start()
+        return carry
+
+    lax.fori_loop(0, tiles, back_step, 0)
+    wait(sent + [back_copy(i, pl.ds(i * WIDE, WIDE)) for i in range(tiles)])
 
 
 def down_forward(depth, w, act, out, wd):
@@ -578,7 +587,7 @@
         *x_two,
         after(cot[0], token),
         *cot[1:],
-        copies=4 * depth + 18,
+        copies=4 * depth + 17 + width // WIDE,
     )
     grad_two = group_reduce(two_part)
 

time: 556 us -> 555 us (level)
  no operation moved by 1% of the time
where the time goes in v7:
time: 555 us; the launch traced here: 546 us
  waiting for transfers between devices  239 us (43%)
  Pallas kernels  103 us (19%)
  starting transfers between devices  75.2 us (14%)
  local copies, waits for them, and re-layouts  46.5 us (8%)
  other arithmetic  30.3 us (5%)
  blocking collectives  25 us (5%)
  between operations  15.6 us (3%)
  matrix products  12.5 us (2%)
    ppermute x67, waiting for transfers between devices, swap(): return lax.ppermute(value, GROUP, [(i, i ^ mask) for i in range(8)])  171 us
    pallas_call x7, Pallas kernels, kernel_call(): pl.pallas_call(body, out_shape=[jax.ShapeDtypeStruct(shape, kind) for sha...  103 us
    ppermute x67, starting transfers between devices, swap(): return lax.ppermute(value, GROUP, [(i, i ^ mask) for i in range(8)])  43.7 us
    all_to_all x4, waiting for transfers between devices, row_exchange(): return lax.all_to_all(parts, ROW, split_axis=0, concat_axis=0, tiled=True)  30.6 us
    all_to_all x1, blocking collectives, to_heads(): got = lax.all_to_all(send, GROUP, split_axis=0, concat_axis=0, tiled=True)  25 us
    reduce_scatter x3, waiting for transfers between devices, home(): return lax.psum_scatter(full, 'z', scatter_dimension=0, tiled=True)  19.7 us
    unnamed x78, local copies, waits for them, and re-layouts  16.6 us
    all_to_all x4, starting transfers between devices, row_exchange(): return lax.all_to_all(parts, ROW, split_axis=0, concat_axis=0, tiled=True)  14.5 us
  transfers between devices with their start and end apart: 83, of which 44 were waited for; matrix products, arithmetic and copies ran while one was open for 15% of the time, Pallas kernels for 15%

profile of v7, /device:TPU:0, one launch (start us, length us, event | category | flops | bytes accessed | tf_op | source)
XLA Modules:
  0.0 546.3 jit_solution(7470640856954687819)
XLA Ops:
  14.0 25.0 %all_to_all.40 = bf16[8,192,512]{2,1,0:T(8,128)(2,1)S(1)} all-to-all(bf16[8,192,512]{2,1,0:T(8,128)(2,1)S(1)} %pad_maximum_fusion), channel_id=1, replica_groups=mesh['x'=2,'k'=2,'z'=4,'y'=2] {'x','k','y'}, dimensions={0} | all-to-all | bytes 3145728 | tf_op jit(solution)/shard_map/all_to_all | solution.py:467
  52.0 14.3 %all-to-all-done.1 = bf16[4,2,128,512]{3,2,1,0:T(8,128)(2,1)S(1)} async-done(((bf16[4,2,128,512]{3,2,1,0:T(8,128)(2,1)}), bf16[4,2,128,512]{3,2,1,0:T(8,128)(2,1)S(1)}, u32[]{:S(2)}, u32[]{:S(2)}) %all-to-all-start.1) | async-done | bytes 1048608 | tf_op jit(solution)/shard_map/all_to_all | solution.py:93
  80.5 4.1 collective-permute-done.7
  84.6 10.1 %collective-permute-done.6 = bf16[128,2048]{1,0:T(8,128)(2,1)} collective-permute-done((bf16[128,2048]{1,0:T(8,128)(2,1)}, bf16[128,2048]{1,0:T(8,128)(2,1)}, u32[]{:S(2)}, u32[]{:S(2)}) %collective-permute-start.6) | collective-permute-done | bytes 524320 | tf_op jit(solution)/shard_map/ppermute | solution.py:29
  98.0 6.5 %all-to-all-done.2 = bf16[4,2,128,512]{3,2,1,0:T(8,128)(2,1)S(1)} async-done(((bf16[4,2,128,512]{3,2,1,0:T(8,128)(2,1)}), bf16[4,2,128,512]{3,2,1,0:T(8,128)(2,1)S(1)}, u32[]{:S(2)}, u32[]{:S(2)}) %all-to-all-start.2) | async-done | bytes 1048608 | tf_op jit(solution)/shard_map/all_to_all | solution.py:93
  127.4 25.0 %collective-permute-done.14.refs_13_ = bf16[128,2048]{1,0:T(8,128)(2,1)} collective-permute-done((bf16[128,2048]{1,0:T(8,128)(2,1)}, bf16[128,2048]{1,0:T(8,128)(2,1)}, u32[]{:S(2)}, u32[]{:S(2)}) %collective-permute-start.14) | collective-permute-done | bytes 524320 | tf_op jit(solution)/shard_map/ppermute | solution.py:29
  152.5 9.9 %collective-permute-done.13.refs_12_ = bf16[128,2048]{1,0:T(8,128)(2,1)} collective-permute-done((bf16[128,2048]{1,0:T(8,128)(2,1)}, bf16[128,2048]{1,0:T(8,128)(2,1)}, u32[]{:S(2)}, u32[]{:S(2)}) %collective-permute-start.13) | collective-permute-done | bytes 524320 | tf_op jit(solution)/shard_map/ppermute | solution.py:29
  170.6 9.2 %shard_map.237 = (bf16[256,1024]{1,0:T(8,128)(2,1)}, bf16[256,1024]{1,0:T(8,128)(2,1)}, bf16[1024,1024]{1,0:T(8,128)(2,1)}) custom-call(bf16[512,2048]{1,0:T(8,128)(2,1)} %bitcast.114, bf16[1024,2048]{1,0:T(8,128)(2,1)} %constant_dynamic-update-slice_fusion.1.x.x_in, s32[1024,1]{1,0:T(8,128)} %copy-done.6, s32[1,1024]{1,0:T(1,128)} %bitcast.171, ...), custom_call_target="tpu_custom_call" | custom-call | flops 2684354560 | bytes 9461760 | tf_op jit(solution)/shard_map/pallas_call | solution.py:156
  179.9 20.7 %shard_map.238 = (f32[512,1024]{1,0:T(8,128)}, bf16[512,1024]{1,0:T(8,128)(2,1)}, bf16[1024,2048]{1,0:T(8,128)(2,1)}, bf16[512,1024]{1,0:T(8,128)(2,1)}, f32[512,1024]{1,0:T(8,128)}, /*index=5*/f32[1,1024]{1,0:T(1,128)}) custom-call(bf16[1536,2048]{1,0:T(8,128)(2,1)} %all-gather.4.cloned.1.call-done.w.vgo, ...), custom_call_target="tpu_custom_call" | custom-call | flops 7516192768 | bytes 23072768 | tf_op jit(solution)/shard_map/pallas_call | solution.py:156
  208.3 6.6 %collective-permute-done.23 = bf16[64,2048]{1,0:T(8,128)(2,1)S(1)} collective-permute-done((bf16[64,2048]{1,0:T(8,128)(2,1)S(1)}, bf16[64,2048]{1,0:T(8,128)(2,1)S(1)}, u32[]{:S(2)}, u32[]{:S(2)}) %collective-permute-start.23) | collective-permute-done | bytes 262176 | tf_op jit(solution)/shard_map/ppermute | solution.py:29
  217.6 10.7 %collective-permute-done.24 = bf16[128,2048]{1,0:T(8,128)(2,1)S(1)} collective-permute-done((bf16[128,2048]{1,0:T(8,128)(2,1)S(1)}, bf16[128,2048]{1,0:T(8,128)(2,1)S(1)}, u32[]{:S(2)}, u32[]{:S(2)}) %collective-permute-start.24) | collective-permute-done | bytes 524320 | tf_op jit(solution)/shard_map/ppermute | solution.py:29
  234.7 12.3 %collective-permute-done.29.refs_5_ = bf16[128,2048]{1,0:T(8,128)(2,1)S(1)} collective-permute-done((bf16[128,2048]{1,0:T(8,128)(2,1)S(1)}, bf16[128,2048]{1,0:T(8,128)(2,1)S(1)}, u32[]{:S(2)}, u32[]{:S(2)}) %collective-permute-start.29) | collective-permute-done | bytes 524320 | tf_op jit(solution)/shard_map/ppermute | solution.py:29
  247.0 8.8 %collective-permute-done.28.refs_4_ = bf16[128,2048]{1,0:T(8,128)(2,1)S(1)} collective-permute-done((bf16[128,2048]{1,0:T(8,128)(2,1)S(1)}, bf16[128,2048]{1,0:T(8,128)(2,1)S(1)}, u32[]{:S(2)}, u32[]{:S(2)}) %collective-permute-start.28) | collective-permute-done | bytes 524320 | tf_op jit(solution)/shard_map/ppermute | solution.py:29
  258.8 19.5 %shard_map.239 = (bf16[512,1024]{1,0:T(8,128)(2,1)}, bf16[1024,2048]{1,0:T(8,128)(2,1)}, bf16[1024,2048]{1,0:T(8,128)(2,1)}) custom-call(bf16[1024,2048]{1,0:T(8,128)(2,1)} %all-gather.8.cloned.1.call-done.w, bf16[128,2048]{1,0:T(8,128)(2,1)} %copy-done.12, bf16[128,2048]{1,0:T(8,128)(2,1)} %collective-permute-done.25.refs_1_, ...), custom_call_target="tpu_custom_call" | custom-call | flops 10737418240 | bytes 22020096 | tf_op jit(solution)/shard_map/pallas_call | solution.py:156
  287.2 5.7 %collective-permute-done.38 = bf16[64,2048]{1,0:T(8,128)(2,1)S(1)} collective-permute-done((bf16[64,2048]{1,0:T(8,128)(2,1)S(1)}, bf16[64,2048]{1,0:T(8,128)(2,1)S(1)}, u32[]{:S(2)}, u32[]{:S(2)}) %collective-permute-start.38) | collective-permute-done | bytes 262176 | tf_op jit(solution)/shard_map/ppermute | solution.py:29
  295.7 10.6 %collective-permute-done.39 = bf16[128,2048]{1,0:T(8,128)(2,1)S(1)} collective-permute-done((bf16[128,2048]{1,0:T(8,128)(2,1)S(1)}, bf16[128,2048]{1,0:T(8,128)(2,1)S(1)}, u32[]{:S(2)}, u32[]{:S(2)}) %collective-permute-start.39) | collective-permute-done | bytes 524320 | tf_op jit(solution)/shard_map/ppermute | solution.py:29
  315.7 12.3 %collective-permute-done.44.refs_5_ = bf16[128,2048]{1,0:T(8,128)(2,1)S(1)} collective-permute-done((bf16[128,2048]{1,0:T(8,128)(2,1)S(1)}, bf16[128,2048]{1,0:T(8,128)(2,1)S(1)}, u32[]{:S(2)}, u32[]{:S(2)}) %collective-permute-start.44) | collective-permute-done | bytes 524320 | tf_op jit(solution)/shard_map/ppermute | solution.py:29
  328.1 8.6 %collective-permute-done.43.refs_4_ = bf16[128,2048]{1,0:T(8,128)(2,1)S(1)} collective-permute-done((bf16[128,2048]{1,0:T(8,128)(2,1)S(1)}, bf16[128,2048]{1,0:T(8,128)(2,1)S(1)}, u32[]{:S(2)}, u32[]{:S(2)}) %collective-permute-start.43) | collective-permute-done | bytes 524320 | tf_op jit(solution)/shard_map/ppermute | solution.py:29
  340.1 13.8 %shard_map.240 = (bf16[512,1024]{1,0:T(8,128)(2,1)}, bf16[512,1024]{1,0:T(8,128)(2,1)}, bf16[1024,2048]{1,0:T(8,128)(2,1)}) custom-call(bf16[1536,2048]{1,0:T(8,128)(2,1)} %all-gather.4.cloned.1.call-done.w.vgo, bf16[1024,2048]{1,0:T(8,128)(2,1)} %constant_dynamic-update-slice_fusion.1.x.x_in, bf16[128,2048]{1,0:T(8,128)(2,1)} %copy-done.13, ...), custom_call_target="tpu_custom_call" | custom-call | flops 6442450944 | bytes 26218496 | tf_op jit(solution)/shard_map/pallas_call | solution.py:156
  363.1 17.7 %shard_map.241 = (bf16[1024,1024]{1,0:T(8,128)(2,1)}, bf16[4,8,128,512]{3,2,1,0:T(8,128)(2,1)}) custom-call(bf16[256,1024]{1,0:T(8,128)(2,1)} %get-tuple-element.57.q, bf16[256,1024]{1,0:T(8,128)(2,1)} %get-tuple-element.58.k, bf16[512,1024]{1,0:T(8,128)(2,1)} %get-tuple-element.59.v, bf16[1024,1024]{1,0:T(8,128)(2,1)} %get-tuple-element.53.weights, ...), custom_call_target="tpu_custom_call" | custom-call | flops 7516192768 | bytes 15753216 | tf_op jit(solution)/shard_map/pallas_call | solution.py:156
  381.9 14.0 %shard_map.242 = bf16[1024,2048]{1,0:T(8,128)(2,1)} custom-call(bf16[1024,1024]{1,0:T(8,128)(2,1)} %get-tuple-element.65.packed, bf16[512,2048]{1,0:T(8,128)(2,1)} %bitcast.115, bf16[512,1024]{1,0:T(8,128)(2,1)} %get-tuple-element.69.ggate, bf16[1536,2048]{1,0:T(8,128)(2,1)} %all-gather.4.cloned.1.call-done.w.vgo), custom_call_target="tpu_custom_call" | custom-call | flops 6442450944 | bytes 15728640 | tf_op jit(solution)/shard_map/pallas_call | solution.py:156
  395.9 7.7 %shard_map.243 = bf16[1024,2048]{1,0:T(8,128)(2,1)} custom-call(bf16[1024,2048]{1,0:T(8,128)(2,1)} %all-gather.8.cloned.1.call-done.w, bf16[512,1024]{1,0:T(8,128)(2,1)} %get-tuple-element.71.act), custom_call_target="tpu_custom_call" | custom-call | flops 2147483648 | bytes 9437184 | tf_op jit(solution)/shard_map/pallas_call | solution.py:156
  419.0 3.9 collective-permute-done.61
  425.5 5.0 collective-permute-done.53
  435.1 4.4 collective-permute-done.62
  439.5 5.7 %collective-permute-done.59 = bf16[128,2048]{1,0:T(8,128)(2,1)S(1)} collective-permute-done((bf16[128,2048]{1,0:T(8,128)(2,1)S(1)}, bf16[128,2048]{1,0:T(8,128)(2,1)S(1)}, u32[]{:S(2)}, u32[]{:S(2)}) %collective-permute-start.59) | collective-permute-done | bytes 524320 | tf_op jit(solution)/shard_map/ppermute | solution.py:29
  449.9 4.2 collective-permute-done.51
  458.4 3.8 all-to-all-start.5
  467.3 9.8 %all-to-all-done.5 = bf16[4,2,128,512]{3,2,1,0:T(8,128)(2,1)S(1)} async-done(((bf16[4,2,128,512]{3,2,1,0:T(8,128)(2,1)}), bf16[4,2,128,512]{3,2,1,0:T(8,128)(2,1)S(1)}, u32[]{:S(2)}, u32[]{:S(2)}) %all-to-all-start.5) | async-done | bytes 1048608 | tf_op jit(solution)/shard_map/all_to_all | solution.py:93
  493.1 6.3 %collective-permute-done.68 = f32[4,2048]{1,0:T(4,128)S(1)} collective-permute-done((f32[4,2048]{1,0:T(4,128)S(1)}, f32[4,2048]{1,0:T(4,128)S(1)}, u32[]{:S(2)}, u32[]{:S(2)}) %collective-permute-start.68) | collective-permute-done | bytes 32800 | tf_op jit(solution)/shard_map/ppermute | solution.py:78
  499.5 17.6 %reduce-scatter.6.cloned.1.call-done = bf16[1,8,128,512]{3,2,1,0:T(8,128)(2,1)} async-done(((bf16[4,8,128,512]{3,2,1,0:T(8,128)(2,1)}), bf16[1,8,128,512]{3,2,1,0:T(8,128)(2,1)}) %reduce-scatter.6.cloned.1.call-update) | async-done | bytes 1048592 | tf_op jit(solution)/shard_map/reduce_scatter | solution.py:595
  524.5 10.8 %all-to-all-done.7 = bf16[8,128,512]{2,1,0:T(8,128)(2,1)S(1)} async-done(((bf16[8,128,512]{2,1,0:T(8,128)(2,1)}), bf16[8,128,512]{2,1,0:T(8,128)(2,1)S(1)}, u32[]{:S(2)}, u32[]{:S(2)}) %all-to-all-start.7) | async-done | bytes 1048608 | tf_op jit(solution)/shard_map/all_to_all | solution.py:682
  (354 shorter events, 186.2 us)
Async XLA Ops:
  7.2 100.0 %all-gather.6.cloned.1.call-start = ((), (), s32[]{:S(2)}) async-start(), calls=%async_computation.12 | async-start | bytes 2621440 | tf_op jit(solution)/shard_map/all_gather | solution.py:491
  10.8 169.1 %all-gather.4.cloned.1.call-start = ((), (), s32[]{:S(2)}) async-start(), calls=%async_computation.11 | async-start | bytes 7864320 | tf_op jit(solution)/shard_map/all_gather | solution.py:491
  68.7 26.1 %collective-permute-start.6 = (bf16[128,2048]{1,0:T(8,128)(2,1)}, bf16[128,2048]{1,0:T(8,128)(2,1)}, u32[]{:S(2)}, u32[]{:S(2)}) collective-permute-start(bf16[128,2048]{1,0:T(8,128)(2,1)} %get-tuple-element.90), channel_id=1, source_target_pairs={{0,16},{1,17},{8,24},{9,25},{16,0},{17,1},{24,8},{25,9},{2,18},{3,... | collective-permute-start | bytes 1572872 | tf_op jit(solution)/shard_map/ppermute | solution.py:29
  70.3 24.4 %collective-permute-start.3 = (bf16[128,2048]{1,0:T(8,128)(2,1)}, bf16[128,2048]{1,0:T(8,128)(2,1)}, u32[]{:S(2)}, u32[]{:S(2)}) collective-permute-start(bf16[128,2048]{1,0:T(8,128)(2,1)} %get-tuple-element.90), channel_id=1, source_target_pairs={{0,1},{1,0},{8,9},{9,8},{16,17},{17,16},{24,25},{25,24},{2,3},{3,2... | collective-permute-start | bytes 1572872 | tf_op jit(solution)/shard_map/ppermute | solution.py:29
  74.4 30.0 %all-to-all-start.2 = ((bf16[4,2,128,512]{3,2,1,0:T(8,128)(2,1)}), bf16[4,2,128,512]{3,2,1,0:T(8,128)(2,1)S(1)}, u32[]{:S(2)}, u32[]{:S(2)}) async-start(bf16[4,2,128,512]{3,2,1,0:T(8,128)(2,1)} %pad_maximum_fusion.2), calls=%async_computation.2 | async-start | bytes 2097152 | tf_op jit(solution)/shard_map/all_to_all | solution.py:93
  84.6 36.0 %collective-permute-start.9 = (bf16[128,2048]{1,0:T(8,128)(2,1)S(1)}, bf16[128,2048]{1,0:T(8,128)(2,1)}, u32[]{:S(2)}, u32[]{:S(2)}) collective-permute-start(bf16[128,2048]{1,0:T(8,128)(2,1)S(1)} %collective-permute-done.7), channel_id=1, source_target_pairs={{0,8},{1,9},{8,0},{9,1},{16,24},{17,25},{24,16},{25,17},{2,10},{3,... | collective-permute-start | bytes 1572872 | tf_op jit(solution)/shard_map/ppermute | solution.py:29
  94.7 24.0 %collective-permute-start.8 = (bf16[128,2048]{1,0:T(8,128)(2,1)}, bf16[128,2048]{1,0:T(8,128)(2,1)}, u32[]{:S(2)}, u32[]{:S(2)}) collective-permute-start(bf16[128,2048]{1,0:T(8,128)(2,1)} %collective-permute-done.6), channel_id=1, source_target_pairs={{0,8},{1,9},{8,0},{9,1},{16,24},{17,25},{24,16},{25,17},{2,10},{3,... | collective-permute-start | bytes 1572872 | tf_op jit(solution)/shard_map/ppermute | solution.py:29
  94.7 19.3 %collective-permute-start.5 = (bf16[128,2048]{1,0:T(8,128)(2,1)}, bf16[128,2048]{1,0:T(8,128)(2,1)}, u32[]{:S(2)}, u32[]{:S(2)}) collective-permute-start(bf16[128,2048]{1,0:T(8,128)(2,1)} %collective-permute-done.3), channel_id=1, source_target_pairs={{0,8},{1,9},{8,0},{9,1},{16,24},{17,25},{24,16},{25,17},{2,10},{3,... | collective-permute-start | bytes 1572872 | tf_op jit(solution)/shard_map/ppermute | solution.py:29
  110.4 56.4 %all-to-all-start.3 = ((bf16[8,4,64,512]{3,2,1,0:T(8,128)(2,1)}), bf16[8,4,64,512]{3,2,1,0:T(8,128)(2,1)S(1)}, u32[]{:S(2)}, u32[]{:S(2)}) async-start(bf16[8,4,64,512]{3,2,1,0:T(8,128)(2,1)} %copy.116), calls=%async_computation.3 | async-start | bytes 4194304 | tf_op jit(solution)/shard_map/all_to_all | solution.py:541
  114.0 142.4 %all-gather.8.cloned.1.call-start = ((), (), s32[]{:S(2)}) async-start(), calls=%async_computation.13 | async-start | bytes 5242880 | tf_op jit(solution)/shard_map/all_gather | solution.py:491
  122.5 30.0 %collective-permute-start.14 = (bf16[128,2048]{1,0:T(8,128)(2,1)}, bf16[128,2048]{1,0:T(8,128)(2,1)}, u32[]{:S(2)}, u32[]{:S(2)}) collective-permute-start(bf16[128,2048]{1,0:T(8,128)(2,1)} %bitcast.68.refs_8_), channel_id=1, source_target_pairs={{0,17},{1,16},{8,25},{9,24},{16,1},{17,0},{24,9},{25,8},{2,19},{3,... | collective-permute-start | bytes 1572872 | tf_op jit(solution)/shard_map/ppermute | solution.py:29
  125.3 37.0 %collective-permute-start.13 = (bf16[128,2048]{1,0:T(8,128)(2,1)}, bf16[128,2048]{1,0:T(8,128)(2,1)}, u32[]{:S(2)}, u32[]{:S(2)}) collective-permute-start(bf16[128,2048]{1,0:T(8,128)(2,1)} %bitcast.68.refs_8_), channel_id=1, source_target_pairs={{0,16},{1,17},{8,24},{9,25},{16,0},{17,1},{24,8},{25,9},{2,18},{3,... | collective-permute-start | bytes 1572872 | tf_op jit(solution)/shard_map/ppermute | solution.py:29
  125.8 36.5 %collective-permute-start.10 = (bf16[128,2048]{1,0:T(8,128)(2,1)}, bf16[128,2048]{1,0:T(8,128)(2,1)}, u32[]{:S(2)}, u32[]{:S(2)}) collective-permute-start(bf16[128,2048]{1,0:T(8,128)(2,1)} %bitcast.68.refs_8_), channel_id=1, source_target_pairs={{0,1},{1,0},{8,9},{9,8},{16,17},{17,16},{24,25},{25,24},{2,3},{3,2... | collective-permute-start | bytes 1572872 | tf_op jit(solution)/shard_map/ppermute | solution.py:29
  127.3 52.5 %collective-permute-start.11 = (bf16[128,2048]{1,0:T(8,128)(2,1)}, bf16[128,2048]{1,0:T(8,128)(2,1)}, u32[]{:S(2)}, u32[]{:S(2)}) collective-permute-start(bf16[128,2048]{1,0:T(8,128)(2,1)} %bitcast.68.refs_8_), channel_id=1, source_target_pairs={{0,8},{1,9},{8,0},{9,1},{16,24},{17,25},{24,16},{25,17},{2,10},{3,... | collective-permute-start | bytes 1572872 | tf_op jit(solution)/shard_map/ppermute | solution.py:29
  152.5 27.4 %collective-permute-start.16 = (bf16[128,2048]{1,0:T(8,128)(2,1)}, bf16[128,2048]{1,0:T(8,128)(2,1)}, u32[]{:S(2)}, u32[]{:S(2)}) collective-permute-start(bf16[128,2048]{1,0:T(8,128)(2,1)} %collective-permute-done.14.refs_13_), channel_id=1, source_target_pairs={{0,8},{1,9},{8,0},{9,1},{16,24},{17,25},{24,16},{25,17},{2,10},{3,... | collective-permute-start | bytes 1572872 | tf_op jit(solution)/shard_map/ppermute | solution.py:29
  166.3 189.7 %reduce-scatter.4.cloned.1.call-start = ((), (), s32[]{:S(2)}) async-start(), calls=%async_computation.14 | async-start | bytes 5242880 | tf_op jit(solution)/shard_map/reduce_scatter | solution.py:595
  233.3 22.5 %collective-permute-start.28 = (bf16[128,2048]{1,0:T(8,128)(2,1)S(1)}, bf16[128,2048]{1,0:T(8,128)(2,1)S(1)}, u32[]{:S(2)}, u32[]{:S(2)}) collective-permute-start(bf16[128,2048]{1,0:T(8,128)(2,1)S(1)} %add_convert_fusion.4.refs_0_), channel_id=1, source_target_pairs={{0,16},{1,17},{8,24},{9,25},{16,0},{17,1},{24,8},{25,9},{2,18},{3,... | collective-permute-start | bytes 1572872 | tf_op jit(solution)/shard_map/ppermute | solution.py:29
  233.6 22.4 %collective-permute-start.25 = (bf16[128,2048]{1,0:T(8,128)(2,1)S(1)}, bf16[128,2048]{1,0:T(8,128)(2,1)}, u32[]{:S(2)}, u32[]{:S(2)}) collective-permute-start(bf16[128,2048]{1,0:T(8,128)(2,1)S(1)} %add_convert_fusion.4.refs_0_), channel_id=1, source_target_pairs={{0,1},{1,0},{8,9},{9,8},{16,17},{17,16},{24,25},{25,24},{2,3},{3,2... | collective-permute-start | bytes 1572872 | tf_op jit(solution)/shard_map/ppermute | solution.py:29
  234.6 21.8 %collective-permute-start.26 = (bf16[128,2048]{1,0:T(8,128)(2,1)S(1)}, bf16[128,2048]{1,0:T(8,128)(2,1)}, u32[]{:S(2)}, u32[]{:S(2)}) collective-permute-start(bf16[128,2048]{1,0:T(8,128)(2,1)S(1)} %add_convert_fusion.4.refs_0_), channel_id=1, source_target_pairs={{0,8},{1,9},{8,0},{9,1},{16,24},{17,25},{24,16},{25,17},{2,10},{3,... | collective-permute-start | bytes 1572872 | tf_op jit(solution)/shard_map/ppermute | solution.py:29
  278.3 200.8 %reduce-scatter.8.cloned.1.call-start = ((), (), s32[]{:S(2)}) async-start(), calls=%async_computation.16 | async-start | bytes 5242880 | tf_op jit(solution)/shard_map/reduce_scatter | solution.py:595
  312.8 23.8 %collective-permute-start.43 = (bf16[128,2048]{1,0:T(8,128)(2,1)S(1)}, bf16[128,2048]{1,0:T(8,128)(2,1)S(1)}, u32[]{:S(2)}, u32[]{:S(2)}) collective-permute-start(bf16[128,2048]{1,0:T(8,128)(2,1)S(1)} %get-tuple-element.84.refs_0_), channel_id=1, source_target_pairs={{0,16},{1,17},{8,24},{9,25},{16,0},{17,1},{24,8},{25,9},{2,18},{3,... | collective-permute-start | bytes 1572872 | tf_op jit(solution)/shard_map/ppermute | solution.py:29
  314.5 22.8 %collective-permute-start.40 = (bf16[128,2048]{1,0:T(8,128)(2,1)S(1)}, bf16[128,2048]{1,0:T(8,128)(2,1)S(1)}, u32[]{:S(2)}, u32[]{:S(2)}) collective-permute-start(bf16[128,2048]{1,0:T(8,128)(2,1)S(1)} %get-tuple-element.84.refs_0_), channel_id=1, source_target_pairs={{0,1},{1,0},{8,9},{9,8},{16,17},{17,16},{24,25},{25,24},{2,3},{3,2... | collective-permute-start | bytes 1572872 | tf_op jit(solution)/shard_map/ppermute | solution.py:29
  315.7 21.7 %collective-permute-start.41 = (bf16[128,2048]{1,0:T(8,128)(2,1)S(1)}, bf16[128,2048]{1,0:T(8,128)(2,1)S(1)}, u32[]{:S(2)}, u32[]{:S(2)}) collective-permute-start(bf16[128,2048]{1,0:T(8,128)(2,1)S(1)} %get-tuple-element.84.refs_0_), channel_id=1, source_target_pairs={{0,8},{1,9},{8,0},{9,1},{16,24},{17,25},{24,16},{25,17},{2,10},{3,... | collective-permute-start | bytes 1572872 | tf_op jit(solution)/shard_map/ppermute | solution.py:29
  359.3 21.5 %all-to-all-start.4 = ((bf16[4,2,128,512]{3,2,1,0:T(8,128)(2,1)}), bf16[4,2,128,512]{3,2,1,0:T(8,128)(2,1)S(1)}, u32[]{:S(2)}, u32[]{:S(2)}) async-start(bf16[4,2,128,512]{3,2,1,0:T(8,128)(2,1)} %maximum_bitcast_fusion), calls=%async_computation.5 | async-start | bytes 2097152 | tf_op jit(solution)/shard_map/all_to_all | solution.py:93
  362.8 154.3 %reduce-scatter.6.cloned.1.call-start = ((), (), s32[]{:S(2)}) async-start(), calls=%async_computation.15 | async-start | bytes 5242880 | tf_op jit(solution)/shard_map/reduce_scatter | solution.py:595
  407.2 27.3 %collective-permute-start.55 = (bf16[128,2048]{1,0:T(8,128)(2,1)S(1)}, bf16[128,2048]{1,0:T(8,128)(2,1)S(1)}, u32[]{:S(2)}, u32[]{:S(2)}) collective-permute-start(bf16[128,2048]{1,0:T(8,128)(2,1)S(1)} %get-tuple-element.98), channel_id=1, source_target_pairs={{0,8},{1,9},{8,0},{9,1},{16,24},{17,25},{24,16},{25,17},{2,10},{3,... | collective-permute-start | bytes 1572872 | tf_op jit(solution)/shard_map/ppermute | solution.py:29
  409.9 36.2 %collective-permute-start.47 = (bf16[128,2048]{1,0:T(8,128)(2,1)}, bf16[128,2048]{1,0:T(8,128)(2,1)}, u32[]{:S(2)}, u32[]{:S(2)}) collective-permute-start(bf16[128,2048]{1,0:T(8,128)(2,1)} %get-tuple-element.91), channel_id=1, source_target_pairs={{0,8},{1,9},{8,0},{9,1},{16,24},{17,25},{24,16},{25,17},{2,10},{3,... | collective-permute-start | bytes 1572872 | tf_op jit(solution)/shard_map/ppermute | solution.py:29
  434.5 19.6 %collective-permute-start.51 = (bf16[128,2048]{1,0:T(8,128)(2,1)}, bf16[128,2048]{1,0:T(8,128)(2,1)}, u32[]{:S(2)}, u32[]{:S(2)}) collective-permute-start(bf16[128,2048]{1,0:T(8,128)(2,1)} %pad_maximum_fusion.9), channel_id=1, source_target_pairs={{0,16},{1,17},{8,24},{9,25},{16,0},{17,1},{24,8},{25,9},{2,18},{3,... | collective-permute-start | bytes 1572872 | tf_op jit(solution)/shard_map/ppermute | solution.py:29
  463.8 23.1 %collective-permute-start.65 = (f32[4,2048]{1,0:T(4,128)S(1)}, f32[4,2048]{1,0:T(4,128)S(1)}, u32[]{:S(2)}, u32[]{:S(2)}) collective-permute-start(f32[4,2048]{1,0:T(4,128)S(1)} %fusion.61), channel_id=1, source_target_pairs={{0,16},{1,17},{8,24},{9,25},{16,0},{17,1},{24,8},{25,9},{2,18},{3,... | collective-permute-start | bytes 98312 | tf_op jit(solution)/shard_map/ppermute | solution.py:29
  465.6 21.3 %collective-permute-start.66 = (f32[4,2048]{1,0:T(4,128)S(1)}, f32[4,2048]{1,0:T(4,128)S(1)}, u32[]{:S(2)}, u32[]{:S(2)}) collective-permute-start(f32[4,2048]{1,0:T(4,128)S(1)} %fusion.61), channel_id=1, source_target_pairs={{0,17},{1,16},{8,25},{9,24},{16,1},{17,0},{24,9},{25,8},{2,19},{3,... | collective-permute-start | bytes 98312 | tf_op jit(solution)/shard_map/ppermute | solution.py:29
  466.4 20.5 %collective-permute-start.64 = (f32[4,2048]{1,0:T(4,128)S(1)}, f32[4,2048]{1,0:T(4,128)S(1)}, u32[]{:S(2)}, u32[]{:S(2)}) collective-permute-start(f32[4,2048]{1,0:T(4,128)S(1)} %fusion.61), channel_id=1, source_target_pairs={{0,1},{1,0},{8,9},{9,8},{16,17},{17,16},{24,25},{25,24},{2,3},{3,2... | collective-permute-start | bytes 98312 | tf_op jit(solution)/shard_map/ppermute | solution.py:29
  482.2 34.9 %all-to-all-start.6 = ((bf16[8,128,512]{2,1,0:T(8,128)(2,1)}), bf16[8,128,512]{2,1,0:T(8,128)(2,1)S(1)}, u32[]{:S(2)}, u32[]{:S(2)}) async-start(bf16[8,128,512]{2,1,0:T(8,128)(2,1)} %bitcast.43), calls=%async_computation.9 | async-start | bytes 2097152 | tf_op jit(solution)/shard_map/all_to_all | solution.py:673
  (82 other events, 783.2 us)
Sparse Core Ops, SparseCore 0:
  10.9 48.6 all-gather.5
  61.2 114.0 all-gather.3
  177.4 78.9 all-gather.7
  278.5 77.4 reduce-scatter.3
  358.2 77.2 reduce-scatter.7
  437.7 79.3 reduce-scatter.5
